TPU v7x, 512 devices: a whole 4x8x8 slice. The times are simulated.
512 devices in a mesh: row: 16 (over z_lo, x), col: 32 (over z_hi, y, core).
Axes of the slice: x: 4, y: 8, z: 8 (z_hi: 2, z_lo: 4; z = z_hi * 4 + z_lo), core: 2. Of those that a mesh axis runs over, the one named last changes fastest.
Arguments:
- object_field: float32 [2, 4096, 8192], P(None, 'row', 'col'), may hold values from -6 to 6
- probe_modes: bfloat16 [2, 6, 256, 256], replicated, may hold values from -1.796875 to 1.796875
- offsets: int32 [16, 32, 1, 2], P('row', 'col'), may hold values from 0 to 255
- counts: int32 [16, 32], P('row', 'col'), may hold values from 0 to 1, as said below
- intensity: bfloat16 [16, 32, 1, 256, 256], P('row', 'col'), may hold values from 0 to 4
Outputs:
- object_new: float32 [2, 4096, 8192], P(None, 'row', 'col')
- probe_new: float32 [2, 6, 256, 256], P(None, None, 'row', 'col')
Inputs may be any that keep to these rules, and one draw needn't show every extreme that they name: The first counts[a, b] slots of tile (a, b) are live and the others are ignored; some tile has 1 and some tile has none.
All inputs are finite; a program needn't handle non-finite values.
Results may differ from a plain program's by a relative error of at most 0.00045.
Values sent between devices are 32-bit elements; how exact they have to be, the bound alone decides.
No kernel may reach another device: no remote copies, remote signals or barrier semaphores. Data moves between devices by JAX's collectives and lax.ppermute only.
A program may use at most 64 MiB of HBM per device.

v0:
```python
import functools
import math

import jax
import jax.numpy as jnp
import ml_dtypes
import numpy as np
from jax import lax
from jax.experimental import pallas as pl
from jax.experimental.pallas import tpu as pltpu
from jax.sharding import PartitionSpec as P

object_rate = 0.25
f32 = jnp.float32
bf16 = jnp.bfloat16
half = 128
full = 256
modes = 6
strip = 16


def passed_along(x, axis, by):
    devices = lax.axis_size(axis)
    pairs = [(i, i + by) for i in range(devices) if 0 <= i + by < devices]
    return lax.ppermute(x, axis, pairs)


def halves_tables():
    place = np.arange(half)[:, None]
    freq = np.arange(half)[None, :]
    columns = column_order()[:half]
    tables = []
    for places in (place, columns[:, None]):
        for odd in (0, 1):
            angle = -2.0 * math.pi * ((places * (2 * freq + odd)) % full) / full
            re, im = np.cos(angle) / 16.0, np.sin(angle) / 16.0
            real_form = np.block([[re, im], [-im, re]]).astype(np.float32)
            for form in (real_form, real_form.T):
                high = form.astype(ml_dtypes.bfloat16)
                low = (form - high.astype(np.float32)).astype(ml_dtypes.bfloat16)
                tables.append(np.stack([high, low]))
    frequencies = np.zeros((full, full), np.float32)
    shuffle = np.zeros((full, full), np.float32)
    for k in range(full):
        frequencies[(k % 2) * half + k // 2, k] = 1.0
    shuffle[column_order(), np.arange(full)] = 1.0
    orders = np.stack([frequencies, frequencies.T, shuffle, shuffle.T])
    return np.stack(tables), orders.astype(ml_dtypes.bfloat16)


def column_order():
    columns = np.arange(full).reshape(2, 8, 2, 8)
    return columns.transpose(0, 2, 1, 3).reshape(-1)


def split(x):
    high = x.astype(bf16)
    return high, (x - high.astype(f32)).astype(bf16)


def dot(a, b):
    return jnp.dot(a, b, preferred_element_type=f32)


def data_by_table(x, table_ref, which):
    high, low = split(x)
    table_high, table_low = table_ref[which, 0], table_ref[which, 1]
    return dot(
        jnp.concatenate([high, high, low], axis=1),
        jnp.concatenate([table_high, table_low, table_high], axis=0),
    )


def table_by_data(table_ref, which, x):
    high, low = split(x)
    table_high, table_low = table_ref[which, 0], table_ref[which, 1]
    return dot(
        jnp.concatenate([table_high, table_low, table_high], axis=1),
        jnp.concatenate([high, high, low], axis=0),
    )


def forward(exit_re, exit_im, table_ref):
    rows = []
    for sign, which in ((1.0, 0), (-1.0, 2)):
        folded = jnp.concatenate(
            [
                exit_re[:, :half] + sign * exit_re[:, half:],
                exit_im[:, :half] + sign * exit_im[:, half:],
            ],
            axis=1,
        )
        rows.append(data_by_table(folded, table_ref, 4 + which))
    even, odd = rows
    outs = []
    for sign, which in ((1.0, 1), (-1.0, 3)):
        fold_even = even[:half] + sign * even[half:]
        fold_odd = odd[:half] + sign * odd[half:]
        stacked = jnp.concatenate(
            [
                jnp.concatenate([fold_even[:, :half], fold_odd[:, :half]], axis=1),
                jnp.concatenate([fold_even[:, half:], fold_odd[:, half:]], axis=1),
            ],
            axis=0,
        )
        outs.append(table_by_data(table_ref, which, stacked))
    return outs


def backward(even, odd, table_ref):
    part_even = table_by_data(table_ref, 0, even)
    part_odd = table_by_data(table_ref, 2, odd)
    upper = part_even + part_odd
    lower = part_even - part_odd
    rows_re = jnp.concatenate([upper[:half], lower[:half]], axis=0)
    rows_im = jnp.concatenate([upper[half:], lower[half:]], axis=0)
    cols_even = data_by_table(
        jnp.concatenate([rows_re[:, :half], rows_im[:, :half]], axis=1), table_ref, 5
    )
    cols_odd = data_by_table(
        jnp.concatenate([rows_re[:, half:], rows_im[:, half:]], axis=1), table_ref, 7
    )
    near_re = jnp.concatenate(
        [cols_even[:, :half] + cols_odd[:, :half], cols_even[:, :half] - cols_odd[:, :half]], axis=1
    )
    near_im = jnp.concatenate(
        [cols_even[:, half:] + cols_odd[:, half:], cols_even[:, half:] - cols_odd[:, half:]], axis=1
    )
    return near_re, near_im


def reorder(x, order):
    high = x.astype(bf16)
    left = x - high.astype(f32)
    mid = left.astype(bf16)
    low = (left - mid.astype(f32)).astype(bf16)
    return dot(jnp.concatenate([high, mid, low], axis=1), jnp.concatenate([order, order, order], axis=0))


def store_strips(mine_ref, peer_ref, index, value, core):
    left, right = value[:, :half], value[:, half:]
    lanes = lax.broadcasted_iota(jnp.int32, (full, half), 1)
    first = jnp.where(lanes < half // 2, left, pltpu.roll(right, half // 2, 1))
    second = jnp.where(lanes < half // 2, pltpu.roll(left, half // 2, 1), right)
    mine = jnp.where(core == 0, first, second)
    peer = jnp.where(core == 0, second, first)
    for z in range(4):
        for x in range(4):
            at = (z * 4 + x) * strip
            mine_ref[x, z, index] = mine[at : at + strip]
            peer_ref[x, z, index] = peer[at : at + strip]


def cells():
    rows = lax.broadcasted_iota(jnp.int32, (full, full), 0)
    cols = lax.broadcasted_iota(jnp.int32, (full, full), 1)
    return rows, cols


def prepare_kernel(probe_ref, intensity_ref, table_ref, order_ref, probe_out, measured_out, table_out, order_out):
    frequencies, turned, shuffle = order_ref[0], order_ref[1], order_ref[2]
    measured_out[...] = dot(dot(frequencies, intensity_ref[...]).astype(bf16), turned)
    for part in range(2):
        for mode in range(modes):
            probe_out[part, mode] = dot(probe_ref[part, mode], shuffle).astype(bf16)
    table_out[...] = table_ref[...]
    order_out[0] = shuffle
    order_out[1] = order_ref[3]


def main_kernel(
    offset_ref, count_ref, own_ref, right_ref, below_ref, diag_ref, probe_ref, measured_ref, table_ref, order_ref,
    mine_ref, peer_ref, upper_ref, lower_ref, window_ref, far_ref,
):
    row_offset = offset_ref[0]
    col_offset = offset_ref[1]
    live = (count_ref[0] > 0).astype(f32)
    core = lax.axis_index("core")
    rows, cols = cells()
    in_row = rows >= row_offset
    in_col = cols >= col_offset
    for part in range(2):
        upper = jnp.where(in_col, own_ref[part], right_ref[part])
        lower = jnp.where(in_col, below_ref[part], diag_ref[part])
        mixed = jnp.where(in_row, upper, lower)
        mixed = pltpu.roll(mixed, lax.rem(full - row_offset, full), 0)
        window_ref[part] = reorder(pltpu.roll(mixed, lax.rem(full - col_offset, full), 1), order_ref[0])
    sum_even = -measured_ref[:half]
    sum_odd = -measured_ref[half:]
    for mode in range(modes):
        win_re, win_im = window_ref[0], window_ref[1]
        probe_re = probe_ref[0, mode].astype(f32)
        probe_im = probe_ref[1, mode].astype(f32)
        even, odd = forward(
            probe_re * win_re - probe_im * win_im, probe_re * win_im + probe_im * win_re, table_ref
        )
        far_ref[mode, 0] = even
        far_ref[mode, 1] = odd
        sum_even = sum_even + (even[:half] * even[:half] + even[half:] * even[half:])
        sum_odd = sum_odd + (odd[:half] * odd[:half] + odd[half:] * odd[half:])
    sum_even = sum_even * live
    sum_odd = sum_odd * live
    res_even = jnp.concatenate([sum_even, sum_even], axis=0)
    res_odd = jnp.concatenate([sum_odd, sum_odd], axis=0)
    obj_re = jnp.zeros((full, full), f32)
    obj_im = jnp.zeros((full, full), f32)
    for mode in range(modes):
        win_re, win_im = window_ref[0], window_ref[1]
        probe_re = probe_ref[0, mode].astype(f32)
        probe_im = probe_ref[1, mode].astype(f32)
        near_re, near_im = backward(far_ref[mode, 0] * res_even, far_ref[mode, 1] * res_odd, table_ref)
        store_strips(mine_ref, peer_ref, mode, win_re * near_re + win_im * near_im, core)
        store_strips(mine_ref, peer_ref, modes + mode, win_re * near_im - win_im * near_re, core)
        obj_re = obj_re + probe_re * near_re + probe_im * near_im
        obj_im = obj_im + probe_re * near_im - probe_im * near_re
    for part, total in enumerate((obj_re, obj_im)):
        placed = reorder(total, order_ref[1])
        placed = pltpu.roll(pltpu.roll(placed, row_offset, 0), col_offset, 1)
        upper_ref[part] = jnp.where(in_row, placed, 0.0)
        lower_ref[part] = jnp.where(in_row, 0.0, placed)


def cores_kernel(mine_ref, theirs_ref, send_ref, keep_ref):
    x = lax.axis_index("x")
    core = lax.axis_index("core")
    first = jnp.where(core == 0, x ^ 1, 3 - x)
    second = jnp.where(core == 0, 3 - x, x ^ 1)
    for ref, slot, index in ((send_ref, 0, first), (send_ref, 1, x ^ 2), (keep_ref, 0, x), (keep_ref, 1, second)):
        ref[slot] = mine_ref[index] + theirs_ref[index]


def columns_kernel(kept_ref, got_ref, came_ref, out_ref):
    lanes = lax.broadcasted_iota(jnp.int32, (96, half), 1)
    for z in range(4):
        total = (kept_ref[0, z] + got_ref[0, z] + came_ref[z]).reshape(192, half)
        top, bottom = total[:96], total[96:]
        out_ref[2 * z] = jnp.where(lanes < half // 2, top, pltpu.roll(bottom, half // 2, 1))
        out_ref[2 * z + 1] = jnp.where(lanes < half // 2, pltpu.roll(top, half // 2, 1), bottom)


def turn_kernel(parts_ref, out_ref):
    total = parts_ref[0]
    for i in range(1, 8):
        total = total + parts_ref[i]
    turned = total.T
    for part in range(2):
        for y in range(8):
            at = part * 64 + y * 8
            out_ref[y, part * 8 : part * 8 + 8] = turned[at : at + 8]


def shaped(*shape, dtype=f32):
    return jax.ShapeDtypeStruct(shape, dtype)


vmem = pl.BlockSpec(memory_space=pltpu.VMEM)
smem = pl.BlockSpec(memory_space=pltpu.SMEM)


def call(kernel, name, inputs, outputs, scratch=(), flops=0, moved=0, limit=16):
    return pl.pallas_call(
        kernel,
        out_shape=tuple(outputs) if len(outputs) > 1 else outputs[0],
        in_specs=inputs,
        out_specs=(vmem,) * len(outputs) if len(outputs) > 1 else vmem,
        scratch_shapes=scratch,
        compiler_params=pltpu.CompilerParams(vmem_limit_bytes=limit * 1024 * 1024),
        cost_estimate=pl.CostEstimate(flops=flops, bytes_accessed=moved, transcendentals=0),
        name=name,
    )


def local(object_field, probe_modes, offsets, counts, intensity):
    rows = ("z_lo", "x")
    cols = ("z_hi", "y", "core")
    tables, orders = halves_tables()
    below = passed_along(object_field, rows, -1)
    right = passed_along(object_field, cols, -1)
    diag = passed_along(below, cols, -1)
    above_offset = passed_along(offsets[:, :, :, 1], rows, 1)
    probe, measured, table, order = call(
        prepare_kernel,
        "prepare",
        [vmem] * 4,
        [
            shaped(2, modes, full, full, dtype=bf16),
            shaped(full, full),
            shaped(8, 2, full, full, dtype=bf16),
            shaped(2, full, full, dtype=bf16),
        ],
        flops=500_000_000,
        moved=8_000_000,
    )(probe_modes, intensity[0, 0, 0], jnp.asarray(tables), jnp.asarray(orders))
    block_shape = (4, 4, 2 * modes, strip, half)
    mine, peer, upper, lower = call(
        main_kernel,
        "step",
        [smem, smem] + [vmem] * 8,
        [shaped(*block_shape), shaped(*block_shape), shaped(2, full, full), shaped(2, full, full)],
        scratch=[pltpu.VMEM((2, full, full), f32), pltpu.VMEM((modes, 2, full, full), f32)],
        flops=5_000_000_000,
        moved=12_000_000,
        limit=24,
    )(offsets.reshape(2), counts.reshape(1), object_field, right, below, diag, probe, measured, table, order)

    theirs = lax.ppermute(peer, "core", [(0, 1), (1, 0)])
    from_above = passed_along(lower, rows, 1)
    half_shape = (2, *block_shape[1:])
    send, keep = call(
        cores_kernel, "add_cores", [vmem] * 2, [shaped(*half_shape)] * 2, moved=6_000_000
    )(mine, theirs)
    near_pairs = [(2 * x + c, 2 * ((x ^ 1) if c == 0 else 3 - x) + c) for x in range(4) for c in range(2)]
    far_pairs = [(2 * x + c, 2 * (3 - x if c == 0 else (x ^ 1)) + c) for x in range(4) for c in range(2)]
    got = lax.ppermute(send, ("x", "core"), near_pairs)
    came = lax.ppermute(keep[1] + got[1], ("x", "core"), far_pairs)
    packed = call(columns_kernel, "add_columns", [vmem] * 3, [shaped(8, 96, half)], moved=2_000_000)(keep, got, came)
    parts = lax.all_to_all(packed, ("z_lo", "z_hi"), 0, 0, tiled=True)
    turned = call(turn_kernel, "add_turn", [vmem], [shaped(8, strip, 96)], moved=500_000)(parts)
    parts = lax.all_to_all(turned, "y", 0, 0, tiled=True)
    share = jnp.sum(parts, axis=0).reshape(2, 8, modes, strip).transpose(0, 2, 3, 1)
    start = (0, 0, lax.axis_index(rows) * strip, lax.axis_index(cols) * 8)
    own_probe = lax.dynamic_slice(probe_modes, start, (2, modes, strip, 8)).astype(f32)
    probe_new = own_probe - (512.0 ** -0.5) * share

    lanes = lax.broadcasted_iota(jnp.int32, (2, full, full), 2)
    stays = lanes >= offsets[0, 0, 0, 1]
    above_stays = lanes >= above_offset[0, 0, 0]
    zero = jnp.zeros((), f32)
    moves = jnp.where(stays, zero, upper) + jnp.where(above_stays, zero, from_above)
    from_left = passed_along(moves, cols, 1)
    held = jnp.where(stays, upper, zero) + jnp.where(above_stays, from_above, zero)
    object_new = object_field - object_rate * (held + from_left)
    return (object_new, probe_new)


def solution(mesh):
    grid = jax.sharding.Mesh(mesh.devices.reshape(4, 4, 2, 8, 2), ("z_lo", "x", "z_hi", "y", "core"))
    rows = ("z_lo", "x")
    cols = ("z_hi", "y", "core")
    in_specs = (
        P(None, rows, cols),
        P(),
        P(rows, cols, None, None),
        P(rows, cols),
        P(rows, cols, None, None, None),
    )
    out_specs = (P(None, rows, cols), P(None, None, rows, cols))
    return jax.shard_map(local, mesh=grid, in_specs=in_specs, out_specs=out_specs, check_vma=False)
```

profile of v0, /device:TPU:70, one launch (start us, length us, event | category | flops | bytes accessed | tf_op | source)
XLA Modules:
  0.0 136.6 jit_solution(13584761376292807310)
XLA Ops:
  0.6 2.7 %collective-permute-start.1 = (f32[2,256,256]{2,1,0:T(8,128)}, f32[2,256,256]{2,1,0:T(8,128)S(1)}, u32[]{:S(2)}, u32[]{:S(2)}) collective-permute-start(f32[2,256,256]{2,1,0:T(8,128)} %own_ref.1), channel_id=1, source_target_pairs={{32,0},{64,32},{96,64},{128,96},{160,128},{192,160},{224,192},{256... | collective-permute-start | bytes 1572872 | tf_op jit(solution)/shard_map/ppermute | solution.py:25
  3.4 1.3 collective-permute-start
  4.7 13.8 %collective-permute-done.1.below_ref = f32[2,256,256]{2,1,0:T(8,128)S(1)} collective-permute-done((f32[2,256,256]{2,1,0:T(8,128)}, f32[2,256,256]{2,1,0:T(8,128)S(1)}, u32[]{:S(2)}, u32[]{:S(2)}) %collective-permute-start.1) | collective-permute-done | bytes 524320 | tf_op jit(solution)/shard_map/ppermute | solution.py:25
  18.5 1.3 collective-permute-start.2
  20.4 0.0 copy-start
  20.5 1.6 %copy-done = bf16[8,2,256,256]{3,2,1,0:T(8,128)(2,1)S(1)} copy-done((bf16[8,2,256,256]{3,2,1,0:T(8,128)(2,1)S(1)}, bf16[8,2,256,256]{3,2,1,0:T(8,128)(2,1)}, u32[]{:S(2)}) %copy-start) | copy-done | bytes 2097176
  22.0 0.0 copy-start.1
  22.0 1.4 %copy-done.1 = bf16[2,6,256,256]{3,2,1,0:T(8,128)(2,1)S(1)} copy-done((bf16[2,6,256,256]{3,2,1,0:T(8,128)(2,1)S(1)}, bf16[2,6,256,256]{3,2,1,0:T(8,128)(2,1)}, u32[]{:S(2)}) %copy-start.1) | copy-done | bytes 1572888
  23.4 0.0 copy-start.3
  23.4 1.0 copy-done.3
  24.5 0.0 copy-start.4
  24.5 0.9 copy-done.4
  25.4 0.0 copy-start.2
  25.4 0.0 copy-start.5
  25.4 0.8 prepare.1
  26.2 0.0 collective-permute-done.right_ref
  26.3 0.0 collective-permute-done.2.diag_ref
  26.3 0.2 copy-done.2
  26.4 0.0 copy-done.5
  26.4 9.7 %step.1 = (f32[4,4,12,16,128]{4,3,2,1,0:T(8,128)S(1)}, f32[4,4,12,16,128]{4,3,2,1,0:T(8,128)S(1)}, f32[2,256,256]{2,1,0:T(8,128)S(1)}, f32[2,256,256]{2,1,0:T(8,128)S(1)}) custom-call(s32[2]{0:T(128)S(1)} %bitcast.12, s32[1]{0:T(128)} %bitcast.10.count_ref, f32[2,256,256]{2,1,0:T(8,128)S(1)} %copy-done.2, f32[2,256,256]{2,1,0:T(8,128)S(1)} %collective-permute-done.right_ref, ...), custom_call_target="tpu_custom_call" | custom-call | flops 5000000000 | bytes 12000000 | tf_op jit(solution)/shard_map/step/pallas_call | solution.py:295
  36.2 4.4 %collective-permute-start.6 = (f32[4,4,12,16,128]{4,3,2,1,0:T(8,128)S(1)}, f32[4,4,12,16,128]{4,3,2,1,0:T(8,128)S(1)}, u32[]{:S(2)}, u32[]{:S(2)}) collective-permute-start(f32[4,4,12,16,128]{4,3,2,1,0:T(8,128)S(1)} %get-tuple-element.19), channel_id=1, source_target_pairs={{0,1},{1,0},{2,3},{3,2},{4,5},{5,4},{6,7},{7,6},{8,9},{9,8},{10,11... | collective-permute-start | bytes 4718600 | tf_op jit(solution)/shard_map/ppermute | solution.py:306
  40.6 3.0 %collective-permute-done.6.theirs_ref = f32[4,4,12,16,128]{4,3,2,1,0:T(8,128)S(1)} collective-permute-done((f32[4,4,12,16,128]{4,3,2,1,0:T(8,128)S(1)}, f32[4,4,12,16,128]{4,3,2,1,0:T(8,128)S(1)}, u32[]{:S(2)}, u32[]{:S(2)}) %collective-permute-start.6) | collective-permute-done | bytes 1572896 | tf_op jit(solution)/shard_map/ppermute | solution.py:306
  43.6 0.2 add_cores.1
  43.8 1.9 %collective-permute-start.7 = (f32[2,4,12,16,128]{4,3,2,1,0:T(8,128)S(1)}, f32[2,4,12,16,128]{4,3,2,1,0:T(8,128)S(1)}, u32[]{:S(2)}, u32[]{:S(2)}) collective-permute-start(f32[2,4,12,16,128]{4,3,2,1,0:T(8,128)S(1)} %get-tuple-element.21), channel_id=1, source_target_pairs={{0,32},{1,97},{32,0},{33,65},{64,96},{65,33},{96,64},{97,1},{2,34}... | collective-permute-start | bytes 2359304 | tf_op jit(solution)/shard_map/ppermute | solution.py:314
  45.7 3.5 %collective-permute-start.4 = (f32[2,256,256]{2,1,0:T(8,128)S(1)}, f32[2,256,256]{2,1,0:T(8,128)S(1)}, u32[]{:S(2)}, u32[]{:S(2)}) collective-permute-start(f32[2,256,256]{2,1,0:T(8,128)S(1)} %get-tuple-element.17), channel_id=1, source_target_pairs={{0,32},{32,64},{64,96},{96,128},{128,160},{160,192},{192,224},{224... | collective-permute-start | bytes 1572872 | tf_op jit(solution)/shard_map/ppermute | solution.py:25
  49.3 14.0 %collective-permute-done.7.got_ref = f32[2,4,12,16,128]{4,3,2,1,0:T(8,128)S(1)} collective-permute-done((f32[2,4,12,16,128]{4,3,2,1,0:T(8,128)S(1)}, f32[2,4,12,16,128]{4,3,2,1,0:T(8,128)S(1)}, u32[]{:S(2)}, u32[]{:S(2)}) %collective-permute-start.7) | collective-permute-done | bytes 786464 | tf_op jit(solution)/shard_map/ppermute | solution.py:314
  63.3 0.1 fusion
  63.4 1.9 %collective-permute-start.8 = (f32[4,12,16,128]{3,2,1,0:T(8,128)S(1)}, f32[4,12,16,128]{3,2,1,0:T(8,128)S(1)}, u32[]{:S(2)}, u32[]{:S(2)}) collective-permute-start(f32[4,12,16,128]{3,2,1,0:T(8,128)S(1)} %fusion), channel_id=1, source_target_pairs={{0,96},{1,33},{32,64},{33,1},{64,32},{65,97},{96,0},{97,65},{2,98}... | collective-permute-start | bytes 1179656 | tf_op jit(solution)/shard_map/ppermute | solution.py:315
  65.3 0.6 slice.10
  65.9 6.9 %collective-permute-start.3 = (s32[1,1,1]{2,1,0:T(1,128)}, s32[1,1,1]{2,1,0:T(1,128)}, u32[]{:S(2)}, u32[]{:S(2)}) collective-permute-start(s32[1,1,1]{2,1,0:T(1,128)} %bitcast.4), channel_id=1, source_target_pairs={{0,32},{32,64},{64,96},{96,128},{128,160},{160,192},{192,224},{224... | collective-permute-start | bytes 20 | tf_op jit(solution)/shard_map/ppermute | solution.py:25
  72.8 0.7 iota_compare_fusion.1
  73.5 0.7 collective-permute-done.3
  74.2 0.7 iota_compare_fusion
  74.9 0.0 collective-permute-done.8.came_ref
  74.9 0.9 add_columns.1
  75.9 13.6 %all-to-all-start = ((f32[8,96,128]{2,1,0:T(8,128)}), f32[8,96,128]{2,1,0:T(8,128)S(1)}, u32[]{:S(2)}, u32[]{:S(2)}) async-start(f32[8,96,128]{2,1,0:T(8,128)} %add_columns.1), calls=%async_computation | async-start | bytes 786432 | tf_op jit(solution)/shard_map/all_to_all | solution.py:317
  89.4 0.0 collective-permute-done.4
  89.4 0.1 select_add_fusion
  89.5 3.3 %collective-permute-start.5 = (f32[2,256,256]{2,1,0:T(8,128)S(1)}, f32[2,256,256]{2,1,0:T(8,128)S(1)}, u32[]{:S(2)}, u32[]{:S(2)}) collective-permute-start(f32[2,256,256]{2,1,0:T(8,128)S(1)} %select_add_fusion), channel_id=1, source_target_pairs={{0,1},{1,2},{2,3},{3,4},{4,5},{5,6},{6,7},{7,8},{8,9},{9,10},{10,1... | collective-permute-start | bytes 1572872 | tf_op jit(solution)/shard_map/ppermute | solution.py:25
  92.8 0.9 constant_dynamic-slice_fusion
  93.7 0.1 copy.12
  93.8 9.5 %all-to-all-done.parts_ref = f32[8,96,128]{2,1,0:T(8,128)S(1)} async-done(((f32[8,96,128]{2,1,0:T(8,128)}), f32[8,96,128]{2,1,0:T(8,128)S(1)}, u32[]{:S(2)}, u32[]{:S(2)}) %all-to-all-start) | async-done | bytes 393248 | tf_op jit(solution)/shard_map/all_to_all | solution.py:317
  103.3 0.7 add_turn.1
  104.0 23.5 %all-to-all-start.1 = ((f32[8,16,96]{2,1,0:T(8,128)}), f32[8,16,96]{2,1,0:T(8,128)S(1)}, u32[]{:S(2)}, u32[]{:S(2)}) async-start(f32[8,16,96]{2,1,0:T(8,128)} %add_turn.1), calls=%async_computation.1 | async-start | bytes 131072 | tf_op jit(solution)/shard_map/all_to_all | solution.py:319
  127.5 0.0 collective-permute-done.5
  127.5 0.9 multiply_subtract_fusion
  128.4 7.4 %all-to-all-done.1 = f32[8,16,96]{2,1,0:T(8,128)S(1)} async-done(((f32[8,16,96]{2,1,0:T(8,128)}), f32[8,16,96]{2,1,0:T(8,128)S(1)}, u32[]{:S(2)}, u32[]{:S(2)}) %all-to-all-start.1) | async-done | bytes 49184 | tf_op jit(solution)/shard_map/all_to_all | solution.py:319
  135.9 0.1 mul.42
  136.0 0.6 copy.11
  (3 shorter events, 0.0 us)
Async XLA Ops:
  0.6 17.9 %collective-permute-start.1 = (f32[2,256,256]{2,1,0:T(8,128)}, f32[2,256,256]{2,1,0:T(8,128)S(1)}, u32[]{:S(2)}, u32[]{:S(2)}) collective-permute-start(f32[2,256,256]{2,1,0:T(8,128)} %own_ref.1), channel_id=1, source_target_pairs={{32,0},{64,32},{96,64},{128,96},{160,128},{192,160},{224,192},{256... | collective-permute-start | bytes 1572872 | tf_op jit(solution)/shard_map/ppermute | solution.py:25
  3.4 22.9 %collective-permute-start = (f32[2,256,256]{2,1,0:T(8,128)}, f32[2,256,256]{2,1,0:T(8,128)S(1)}, u32[]{:S(2)}, u32[]{:S(2)}) collective-permute-start(f32[2,256,256]{2,1,0:T(8,128)} %own_ref.1), channel_id=1, source_target_pairs={{1,0},{2,1},{3,2},{4,3},{5,4},{6,5},{7,6},{8,7},{9,8},{10,9},{11,1... | collective-permute-start | bytes 1572872 | tf_op jit(solution)/shard_map/ppermute | solution.py:25
  18.5 7.7 %collective-permute-start.2 = (f32[2,256,256]{2,1,0:T(8,128)S(1)}, f32[2,256,256]{2,1,0:T(8,128)S(1)}, u32[]{:S(2)}, u32[]{:S(2)}) collective-permute-start(f32[2,256,256]{2,1,0:T(8,128)S(1)} %collective-permute-done.1.below_ref), channel_id=1, source_target_pairs={{1,0},{2,1},{3,2},{4,3},{5,4},{6,5},{7,6},{8,7},{9,8},{10,9},{11,1... | collective-permute-start | bytes 1572872 | tf_op jit(solution)/shard_map/ppermute | solution.py:25
  20.4 1.6 %copy-start = (bf16[8,2,256,256]{3,2,1,0:T(8,128)(2,1)S(1)}, bf16[8,2,256,256]{3,2,1,0:T(8,128)(2,1)}, u32[]{:S(2)}) copy-start(bf16[8,2,256,256]{3,2,1,0:T(8,128)(2,1)} %constant.43.clone.table_ref) | copy-start | bytes 6291460
  22.0 1.4 %copy-start.1 = (bf16[2,6,256,256]{3,2,1,0:T(8,128)(2,1)S(1)}, bf16[2,6,256,256]{3,2,1,0:T(8,128)(2,1)}, u32[]{:S(2)}) copy-start(bf16[2,6,256,256]{3,2,1,0:T(8,128)(2,1)} %probe_ref.1) | copy-start | bytes 4718596
  23.4 1.0 copy-start.3
  24.5 0.9 copy-start.4
  25.4 1.0 copy-start.2
  25.4 1.0 copy-start.5
  36.2 7.5 %collective-permute-start.6 = (f32[4,4,12,16,128]{4,3,2,1,0:T(8,128)S(1)}, f32[4,4,12,16,128]{4,3,2,1,0:T(8,128)S(1)}, u32[]{:S(2)}, u32[]{:S(2)}) collective-permute-start(f32[4,4,12,16,128]{4,3,2,1,0:T(8,128)S(1)} %get-tuple-element.19), channel_id=1, source_target_pairs={{0,1},{1,0},{2,3},{3,2},{4,5},{5,4},{6,7},{7,6},{8,9},{9,8},{10,11... | collective-permute-start | bytes 4718600 | tf_op jit(solution)/shard_map/ppermute | solution.py:306
  43.8 19.5 %collective-permute-start.7 = (f32[2,4,12,16,128]{4,3,2,1,0:T(8,128)S(1)}, f32[2,4,12,16,128]{4,3,2,1,0:T(8,128)S(1)}, u32[]{:S(2)}, u32[]{:S(2)}) collective-permute-start(f32[2,4,12,16,128]{4,3,2,1,0:T(8,128)S(1)} %get-tuple-element.21), channel_id=1, source_target_pairs={{0,32},{1,97},{32,0},{33,65},{64,96},{65,33},{96,64},{97,1},{2,34}... | collective-permute-start | bytes 2359304 | tf_op jit(solution)/shard_map/ppermute | solution.py:314
  45.7 43.7 %collective-permute-start.4 = (f32[2,256,256]{2,1,0:T(8,128)S(1)}, f32[2,256,256]{2,1,0:T(8,128)S(1)}, u32[]{:S(2)}, u32[]{:S(2)}) collective-permute-start(f32[2,256,256]{2,1,0:T(8,128)S(1)} %get-tuple-element.17), channel_id=1, source_target_pairs={{0,32},{32,64},{64,96},{96,128},{128,160},{160,192},{192,224},{224... | collective-permute-start | bytes 1572872 | tf_op jit(solution)/shard_map/ppermute | solution.py:25
  63.4 11.6 %collective-permute-start.8 = (f32[4,12,16,128]{3,2,1,0:T(8,128)S(1)}, f32[4,12,16,128]{3,2,1,0:T(8,128)S(1)}, u32[]{:S(2)}, u32[]{:S(2)}) collective-permute-start(f32[4,12,16,128]{3,2,1,0:T(8,128)S(1)} %fusion), channel_id=1, source_target_pairs={{0,96},{1,33},{32,64},{33,1},{64,32},{65,97},{96,0},{97,65},{2,98}... | collective-permute-start | bytes 1179656 | tf_op jit(solution)/shard_map/ppermute | solution.py:315
  65.9 8.4 %collective-permute-start.3 = (s32[1,1,1]{2,1,0:T(1,128)}, s32[1,1,1]{2,1,0:T(1,128)}, u32[]{:S(2)}, u32[]{:S(2)}) collective-permute-start(s32[1,1,1]{2,1,0:T(1,128)} %bitcast.4), channel_id=1, source_target_pairs={{0,32},{32,64},{64,96},{96,128},{128,160},{160,192},{192,224},{224... | collective-permute-start | bytes 20 | tf_op jit(solution)/shard_map/ppermute | solution.py:25
  75.9 27.4 %all-to-all-start = ((f32[8,96,128]{2,1,0:T(8,128)}), f32[8,96,128]{2,1,0:T(8,128)S(1)}, u32[]{:S(2)}, u32[]{:S(2)}) async-start(f32[8,96,128]{2,1,0:T(8,128)} %add_columns.1), calls=%async_computation | async-start | bytes 786432 | tf_op jit(solution)/shard_map/all_to_all | solution.py:317
  89.5 38.0 %collective-permute-start.5 = (f32[2,256,256]{2,1,0:T(8,128)S(1)}, f32[2,256,256]{2,1,0:T(8,128)S(1)}, u32[]{:S(2)}, u32[]{:S(2)}) collective-permute-start(f32[2,256,256]{2,1,0:T(8,128)S(1)} %select_add_fusion), channel_id=1, source_target_pairs={{0,1},{1,2},{2,3},{3,4},{4,5},{5,6},{6,7},{7,8},{8,9},{9,10},{10,1... | collective-permute-start | bytes 1572872 | tf_op jit(solution)/shard_map/ppermute | solution.py:25
  104.0 31.8 %all-to-all-start.1 = ((f32[8,16,96]{2,1,0:T(8,128)}), f32[8,16,96]{2,1,0:T(8,128)S(1)}, u32[]{:S(2)}, u32[]{:S(2)}) async-start(f32[8,16,96]{2,1,0:T(8,128)} %add_turn.1), calls=%async_computation.1 | async-start | bytes 131072 | tf_op jit(solution)/shard_map/all_to_all | solution.py:319
where the time goes:
time: 137 us
  starting transfers between devices  64.4 us (47%)
  waiting for transfers between devices  48.5 us (35%)
  Pallas kernels  12.4 us (9%)
  local copies, waits for them, and re-layouts  7.4 us (5%)
  other arithmetic  2.44 us (2%)
  between operations  1.47 us (1%)
    all_to_all x1, starting transfers between devices, local(): parts = lax.all_to_all(turned, 'y', 0, 0, tiled=True)  23.5 us
    ppermute x6, starting transfers between devices, passed_along(): return lax.ppermute(x, axis, pairs)  19.1 us
    ppermute x6, waiting for transfers between devices, passed_along(): return lax.ppermute(x, axis, pairs)  14.6 us
    ppermute x1, waiting for transfers between devices, local(): got = lax.ppermute(send, ('x', 'core'), near_pairs)  14 us
    all_to_all x1, starting transfers between devices, local(): parts = lax.all_to_all(packed, ('z_lo', 'z_hi'), 0, 0, tiled=True)  13.6 us
    pallas_call x1, Pallas kernels, local(): call(main_kernel, 'step', [smem, smem] + [vmem] * 8, [shaped(*block_shape...  9.75 us
    all_to_all x1, waiting for transfers between devices, local(): parts = lax.all_to_all(packed, ('z_lo', 'z_hi'), 0, 0, tiled=True)  9.47 us
    all_to_all x1, waiting for transfers between devices, local(): parts = lax.all_to_all(turned, 'y', 0, 0, tiled=True)  7.44 us
  transfers between devices with their start and end apart: 11, of which 6 were waited for; matrix products, arithmetic and copies ran while one was open for 3% of the time, Pallas kernels for 2%

commit v1 on v0

--- a/solution.py
+++ b/solution.py
@@ -157,20 +157,35 @@
     return rows, cols
 
 
-def prepare_kernel(probe_ref, intensity_ref, table_ref, order_ref, probe_out, measured_out, table_out, order_out):
+def prepare_kernel(
+    probe_in, intensity_in, table_in, order_in, probe_out, measured_out, table_out, order_out,
+    probe_ref, intensity_ref, order_ref, sems,
+):
+    copies = [
+        pltpu.make_async_copy(source, target, sems.at[i])
+        for i, (source, target) in enumerate(
+            [(order_in, order_ref), (intensity_in, intensity_ref), (probe_in, probe_ref), (table_in, table_out)]
+        )
+    ]
+    for copy in copies:
+        copy.start()
+    copies[0].wait()
+    copies[1].wait()
     frequencies, turned, shuffle = order_ref[0], order_ref[1], order_ref[2]
     measured_out[...] = dot(dot(frequencies, intensity_ref[...]).astype(bf16), turned)
+    order_out[0] = shuffle
+    order_out[1] = order_ref[3]
+    copies[2].wait()
     for part in range(2):
         for mode in range(modes):
             probe_out[part, mode] = dot(probe_ref[part, mode], shuffle).astype(bf16)
-    table_out[...] = table_ref[...]
-    order_out[0] = shuffle
-    order_out[1] = order_ref[3]
+    copies[3].wait()
 
 
 def main_kernel(
-    offset_ref, count_ref, own_ref, right_ref, below_ref, diag_ref, probe_ref, measured_ref, table_ref, order_ref,
-    mine_ref, peer_ref, upper_ref, lower_ref, window_ref, far_ref,
+    offset_ref, count_ref, own_re, own_im, right_re, right_im, lower_re, lower_im, probe_ref, measured_ref,
+    table_ref, order_ref, mine_re_ref, mine_im_ref, peer_re_ref, peer_im_ref, stays_ref, moves_ref,
+    window_ref, far_ref,
 ):
     row_offset = offset_ref[0]
     col_offset = offset_ref[1]
@@ -179,10 +194,9 @@
     rows, cols = cells()
     in_row = rows >= row_offset
     in_col = cols >= col_offset
-    for part in range(2):
-        upper = jnp.where(in_col, own_ref[part], right_ref[part])
-        lower = jnp.where(in_col, below_ref[part], diag_ref[part])
-        mixed = jnp.where(in_row, upper, lower)
+    parts = ((own_re, right_re, lower_re), (own_im, right_im, lower_im))
+    for part, (own_ref, right_ref, lower_ref) in enumerate(parts):
+        mixed = jnp.where(in_row, jnp.where(in_col, own_ref[...], right_ref[...]), lower_ref[...])
         mixed = pltpu.roll(mixed, lax.rem(full - row_offset, full), 0)
         window_ref[part] = reorder(pltpu.roll(mixed, lax.rem(full - col_offset, full), 1), order_ref[0])
     sum_even = -measured_ref[:half]
@@ -209,15 +223,31 @@
         probe_re = probe_ref[0, mode].astype(f32)
         probe_im = probe_ref[1, mode].astype(f32)
         near_re, near_im = backward(far_ref[mode, 0] * res_even, far_ref[mode, 1] * res_odd, table_ref)
-        store_strips(mine_ref, peer_ref, mode, win_re * near_re + win_im * near_im, core)
-        store_strips(mine_ref, peer_ref, modes + mode, win_re * near_im - win_im * near_re, core)
+        store_strips(mine_re_ref, peer_re_ref, mode, win_re * near_re + win_im * near_im, core)
+        store_strips(mine_im_ref, peer_im_ref, mode, win_re * near_im - win_im * near_re, core)
         obj_re = obj_re + probe_re * near_re + probe_im * near_im
         obj_im = obj_im + probe_re * near_im - probe_im * near_re
     for part, total in enumerate((obj_re, obj_im)):
         placed = reorder(total, order_ref[1])
         placed = pltpu.roll(pltpu.roll(placed, row_offset, 0), col_offset, 1)
-        upper_ref[part] = jnp.where(in_row, placed, 0.0)
-        lower_ref[part] = jnp.where(in_row, 0.0, placed)
+        stays_ref[part] = jnp.where(in_col, placed, 0.0)
+        moves_ref[part, :full] = jnp.where(in_col, 0.0, placed)
+        moves_ref[part, full:] = jnp.zeros((8, full), f32) + row_offset.astype(f32)
+
+
+def mix_kernel(offset_ref, own_ref, right_ref, out_ref):
+    rows, cols = cells()
+    out_ref[...] = jnp.where(cols >= offset_ref[1], own_ref[...], right_ref[...])
+
+
+def down_kernel(offset_ref, stays_ref, moved_ref, down_ref, held_ref):
+    rows, cols = cells()
+    in_row = rows >= offset_ref[0]
+    left_in_row = rows.astype(f32) >= moved_ref[0, full : full + 1]
+    for part in range(2):
+        stays, moved = stays_ref[part], moved_ref[part, :full]
+        down_ref[part] = jnp.where(in_row, 0.0, stays) + jnp.where(left_in_row, 0.0, moved)
+        held_ref[part] = jnp.where(in_row, stays, 0.0) + jnp.where(left_in_row, moved, 0.0)
 
 
 def cores_kernel(mine_ref, theirs_ref, send_ref, keep_ref):
@@ -229,24 +259,24 @@
         ref[slot] = mine_ref[index] + theirs_ref[index]
 
 
-def columns_kernel(kept_ref, got_ref, came_ref, out_ref):
-    lanes = lax.broadcasted_iota(jnp.int32, (96, half), 1)
-    for z in range(4):
-        total = (kept_ref[0, z] + got_ref[0, z] + came_ref[z]).reshape(192, half)
-        top, bottom = total[:96], total[96:]
-        out_ref[2 * z] = jnp.where(lanes < half // 2, top, pltpu.roll(bottom, half // 2, 1))
-        out_ref[2 * z + 1] = jnp.where(lanes < half // 2, pltpu.roll(top, half // 2, 1), bottom)
-
-
-def turn_kernel(parts_ref, out_ref):
+def columns_kernel(kept_re, got_re, came_re, kept_im, got_im, came_im, out_ref):
+    for part, (kept_ref, got_ref, came_ref) in enumerate(((kept_re, got_re, came_re), (kept_im, got_im, came_im))):
+        for z in range(4):
+            turned = (kept_ref[0, z] + got_ref[0, z] + came_ref[z]).reshape(96, half).T
+            lane = z * 192 + part * 96
+            for y in range(8):
+                for z_hi in range(2):
+                    at = z_hi * 64 + y * 8
+                    out_ref[y, z_hi * 8 : z_hi * 8 + 8, lane : lane + 96] = turned[at : at + 8]
+
+
+def depth_kernel(parts_ref, out_ref):
     total = parts_ref[0]
     for i in range(1, 8):
         total = total + parts_ref[i]
-    turned = total.T
-    for part in range(2):
-        for y in range(8):
-            at = part * 64 + y * 8
-            out_ref[y, part * 8 : part * 8 + 8] = turned[at : at + 8]
+    for z in range(4):
+        for z_hi in range(2):
+            out_ref[2 * z + z_hi] = total[z_hi * 8 : z_hi * 8 + 8, z * 192 : z * 192 + 192]
 
 
 def shaped(*shape, dtype=f32):
@@ -274,62 +304,76 @@
     rows = ("z_lo", "x")
     cols = ("z_hi", "y", "core")
     tables, orders = halves_tables()
-    below = passed_along(object_field, rows, -1)
-    right = passed_along(object_field, cols, -1)
-    diag = passed_along(below, cols, -1)
-    above_offset = passed_along(offsets[:, :, :, 1], rows, 1)
+    above_offset = passed_along(offsets, rows, 1).reshape(2)
+    own = (object_field[0], object_field[1])
+    above_offset, *own = lax.optimization_barrier((above_offset, *own))
+    right = [passed_along(part, cols, -1) for part in own]
+    lower = []
+    for part, beside in zip(own, right):
+        mixed = call(mix_kernel, "mix", [smem, vmem, vmem], [shaped(full, full)], moved=1_000_000)(
+            above_offset, part, beside
+        )
+        lower.append(passed_along(mixed, rows, -1))
+    start = (0, 0, lax.axis_index(rows) * strip, lax.axis_index(cols) * 8)
+    own_probe = lax.dynamic_slice(probe_modes, start, (2, modes, strip, 8)).astype(f32)
     probe, measured, table, order = call(
         prepare_kernel,
         "prepare",
-        [vmem] * 4,
+        [pl.BlockSpec(memory_space=pl.ANY)] * 4,
         [
             shaped(2, modes, full, full, dtype=bf16),
             shaped(full, full),
             shaped(8, 2, full, full, dtype=bf16),
             shaped(2, full, full, dtype=bf16),
         ],
+        scratch=[
+            pltpu.VMEM((2, modes, full, full), bf16),
+            pltpu.VMEM((full, full), bf16),
+            pltpu.VMEM((4, full, full), bf16),
+            pltpu.SemaphoreType.DMA((4,)),
+        ],
         flops=500_000_000,
         moved=8_000_000,
     )(probe_modes, intensity[0, 0, 0], jnp.asarray(tables), jnp.asarray(orders))
-    block_shape = (4, 4, 2 * modes, strip, half)
-    mine, peer, upper, lower = call(
+    block_shape = (4, 4, modes, strip, half)
+    mine_re, mine_im, peer_re, peer_im, stays, moves = call(
         main_kernel,
         "step",
-        [smem, smem] + [vmem] * 8,
-        [shaped(*block_shape), shaped(*block_shape), shaped(2, full, full), shaped(2, full, full)],
+        [smem, smem] + [vmem] * 10,
+        [shaped(*block_shape)] * 4 + [shaped(2, full, full), shaped(2, full + 8, full)],
         scratch=[pltpu.VMEM((2, full, full), f32), pltpu.VMEM((modes, 2, full, full), f32)],
         flops=5_000_000_000,
         moved=12_000_000,
         limit=24,
-    )(offsets.reshape(2), counts.reshape(1), object_field, right, below, diag, probe, measured, table, order)
-
-    theirs = lax.ppermute(peer, "core", [(0, 1), (1, 0)])
-    from_above = passed_along(lower, rows, 1)
-    half_shape = (2, *block_shape[1:])
-    send, keep = call(
-        cores_kernel, "add_cores", [vmem] * 2, [shaped(*half_shape)] * 2, moved=6_000_000
-    )(mine, theirs)
+    )(offsets.reshape(2), counts.reshape(1), *own, *right, *lower, probe, measured, table, order)
+
     near_pairs = [(2 * x + c, 2 * ((x ^ 1) if c == 0 else 3 - x) + c) for x in range(4) for c in range(2)]
     far_pairs = [(2 * x + c, 2 * (3 - x if c == 0 else (x ^ 1)) + c) for x in range(4) for c in range(2)]
-    got = lax.ppermute(send, ("x", "core"), near_pairs)
-    came = lax.ppermute(keep[1] + got[1], ("x", "core"), far_pairs)
-    packed = call(columns_kernel, "add_columns", [vmem] * 3, [shaped(8, 96, half)], moved=2_000_000)(keep, got, came)
+    half_shape = (2, *block_shape[1:])
+    summed = []
+    theirs = [lax.ppermute(peer, "core", [(0, 1), (1, 0)]) for peer in (peer_re, peer_im)]
+    for mine, other in zip((mine_re, mine_im), theirs):
+        send, keep = call(
+            cores_kernel, "add_cores", [vmem] * 2, [shaped(*half_shape)] * 2, moved=3_000_000
+        )(mine, other)
+        summed.append((keep, lax.ppermute(send, ("x", "core"), near_pairs)))
+    from_left = passed_along(moves, cols, 1)
+    arrived = []
+    for keep, got in summed:
+        arrived += [keep, got, lax.ppermute(keep[1] + got[1], ("x", "core"), far_pairs)]
+    packed = call(columns_kernel, "add_columns", [vmem] * 6, [shaped(8, strip, 768)], moved=2_000_000)(*arrived)
+    stays, _ = lax.optimization_barrier((stays, packed))
+    down, held = call(down_kernel, "down", [smem, vmem, vmem], [shaped(2, full, full)] * 2, moved=2_000_000)(
+        offsets.reshape(2), stays, from_left
+    )
+    from_above = passed_along(down, rows, 1)
+    parts = lax.all_to_all(packed, "y", 0, 0, tiled=True)
+    packed = call(depth_kernel, "add_depth", [vmem], [shaped(8, 8, 192)], moved=500_000)(parts)
     parts = lax.all_to_all(packed, ("z_lo", "z_hi"), 0, 0, tiled=True)
-    turned = call(turn_kernel, "add_turn", [vmem], [shaped(8, strip, 96)], moved=500_000)(parts)
-    parts = lax.all_to_all(turned, "y", 0, 0, tiled=True)
-    share = jnp.sum(parts, axis=0).reshape(2, 8, modes, strip).transpose(0, 2, 3, 1)
-    start = (0, 0, lax.axis_index(rows) * strip, lax.axis_index(cols) * 8)
-    own_probe = lax.dynamic_slice(probe_modes, start, (2, modes, strip, 8)).astype(f32)
+    share = jnp.sum(parts, axis=0).reshape(8, 2, modes, strip).transpose(1, 2, 3, 0)
     probe_new = own_probe - (512.0 ** -0.5) * share
 
-    lanes = lax.broadcasted_iota(jnp.int32, (2, full, full), 2)
-    stays = lanes >= offsets[0, 0, 0, 1]
-    above_stays = lanes >= above_offset[0, 0, 0]
-    zero = jnp.zeros((), f32)
-    moves = jnp.where(stays, zero, upper) + jnp.where(above_stays, zero, from_above)
-    from_left = passed_along(moves, cols, 1)
-    held = jnp.where(stays, upper, zero) + jnp.where(above_stays, from_above, zero)
-    object_new = object_field - object_rate * (held + from_left)
+    object_new = object_field - object_rate * (held + from_above)
     return (object_new, probe_new)
 
 

time: 137 us -> 110 us (0.80)
  the two profiles are of different devices: /device:TPU:70 before, /device:TPU:6 now
where the time goes in v1:
time: 110 us
  starting transfers between devices  59.7 us (54%)
  waiting for transfers between devices  27.6 us (25%)
  Pallas kernels  14.7 us (13%)
  local copies, waits for them, and re-layouts  5.11 us (5%)
  between operations  1.56 us (1%)
    ppermute x7, starting transfers between devices, passed_along(): return lax.ppermute(x, axis, pairs)  21.3 us
    all_to_all x1, starting transfers between devices, local(): parts = lax.all_to_all(packed, 'y', 0, 0, tiled=True)  13.7 us
    pallas_call x1, Pallas kernels, local(): call(main_kernel, 'step', [smem, smem] + [vmem] * 10, [shaped(*block_shap...  9.5 us
    all_to_all x1, waiting for transfers between devices, local(): parts = lax.all_to_all(packed, 'y', 0, 0, tiled=True)  8.7 us
    all_to_all x1, waiting for transfers between devices, local(): parts = lax.all_to_all(packed, ('z_lo', 'z_hi'), 0, 0, tiled=True)  6.86 us
    ppermute x2, starting transfers between devices, local(): lax.ppermute(peer, 'core', [(0, 1), (1, 0)])  6.85 us
    all_to_all x1, starting transfers between devices, local(): parts = lax.all_to_all(packed, ('z_lo', 'z_hi'), 0, 0, tiled=True)  6.68 us
    ppermute x2, waiting for transfers between devices, local(): lax.ppermute(keep[1] + got[1], ('x', 'core'), far_pairs)  5.87 us
  transfers between devices with their start and end apart: 15, of which 10 were waited for; matrix products, arithmetic and copies ran while one was open for 3% of the time, Pallas kernels for 5%

profile of v1, /device:TPU:6, one launch (start us, length us, event | category | flops | bytes accessed | tf_op | source)
XLA Modules:
  0.0 109.7 jit_solution(14147146045911139851)
XLA Ops:
  0.6 0.0 copy-start
  0.6 0.0 copy-start.2
  0.7 4.3 %collective-permute-start = (s32[1,1,1,2]{3,2,1,0:T(1,128)}, s32[1,1,1,2]{3,2,1,0:T(1,128)S(1)}, u32[]{:S(2)}, u32[]{:S(2)}) collective-permute-start(s32[1,1,1,2]{3,2,1,0:T(1,128)} %param.9), channel_id=1, source_target_pairs={{0,32},{32,64},{64,96},{96,128},{128,160},{160,192},{192,224},{224... | collective-permute-start | bytes 32 | tf_op jit(solution)/shard_map/ppermute | solution.py:25
  5.0 1.1 slice_bitcast_fusion
  6.1 0.3 collective-permute-done
  6.4 1.3 %collective-permute-start.2 = (f32[256,256]{1,0:T(8,128)S(1)}, f32[256,256]{1,0:T(8,128)S(1)}, u32[]{:S(2)}, u32[]{:S(2)}) collective-permute-start(f32[256,256]{1,0:T(8,128)S(1)} %get-tuple-element.23.own_ref.own_im), channel_id=1, source_target_pairs={{1,0},{2,1},{3,2},{4,3},{5,4},{6,5},{7,6},{8,7},{9,8},{10,9},{11,1... | collective-permute-start | bytes 786440 | tf_op jit(solution)/shard_map/ppermute | solution.py:25
  7.7 1.3 %collective-permute-start.1 = (f32[256,256]{1,0:T(8,128)S(1)}, f32[256,256]{1,0:T(8,128)S(1)}, u32[]{:S(2)}, u32[]{:S(2)}) collective-permute-start(f32[256,256]{1,0:T(8,128)S(1)} %get-tuple-element.22.own_ref.own_re), channel_id=1, source_target_pairs={{1,0},{2,1},{3,2},{4,3},{5,4},{6,5},{7,6},{8,7},{9,8},{10,9},{11,1... | collective-permute-start | bytes 786440 | tf_op jit(solution)/shard_map/ppermute | solution.py:25
  9.0 0.8 collective-permute-done.2.right_ref.right_im
  9.8 0.6 mix.3
  10.4 2.7 %collective-permute-start.4 = (f32[256,256]{1,0:T(8,128)S(1)}, f32[256,256]{1,0:T(8,128)S(1)}, u32[]{:S(2)}, u32[]{:S(2)}) collective-permute-start(f32[256,256]{1,0:T(8,128)S(1)} %mix.3), channel_id=1, source_target_pairs={{32,0},{64,32},{96,64},{128,96},{160,128},{192,160},{224,192},{256... | collective-permute-start | bytes 786440 | tf_op jit(solution)/shard_map/ppermute | solution.py:25
  13.1 0.0 collective-permute-done.1.right_ref.right_re
  13.1 0.6 mix.2
  13.7 5.7 %collective-permute-start.3 = (f32[256,256]{1,0:T(8,128)S(1)}, f32[256,256]{1,0:T(8,128)S(1)}, u32[]{:S(2)}, u32[]{:S(2)}) collective-permute-start(f32[256,256]{1,0:T(8,128)S(1)} %mix.2), channel_id=1, source_target_pairs={{32,0},{64,32},{96,64},{128,96},{160,128},{192,160},{224,192},{256... | collective-permute-start | bytes 786440 | tf_op jit(solution)/shard_map/ppermute | solution.py:25
  20.1 0.0 copy-done
  20.1 0.0 copy-done.2
  20.1 0.0 copy-start.1
  20.1 1.4 %copy-done.1 = bf16[2,6,256,256]{3,2,1,0:T(8,128)(2,1)S(1)} copy-done((bf16[2,6,256,256]{3,2,1,0:T(8,128)(2,1)S(1)}, bf16[2,6,256,256]{3,2,1,0:T(8,128)(2,1)}, u32[]{:S(2)}) %copy-start.1) | copy-done | bytes 1572888
  21.5 0.0 copy-start.3
  21.5 0.9 copy-done.3
  22.4 0.0 copy-start.4
  22.4 1.4 %prepare.1 = (bf16[2,6,256,256]{3,2,1,0:T(8,128)(2,1)S(1)}, f32[256,256]{1,0:T(8,128)S(1)}, bf16[8,2,256,256]{3,2,1,0:T(8,128)(2,1)S(1)}, bf16[2,256,256]{2,1,0:T(8,128)(2,1)S(1)}) custom-call(bf16[2,6,256,256]{3,2,1,0:T(8,128)(2,1)S(1)} %copy-done.1, bf16[256,256]{1,0:T(8,128)(2,1)S(1)} %bitcast.15, bf16[8,2,256,256]{3,2,1,0:T(8,128)(2,1)S(1)} %copy-done, ...), custom_call_target="tpu_custom_call" | custom-call | flops 500000000 | bytes 8000000 | tf_op jit(solution)/shard_map/prepare/pallas_call | solution.py:319
  23.8 0.0 collective-permute-done.4.lower_im
  23.8 2.7 %collective-permute-done.3.lower_re = f32[256,256]{1,0:T(8,128)S(1)} collective-permute-done((f32[256,256]{1,0:T(8,128)S(1)}, f32[256,256]{1,0:T(8,128)S(1)}, u32[]{:S(2)}, u32[]{:S(2)}) %collective-permute-start.3) | collective-permute-done | bytes 262176 | tf_op jit(solution)/shard_map/ppermute | solution.py:25
  26.5 0.0 copy-done.4
  26.5 9.5 %step.1 = (f32[4,4,6,16,128]{4,3,2,1,0:T(8,128)S(1)}, f32[4,4,6,16,128]{4,3,2,1,0:T(8,128)S(1)}, f32[4,4,6,16,128]{4,3,2,1,0:T(8,128)S(1)}, f32[4,4,6,16,128]{4,...) custom-call(s32[2]{0:T(128)S(1)} %bitcast.18, s32[1]{0:T(128)} %bitcast.14.count_ref, ...), custom_call_target="tpu_custom_call" | custom-call | flops 5000000000 | bytes 12000000 | tf_op jit(solution)/shard_map/step/pallas_call | solution.py:339
  36.0 4.9 %collective-permute-start.8 = (f32[4,4,6,16,128]{4,3,2,1,0:T(8,128)S(1)}, f32[4,4,6,16,128]{4,3,2,1,0:T(8,128)S(1)}, u32[]{:S(2)}, u32[]{:S(2)}) collective-permute-start(f32[4,4,6,16,128]{4,3,2,1,0:T(8,128)S(1)} %get-tuple-element.35), channel_id=1, source_target_pairs={{0,1},{1,0},{2,3},{3,2},{4,5},{5,4},{6,7},{7,6},{8,9},{9,8},{10,11... | collective-permute-start | bytes 2359304 | tf_op jit(solution)/shard_map/ppermute | solution.py:354
  40.9 1.9 %collective-permute-start.5 = (f32[4,4,6,16,128]{4,3,2,1,0:T(8,128)S(1)}, f32[4,4,6,16,128]{4,3,2,1,0:T(8,128)S(1)}, u32[]{:S(2)}, u32[]{:S(2)}) collective-permute-start(f32[4,4,6,16,128]{4,3,2,1,0:T(8,128)S(1)} %get-tuple-element.31), channel_id=1, source_target_pairs={{0,1},{1,0},{2,3},{3,2},{4,5},{5,4},{6,7},{7,6},{8,9},{9,8},{10,11... | collective-permute-start | bytes 2359304 | tf_op jit(solution)/shard_map/ppermute | solution.py:354
  42.9 0.0 collective-permute-done.8.theirs_ref
  42.9 0.1 add_cores.3
  43.0 1.9 %collective-permute-start.9 = (f32[2,4,6,16,128]{4,3,2,1,0:T(8,128)S(1)}, f32[2,4,6,16,128]{4,3,2,1,0:T(8,128)S(1)}, u32[]{:S(2)}, u32[]{:S(2)}) collective-permute-start(f32[2,4,6,16,128]{4,3,2,1,0:T(8,128)S(1)} %get-tuple-element.37), channel_id=1, source_target_pairs={{0,32},{1,97},{32,0},{33,65},{64,96},{65,33},{96,64},{97,1},{2,34}... | collective-permute-start | bytes 1179656 | tf_op jit(solution)/shard_map/ppermute | solution.py:359
  44.9 0.2 collective-permute-done.5.theirs_ref
  45.1 0.1 add_cores.2
  45.2 3.7 %collective-permute-start.6 = (f32[2,4,6,16,128]{4,3,2,1,0:T(8,128)S(1)}, f32[2,4,6,16,128]{4,3,2,1,0:T(8,128)S(1)}, u32[]{:S(2)}, u32[]{:S(2)}) collective-permute-start(f32[2,4,6,16,128]{4,3,2,1,0:T(8,128)S(1)} %get-tuple-element.33), channel_id=1, source_target_pairs={{0,32},{1,97},{32,0},{33,65},{64,96},{65,33},{96,64},{97,1},{2,34}... | collective-permute-start | bytes 1179656 | tf_op jit(solution)/shard_map/ppermute | solution.py:359
  48.9 3.1 %collective-permute-start.11 = (f32[2,264,256]{2,1,0:T(8,128)S(1)}, f32[2,264,256]{2,1,0:T(8,128)S(1)}, u32[]{:S(2)}, u32[]{:S(2)}) collective-permute-start(f32[2,264,256]{2,1,0:T(8,128)S(1)} %get-tuple-element.39), channel_id=1, source_target_pairs={{0,1},{1,2},{2,3},{3,4},{4,5},{5,6},{6,7},{7,8},{8,9},{9,10},{10,1... | collective-permute-start | bytes 1622024 | tf_op jit(solution)/shard_map/ppermute | solution.py:25
  52.0 0.6 collective-permute-done.9.got_im
  52.7 2.7 %collective-permute-start.10 = (f32[4,6,16,128]{3,2,1,0:T(8,128)S(1)}, f32[4,6,16,128]{3,2,1,0:T(8,128)S(1)}, u32[]{:S(2)}, u32[]{:S(2)}) collective-permute-start(f32[4,6,16,128]{3,2,1,0:T(8,128)S(1)} %fusion), channel_id=1, source_target_pairs={{0,96},{1,33},{32,64},{33,1},{64,32},{65,97},{96,0},{97,65},{2,98}... | collective-permute-start | bytes 589832 | tf_op jit(solution)/shard_map/ppermute | solution.py:363
  55.3 1.5 %collective-permute-done.6.got_re = f32[2,4,6,16,128]{4,3,2,1,0:T(8,128)S(1)} collective-permute-done((f32[2,4,6,16,128]{4,3,2,1,0:T(8,128)S(1)}, f32[2,4,6,16,128]{4,3,2,1,0:T(8,128)S(1)}, u32[]{:S(2)}, u32[]{:S(2)}) %collective-permute-start.6) | collective-permute-done | bytes 393248 | tf_op jit(solution)/shard_map/ppermute | solution.py:359
  56.9 2.9 %collective-permute-start.7 = (f32[4,6,16,128]{3,2,1,0:T(8,128)S(1)}, f32[4,6,16,128]{3,2,1,0:T(8,128)S(1)}, u32[]{:S(2)}, u32[]{:S(2)}) collective-permute-start(f32[4,6,16,128]{3,2,1,0:T(8,128)S(1)} %fusion.1), channel_id=1, source_target_pairs={{0,96},{1,33},{32,64},{33,1},{64,32},{65,97},{96,0},{97,65},{2,98}... | collective-permute-start | bytes 589832 | tf_op jit(solution)/shard_map/ppermute | solution.py:363
  59.8 1.7 %collective-permute-done.10.came_im = f32[4,6,16,128]{3,2,1,0:T(8,128)S(1)} collective-permute-done((f32[4,6,16,128]{3,2,1,0:T(8,128)S(1)}, f32[4,6,16,128]{3,2,1,0:T(8,128)S(1)}, u32[]{:S(2)}, u32[]{:S(2)}) %collective-permute-start.10) | collective-permute-done | bytes 196640 | tf_op jit(solution)/shard_map/ppermute | solution.py:363
  61.4 4.2 %collective-permute-done.7.came_re = f32[4,6,16,128]{3,2,1,0:T(8,128)S(1)} collective-permute-done((f32[4,6,16,128]{3,2,1,0:T(8,128)S(1)}, f32[4,6,16,128]{3,2,1,0:T(8,128)S(1)}, u32[]{:S(2)}, u32[]{:S(2)}) %collective-permute-start.7) | collective-permute-done | bytes 196640 | tf_op jit(solution)/shard_map/ppermute | solution.py:363
  65.7 1.1 add_columns.1
  66.7 0.0 copy-start.5
  66.7 13.7 %all-to-all-start = ((f32[8,16,768]{2,1,0:T(8,128)}), f32[8,16,768]{2,1,0:T(8,128)S(1)}, u32[]{:S(2)}, u32[]{:S(2)}) async-start(f32[8,16,768]{2,1,0:T(8,128)} %add_columns.1), calls=%async_computation | async-start | bytes 786432 | tf_op jit(solution)/shard_map/all_to_all | solution.py:370
  80.4 0.0 collective-permute-done.11.moved_ref
  80.4 0.7 down.1
  81.1 2.9 %collective-permute-start.12 = (f32[2,256,256]{2,1,0:T(8,128)S(1)}, f32[2,256,256]{2,1,0:T(8,128)S(1)}, u32[]{:S(2)}, u32[]{:S(2)}) collective-permute-start(f32[2,256,256]{2,1,0:T(8,128)S(1)} %get-tuple-element.41), channel_id=1, source_target_pairs={{0,32},{32,64},{64,96},{96,128},{128,160},{160,192},{192,224},{224... | collective-permute-start | bytes 1572872 | tf_op jit(solution)/shard_map/ppermute | solution.py:25
  84.0 0.9 constant_dynamic-slice_fusion
  84.9 0.1 copy.12
  85.0 8.7 %all-to-all-done.parts_ref = f32[8,16,768]{2,1,0:T(8,128)S(1)} async-done(((f32[8,16,768]{2,1,0:T(8,128)}), f32[8,16,768]{2,1,0:T(8,128)S(1)}, u32[]{:S(2)}, u32[]{:S(2)}) %all-to-all-start) | async-done | bytes 393248 | tf_op jit(solution)/shard_map/all_to_all | solution.py:370
  93.7 0.7 add_depth.1
  94.5 6.7 %all-to-all-start.1 = ((f32[8,8,192]{2,1,0:T(8,128)}), f32[8,8,192]{2,1,0:T(8,128)S(1)}, u32[]{:S(2)}, u32[]{:S(2)}) async-start(f32[8,8,192]{2,1,0:T(8,128)} %add_depth.1), calls=%async_computation.1 | async-start | bytes 131072 | tf_op jit(solution)/shard_map/all_to_all | solution.py:372
  101.1 0.0 collective-permute-done.12
  101.1 0.0 copy-done.5
  101.1 0.9 multiply_subtract_fusion
  102.0 6.9 %all-to-all-done.1 = f32[8,8,192]{2,1,0:T(8,128)S(1)} async-done(((f32[8,8,192]{2,1,0:T(8,128)}), f32[8,8,192]{2,1,0:T(8,128)S(1)}, u32[]{:S(2)}, u32[]{:S(2)}) %all-to-all-start.1) | async-done | bytes 49184 | tf_op jit(solution)/shard_map/all_to_all | solution.py:372
  108.9 0.1 mul.42
  109.0 0.6 copy.11
  (5 shorter events, 0.1 us)
Async XLA Ops:
  0.6 19.4 %copy-start = (bf16[8,2,256,256]{3,2,1,0:T(8,128)(2,1)S(1)}, bf16[8,2,256,256]{3,2,1,0:T(8,128)(2,1)}, u32[]{:S(2)}) copy-start(bf16[8,2,256,256]{3,2,1,0:T(8,128)(2,1)} %constant.43.clone.table_in) | copy-start | bytes 6291460
  0.6 19.4 %copy-start.2 = (bf16[4,256,256]{2,1,0:T(8,128)(2,1)S(1)}, bf16[4,256,256]{2,1,0:T(8,128)(2,1)}, u32[]{:S(2)}) copy-start(bf16[4,256,256]{2,1,0:T(8,128)(2,1)} %constant.44.clone.order_in) | copy-start | bytes 1572868
  0.7 5.7 %collective-permute-start = (s32[1,1,1,2]{3,2,1,0:T(1,128)}, s32[1,1,1,2]{3,2,1,0:T(1,128)S(1)}, u32[]{:S(2)}, u32[]{:S(2)}) collective-permute-start(s32[1,1,1,2]{3,2,1,0:T(1,128)} %param.9), channel_id=1, source_target_pairs={{0,32},{32,64},{64,96},{96,128},{128,160},{160,192},{192,224},{224... | collective-permute-start | bytes 32 | tf_op jit(solution)/shard_map/ppermute | solution.py:25
  6.4 3.4 %collective-permute-start.2 = (f32[256,256]{1,0:T(8,128)S(1)}, f32[256,256]{1,0:T(8,128)S(1)}, u32[]{:S(2)}, u32[]{:S(2)}) collective-permute-start(f32[256,256]{1,0:T(8,128)S(1)} %get-tuple-element.23.own_ref.own_im), channel_id=1, source_target_pairs={{1,0},{2,1},{3,2},{4,3},{5,4},{6,5},{7,6},{8,7},{9,8},{10,9},{11,1... | collective-permute-start | bytes 786440 | tf_op jit(solution)/shard_map/ppermute | solution.py:25
  7.7 5.4 %collective-permute-start.1 = (f32[256,256]{1,0:T(8,128)S(1)}, f32[256,256]{1,0:T(8,128)S(1)}, u32[]{:S(2)}, u32[]{:S(2)}) collective-permute-start(f32[256,256]{1,0:T(8,128)S(1)} %get-tuple-element.22.own_ref.own_re), channel_id=1, source_target_pairs={{1,0},{2,1},{3,2},{4,3},{5,4},{6,5},{7,6},{8,7},{9,8},{10,9},{11,1... | collective-permute-start | bytes 786440 | tf_op jit(solution)/shard_map/ppermute | solution.py:25
  10.4 13.4 %collective-permute-start.4 = (f32[256,256]{1,0:T(8,128)S(1)}, f32[256,256]{1,0:T(8,128)S(1)}, u32[]{:S(2)}, u32[]{:S(2)}) collective-permute-start(f32[256,256]{1,0:T(8,128)S(1)} %mix.3), channel_id=1, source_target_pairs={{32,0},{64,32},{96,64},{128,96},{160,128},{192,160},{224,192},{256... | collective-permute-start | bytes 786440 | tf_op jit(solution)/shard_map/ppermute | solution.py:25
  13.7 12.8 %collective-permute-start.3 = (f32[256,256]{1,0:T(8,128)S(1)}, f32[256,256]{1,0:T(8,128)S(1)}, u32[]{:S(2)}, u32[]{:S(2)}) collective-permute-start(f32[256,256]{1,0:T(8,128)S(1)} %mix.2), channel_id=1, source_target_pairs={{32,0},{64,32},{96,64},{128,96},{160,128},{192,160},{224,192},{256... | collective-permute-start | bytes 786440 | tf_op jit(solution)/shard_map/ppermute | solution.py:25
  20.1 1.4 %copy-start.1 = (bf16[2,6,256,256]{3,2,1,0:T(8,128)(2,1)S(1)}, bf16[2,6,256,256]{3,2,1,0:T(8,128)(2,1)}, u32[]{:S(2)}) copy-start(bf16[2,6,256,256]{3,2,1,0:T(8,128)(2,1)} %probe_in.1) | copy-start | bytes 4718596
  21.5 0.9 copy-start.3
  22.4 4.1 %copy-start.4 = (s32[1,1,1,2]{3,2,1,0:T(1,128)S(1)}, s32[1,1,1,2]{3,2,1,0:T(1,128)}, u32[]{:S(2)}) copy-start(s32[1,1,1,2]{3,2,1,0:T(1,128)} %param.9) | copy-start | bytes 28
  36.0 6.9 %collective-permute-start.8 = (f32[4,4,6,16,128]{4,3,2,1,0:T(8,128)S(1)}, f32[4,4,6,16,128]{4,3,2,1,0:T(8,128)S(1)}, u32[]{:S(2)}, u32[]{:S(2)}) collective-permute-start(f32[4,4,6,16,128]{4,3,2,1,0:T(8,128)S(1)} %get-tuple-element.35), channel_id=1, source_target_pairs={{0,1},{1,0},{2,3},{3,2},{4,5},{5,4},{6,7},{7,6},{8,9},{9,8},{10,11... | collective-permute-start | bytes 2359304 | tf_op jit(solution)/shard_map/ppermute | solution.py:354
  40.9 4.2 %collective-permute-start.5 = (f32[4,4,6,16,128]{4,3,2,1,0:T(8,128)S(1)}, f32[4,4,6,16,128]{4,3,2,1,0:T(8,128)S(1)}, u32[]{:S(2)}, u32[]{:S(2)}) collective-permute-start(f32[4,4,6,16,128]{4,3,2,1,0:T(8,128)S(1)} %get-tuple-element.31), channel_id=1, source_target_pairs={{0,1},{1,0},{2,3},{3,2},{4,5},{5,4},{6,7},{7,6},{8,9},{9,8},{10,11... | collective-permute-start | bytes 2359304 | tf_op jit(solution)/shard_map/ppermute | solution.py:354
  43.0 9.7 %collective-permute-start.9 = (f32[2,4,6,16,128]{4,3,2,1,0:T(8,128)S(1)}, f32[2,4,6,16,128]{4,3,2,1,0:T(8,128)S(1)}, u32[]{:S(2)}, u32[]{:S(2)}) collective-permute-start(f32[2,4,6,16,128]{4,3,2,1,0:T(8,128)S(1)} %get-tuple-element.37), channel_id=1, source_target_pairs={{0,32},{1,97},{32,0},{33,65},{64,96},{65,33},{96,64},{97,1},{2,34}... | collective-permute-start | bytes 1179656 | tf_op jit(solution)/shard_map/ppermute | solution.py:359
  45.2 11.7 %collective-permute-start.6 = (f32[2,4,6,16,128]{4,3,2,1,0:T(8,128)S(1)}, f32[2,4,6,16,128]{4,3,2,1,0:T(8,128)S(1)}, u32[]{:S(2)}, u32[]{:S(2)}) collective-permute-start(f32[2,4,6,16,128]{4,3,2,1,0:T(8,128)S(1)} %get-tuple-element.33), channel_id=1, source_target_pairs={{0,32},{1,97},{32,0},{33,65},{64,96},{65,33},{96,64},{97,1},{2,34}... | collective-permute-start | bytes 1179656 | tf_op jit(solution)/shard_map/ppermute | solution.py:359
  48.9 31.5 %collective-permute-start.11 = (f32[2,264,256]{2,1,0:T(8,128)S(1)}, f32[2,264,256]{2,1,0:T(8,128)S(1)}, u32[]{:S(2)}, u32[]{:S(2)}) collective-permute-start(f32[2,264,256]{2,1,0:T(8,128)S(1)} %get-tuple-element.39), channel_id=1, source_target_pairs={{0,1},{1,2},{2,3},{3,4},{4,5},{5,6},{6,7},{7,8},{8,9},{9,10},{10,1... | collective-permute-start | bytes 1622024 | tf_op jit(solution)/shard_map/ppermute | solution.py:25
  52.7 8.8 %collective-permute-start.10 = (f32[4,6,16,128]{3,2,1,0:T(8,128)S(1)}, f32[4,6,16,128]{3,2,1,0:T(8,128)S(1)}, u32[]{:S(2)}, u32[]{:S(2)}) collective-permute-start(f32[4,6,16,128]{3,2,1,0:T(8,128)S(1)} %fusion), channel_id=1, source_target_pairs={{0,96},{1,33},{32,64},{33,1},{64,32},{65,97},{96,0},{97,65},{2,98}... | collective-permute-start | bytes 589832 | tf_op jit(solution)/shard_map/ppermute | solution.py:363
  56.9 8.8 %collective-permute-start.7 = (f32[4,6,16,128]{3,2,1,0:T(8,128)S(1)}, f32[4,6,16,128]{3,2,1,0:T(8,128)S(1)}, u32[]{:S(2)}, u32[]{:S(2)}) collective-permute-start(f32[4,6,16,128]{3,2,1,0:T(8,128)S(1)} %fusion.1), channel_id=1, source_target_pairs={{0,96},{1,33},{32,64},{33,1},{64,32},{65,97},{96,0},{97,65},{2,98}... | collective-permute-start | bytes 589832 | tf_op jit(solution)/shard_map/ppermute | solution.py:363
  66.7 34.4 %copy-start.5 = (f32[2,256,256]{2,1,0:T(8,128)S(1)}, f32[2,256,256]{2,1,0:T(8,128)}, u32[]{:S(2)}) copy-start(f32[2,256,256]{2,1,0:T(8,128)} %param.7) | copy-start | bytes 1572868
  66.7 27.0 %all-to-all-start = ((f32[8,16,768]{2,1,0:T(8,128)}), f32[8,16,768]{2,1,0:T(8,128)S(1)}, u32[]{:S(2)}, u32[]{:S(2)}) async-start(f32[8,16,768]{2,1,0:T(8,128)} %add_columns.1), calls=%async_computation | async-start | bytes 786432 | tf_op jit(solution)/shard_map/all_to_all | solution.py:370
  81.1 20.0 %collective-permute-start.12 = (f32[2,256,256]{2,1,0:T(8,128)S(1)}, f32[2,256,256]{2,1,0:T(8,128)S(1)}, u32[]{:S(2)}, u32[]{:S(2)}) collective-permute-start(f32[2,256,256]{2,1,0:T(8,128)S(1)} %get-tuple-element.41), channel_id=1, source_target_pairs={{0,32},{32,64},{64,96},{96,128},{128,160},{160,192},{192,224},{224... | collective-permute-start | bytes 1572872 | tf_op jit(solution)/shard_map/ppermute | solution.py:25
  94.5 14.4 %all-to-all-start.1 = ((f32[8,8,192]{2,1,0:T(8,128)}), f32[8,8,192]{2,1,0:T(8,128)S(1)}, u32[]{:S(2)}, u32[]{:S(2)}) async-start(f32[8,8,192]{2,1,0:T(8,128)} %add_depth.1), calls=%async_computation.1 | async-start | bytes 131072 | tf_op jit(solution)/shard_map/all_to_all | solution.py:372

commit v2 on v1

--- a/solution.py
+++ b/solution.py
@@ -62,71 +62,118 @@
     return jnp.dot(a, b, preferred_element_type=f32)
 
 
-def data_by_table(x, table_ref, which):
-    high, low = split(x)
+def data_by_table(high, low, table_ref, which):
     table_high, table_low = table_ref[which, 0], table_ref[which, 1]
-    return dot(
-        jnp.concatenate([high, high, low], axis=1),
-        jnp.concatenate([table_high, table_low, table_high], axis=0),
-    )
-
-
-def table_by_data(table_ref, which, x):
-    high, low = split(x)
+    return dot(high, table_high) + (dot(high, table_low) + dot(low, table_high))
+
+
+def table_by_data(table_ref, which, high, low):
     table_high, table_low = table_ref[which, 0], table_ref[which, 1]
-    return dot(
-        jnp.concatenate([table_high, table_low, table_high], axis=1),
-        jnp.concatenate([high, high, low], axis=0),
-    )
-
-
-def forward(exit_re, exit_im, table_ref):
-    rows = []
-    for sign, which in ((1.0, 0), (-1.0, 2)):
-        folded = jnp.concatenate(
-            [
-                exit_re[:, :half] + sign * exit_re[:, half:],
-                exit_im[:, :half] + sign * exit_im[:, half:],
-            ],
-            axis=1,
+    return dot(table_high, high) + (dot(table_low, high) + dot(table_high, low))
+
+
+def put(high_ref, low_ref, index, at, left, right):
+    high, low = split(jnp.concatenate([left, right], axis=1))
+    high_ref[index, at : at + strip] = high
+    low_ref[index, at : at + strip] = low
+
+
+def beside(products, strips):
+    count = len(products)
+    for i, product in enumerate(products):
+        product()
+        for work in strips[i * len(strips) // count : (i + 1) * len(strips) // count]:
+            work()
+
+
+def step_stages(mode, core, refs):
+    (probe_ref, window_ref, table_ref, a_high, a_low, b_high, b_low, mid_ref, near_ref, far_ref, sum_ref, obj_ref,
+     mine_re_ref, mine_im_ref, peer_re_ref, peer_im_ref) = refs
+    p = 2 * (mode % 2)
+
+    def exits(r):
+        at = slice(r, r + strip)
+        probe_re, probe_im = probe_ref[0, mode, at].astype(f32), probe_ref[1, mode, at].astype(f32)
+        win_re, win_im = window_ref[0, at], window_ref[1, at]
+        re = probe_re * win_re - probe_im * win_im
+        im = probe_re * win_im + probe_im * win_re
+        put(a_high, a_low, p, r, re[:, :half] + re[:, half:], im[:, :half] + im[:, half:])
+        put(a_high, a_low, p + 1, r, re[:, :half] - re[:, half:], im[:, :half] - im[:, half:])
+
+    def far_columns(odd):
+        mid_ref[p + odd] = data_by_table(a_high[p + odd], a_low[p + odd], table_ref, 4 + 2 * odd)
+
+    def folds(r):
+        even_top, even_bottom = mid_ref[p, r : r + strip], mid_ref[p, half + r : half + r + strip]
+        odd_top, odd_bottom = mid_ref[p + 1, r : r + strip], mid_ref[p + 1, half + r : half + r + strip]
+        for odd, even_fold, odd_fold in (
+            (0, even_top + even_bottom, odd_top + odd_bottom),
+            (1, even_top - even_bottom, odd_top - odd_bottom),
+        ):
+            put(b_high, b_low, p + odd, r, even_fold[:, :half], odd_fold[:, :half])
+            put(b_high, b_low, p + odd, half + r, even_fold[:, half:], odd_fold[:, half:])
+
+    def far_rows(odd):
+        far_ref[mode, odd] = table_by_data(table_ref, 1 + 2 * odd, b_high[p + odd], b_low[p + odd])
+
+    def sums(odd, r):
+        re, im = far_ref[mode, odd, r : r + strip], far_ref[mode, odd, half + r : half + r + strip]
+        sum_ref[odd, r : r + strip] += re * re + im * im
+
+    def scale(odd, r):
+        residual = sum_ref[odd, r : r + strip]
+        for at in (r, half + r):
+            scaled = far_ref[mode, odd, at : at + strip] * residual
+            put(b_high, b_low, p + odd, at, scaled[:, :half], scaled[:, half:])
+
+    def near_rows(odd):
+        mid_ref[p + odd] = table_by_data(table_ref, 2 * odd, b_high[p + odd], b_low[p + odd])
+
+    def unfolds(r):
+        even_re, even_im = mid_ref[p, r : r + strip], mid_ref[p, half + r : half + r + strip]
+        odd_re, odd_im = mid_ref[p + 1, r : r + strip], mid_ref[p + 1, half + r : half + r + strip]
+        for at, re, im in ((r, even_re + odd_re, even_im + odd_im), (half + r, even_re - odd_re, even_im - odd_im)):
+            put(a_high, a_low, p, at, re[:, :half], im[:, :half])
+            put(a_high, a_low, p + 1, at, re[:, half:], im[:, half:])
+
+    def near_columns(odd):
+        near_ref[p + odd] = data_by_table(a_high[p + odd], a_low[p + odd], table_ref, 5 + 2 * odd)
+
+    def grads(r):
+        gradients(
+            mode, r, core, probe_ref, window_ref, near_ref, obj_ref, mine_re_ref, mine_im_ref, peer_re_ref, peer_im_ref
         )
-        rows.append(data_by_table(folded, table_ref, 4 + which))
-    even, odd = rows
-    outs = []
-    for sign, which in ((1.0, 1), (-1.0, 3)):
-        fold_even = even[:half] + sign * even[half:]
-        fold_odd = odd[:half] + sign * odd[half:]
-        stacked = jnp.concatenate(
-            [
-                jnp.concatenate([fold_even[:, :half], fold_odd[:, :half]], axis=1),
-                jnp.concatenate([fold_even[:, half:], fold_odd[:, half:]], axis=1),
-            ],
-            axis=0,
-        )
-        outs.append(table_by_data(table_ref, which, stacked))
-    return outs
-
-
-def backward(even, odd, table_ref):
-    part_even = table_by_data(table_ref, 0, even)
-    part_odd = table_by_data(table_ref, 2, odd)
-    upper = part_even + part_odd
-    lower = part_even - part_odd
-    rows_re = jnp.concatenate([upper[:half], lower[:half]], axis=0)
-    rows_im = jnp.concatenate([upper[half:], lower[half:]], axis=0)
-    cols_even = data_by_table(
-        jnp.concatenate([rows_re[:, :half], rows_im[:, :half]], axis=1), table_ref, 5
-    )
-    cols_odd = data_by_table(
-        jnp.concatenate([rows_re[:, half:], rows_im[:, half:]], axis=1), table_ref, 7
-    )
-    near_re = jnp.concatenate(
-        [cols_even[:, :half] + cols_odd[:, :half], cols_even[:, :half] - cols_odd[:, :half]], axis=1
-    )
-    near_im = jnp.concatenate(
-        [cols_even[:, half:] + cols_odd[:, half:], cols_even[:, half:] - cols_odd[:, half:]], axis=1
-    )
-    return near_re, near_im
+
+    both = range(2)
+    long, short = range(0, full, strip), range(0, half, strip)
+    ahead = (
+        [functools.partial(exits, r) for r in long],
+        [functools.partial(far_columns, odd) for odd in both],
+        [functools.partial(folds, r) for r in short],
+        [functools.partial(far_rows, odd) for odd in both],
+        [functools.partial(sums, odd, r) for odd in both for r in short],
+    )
+    back = (
+        [functools.partial(scale, odd, r) for odd in both for r in short],
+        [functools.partial(near_rows, odd) for odd in both],
+        [functools.partial(unfolds, r) for r in short],
+        [functools.partial(near_columns, odd) for odd in both],
+        [functools.partial(grads, r) for r in long],
+    )
+    return ahead, back
+
+
+def pipelined(stages):
+    none = ([], [], [], [], [])
+    item = lambda i: stages[i] if 0 <= i < len(stages) else none
+    for work in item(0)[0]:
+        work()
+    beside(item(0)[1], item(1)[0])
+    for i in range(len(stages)):
+        beside(item(i + 1)[1] or [lambda: None], item(i)[2])
+        beside(item(i)[3], item(i - 1)[4] + item(i + 2)[0])
+    for work in item(len(stages) - 1)[4]:
+        work()
 
 
 def reorder(x, order):
@@ -137,18 +184,37 @@
     return dot(jnp.concatenate([high, mid, low], axis=1), jnp.concatenate([order, order, order], axis=0))
 
 
-def store_strips(mine_ref, peer_ref, index, value, core):
-    left, right = value[:, :half], value[:, half:]
-    lanes = lax.broadcasted_iota(jnp.int32, (full, half), 1)
+def store_strip(mine_ref, peer_ref, mode, r, left, right, core):
+    z, x = r // strip // 4, r // strip % 4
+    lanes = lax.broadcasted_iota(jnp.int32, (strip, half), 1)
     first = jnp.where(lanes < half // 2, left, pltpu.roll(right, half // 2, 1))
     second = jnp.where(lanes < half // 2, pltpu.roll(left, half // 2, 1), right)
-    mine = jnp.where(core == 0, first, second)
-    peer = jnp.where(core == 0, second, first)
-    for z in range(4):
-        for x in range(4):
-            at = (z * 4 + x) * strip
-            mine_ref[x, z, index] = mine[at : at + strip]
-            peer_ref[x, z, index] = peer[at : at + strip]
+    mine_ref[x, z, mode] = jnp.where(core == 0, first, second)
+    peer_ref[x, z, mode] = jnp.where(core == 0, second, first)
+
+
+def gradients(mode, r, core, probe_ref, window_ref, mid_ref, obj_ref, mine_re_ref, mine_im_ref, peer_re_ref, peer_im_ref):
+    a = 2 * (mode % 2)
+    at = slice(r, r + strip)
+    even, odd = mid_ref[a, at], mid_ref[a + 1, at]
+    up, down = even + odd, even - odd
+    parts_re, parts_im = [], []
+    for side, near in enumerate((up, down)):
+        lanes = slice(side * half, side * half + half)
+        near_re, near_im = near[:, :half], near[:, half:]
+        probe_re, probe_im = probe_ref[0, mode, at, lanes].astype(f32), probe_ref[1, mode, at, lanes].astype(f32)
+        win_re, win_im = window_ref[0, at, lanes], window_ref[1, at, lanes]
+        parts_re.append(win_re * near_re + win_im * near_im)
+        parts_im.append(win_re * near_im - win_im * near_re)
+        obj_re = probe_re * near_re + probe_im * near_im
+        obj_im = probe_re * near_im - probe_im * near_re
+        if mode:
+            obj_re = obj_re + obj_ref[0, at, lanes]
+            obj_im = obj_im + obj_ref[1, at, lanes]
+        obj_ref[0, at, lanes] = obj_re
+        obj_ref[1, at, lanes] = obj_im
+    store_strip(mine_re_ref, peer_re_ref, mode, r, *parts_re, core)
+    store_strip(mine_im_ref, peer_im_ref, mode, r, *parts_im, core)
 
 
 def cells():
@@ -185,7 +251,7 @@
 def main_kernel(
     offset_ref, count_ref, own_re, own_im, right_re, right_im, lower_re, lower_im, probe_ref, measured_ref,
     table_ref, order_ref, mine_re_ref, mine_im_ref, peer_re_ref, peer_im_ref, stays_ref, moves_ref,
-    window_ref, far_ref,
+    window_ref, far_ref, a_high, a_low, b_high, b_low, mid_ref, near_ref, sum_ref, obj_ref,
 ):
     row_offset = offset_ref[0]
     col_offset = offset_ref[1]
@@ -199,36 +265,18 @@
         mixed = jnp.where(in_row, jnp.where(in_col, own_ref[...], right_ref[...]), lower_ref[...])
         mixed = pltpu.roll(mixed, lax.rem(full - row_offset, full), 0)
         window_ref[part] = reorder(pltpu.roll(mixed, lax.rem(full - col_offset, full), 1), order_ref[0])
-    sum_even = -measured_ref[:half]
-    sum_odd = -measured_ref[half:]
-    for mode in range(modes):
-        win_re, win_im = window_ref[0], window_ref[1]
-        probe_re = probe_ref[0, mode].astype(f32)
-        probe_im = probe_ref[1, mode].astype(f32)
-        even, odd = forward(
-            probe_re * win_re - probe_im * win_im, probe_re * win_im + probe_im * win_re, table_ref
-        )
-        far_ref[mode, 0] = even
-        far_ref[mode, 1] = odd
-        sum_even = sum_even + (even[:half] * even[:half] + even[half:] * even[half:])
-        sum_odd = sum_odd + (odd[:half] * odd[:half] + odd[half:] * odd[half:])
-    sum_even = sum_even * live
-    sum_odd = sum_odd * live
-    res_even = jnp.concatenate([sum_even, sum_even], axis=0)
-    res_odd = jnp.concatenate([sum_odd, sum_odd], axis=0)
-    obj_re = jnp.zeros((full, full), f32)
-    obj_im = jnp.zeros((full, full), f32)
-    for mode in range(modes):
-        win_re, win_im = window_ref[0], window_ref[1]
-        probe_re = probe_ref[0, mode].astype(f32)
-        probe_im = probe_ref[1, mode].astype(f32)
-        near_re, near_im = backward(far_ref[mode, 0] * res_even, far_ref[mode, 1] * res_odd, table_ref)
-        store_strips(mine_re_ref, peer_re_ref, mode, win_re * near_re + win_im * near_im, core)
-        store_strips(mine_im_ref, peer_im_ref, mode, win_re * near_im - win_im * near_re, core)
-        obj_re = obj_re + probe_re * near_re + probe_im * near_im
-        obj_im = obj_im + probe_re * near_im - probe_im * near_re
-    for part, total in enumerate((obj_re, obj_im)):
-        placed = reorder(total, order_ref[1])
+    sum_ref[0] = -measured_ref[:half]
+    sum_ref[1] = -measured_ref[half:]
+    refs = (
+        probe_ref, window_ref, table_ref, a_high, a_low, b_high, b_low, mid_ref, near_ref, far_ref, sum_ref, obj_ref,
+        mine_re_ref, mine_im_ref, peer_re_ref, peer_im_ref,
+    )
+    stages = [step_stages(mode, core, refs) for mode in range(modes)]
+    pipelined([ahead for ahead, back in stages])
+    sum_ref[...] = sum_ref[...] * live
+    pipelined([back for ahead, back in stages])
+    for part in range(2):
+        placed = reorder(obj_ref[part], order_ref[1])
         placed = pltpu.roll(pltpu.roll(placed, row_offset, 0), col_offset, 1)
         stays_ref[part] = jnp.where(in_col, placed, 0.0)
         moves_ref[part, :full] = jnp.where(in_col, 0.0, placed)
@@ -283,6 +331,12 @@
     return jax.ShapeDtypeStruct(shape, dtype)
 
 
+step_scratch = [pltpu.VMEM((4, full, full), bf16)] * 4 + [
+    pltpu.VMEM((4, full, full), f32),
+    pltpu.VMEM((4, full, full), f32),
+    pltpu.VMEM((2, half, full), f32),
+    pltpu.VMEM((2, full, full), f32),
+]
 vmem = pl.BlockSpec(memory_space=pltpu.VMEM)
 smem = pl.BlockSpec(memory_space=pltpu.SMEM)
 
@@ -306,7 +360,8 @@
     tables, orders = halves_tables()
     above_offset = passed_along(offsets, rows, 1).reshape(2)
     own = (object_field[0], object_field[1])
-    above_offset, *own = lax.optimization_barrier((above_offset, *own))
+    above_offset, own_im = lax.optimization_barrier((above_offset, own[1]))
+    own = (own[0], own_im)
     right = [passed_along(part, cols, -1) for part in own]
     lower = []
     for part, beside in zip(own, right):
@@ -341,7 +396,7 @@
         "step",
         [smem, smem] + [vmem] * 10,
         [shaped(*block_shape)] * 4 + [shaped(2, full, full), shaped(2, full + 8, full)],
-        scratch=[pltpu.VMEM((2, full, full), f32), pltpu.VMEM((modes, 2, full, full), f32)],
+        scratch=[pltpu.VMEM((2, full, full), f32), pltpu.VMEM((modes, 2, full, full), f32), *step_scratch],
         flops=5_000_000_000,
         moved=12_000_000,
         limit=24,

time: 110 us -> 107 us (0.973)
  waiting for transfers between devices: 27.6 us -> 25.8 us
  Pallas kernels: 14.7 us -> 13.2 us
    all_to_all x1, waiting for transfers between devices: 8.7 us -> 6.36 us  [local(): parts = lax.all_to_all(packed, 'y', 0, 0, tiled=True)]
    pallas_call x1, Pallas kernels: 9.5 us -> 8 us  [local(): call(main_kernel, 'step', [smem, smem] + [vmem] * 10, [shaped(*block_shap...]
    all_to_all x1, starting transfers between devices: 13.7 us -> 12.2 us  [local(): parts = lax.all_to_all(packed, 'y', 0, 0, tiled=True)]
  transfers between devices with their start and end apart: 15 -> 15, of which waited for: 10 -> 9; matrix products, arithmetic and copies ran while one was open for 3% -> 3% of each run, Pallas kernels for 5% -> 5%
where the time goes in v2:
time: 107 us; the launch traced here: 106 us
  starting transfers between devices  59.6 us (56%)
  waiting for transfers between devices  25.8 us (24%)
  Pallas kernels  13.2 us (12%)
  local copies, waits for them, and re-layouts  5.11 us (5%)
  between operations  1.57 us (1%)
    ppermute x7, starting transfers between devices, passed_along(): return lax.ppermute(x, axis, pairs)  21.8 us
    all_to_all x1, starting transfers between devices, local(): parts = lax.all_to_all(packed, 'y', 0, 0, tiled=True)  12.2 us
    pallas_call x1, Pallas kernels, local(): call(main_kernel, 'step', [smem, smem] + [vmem] * 10, [shaped(*block_shap...  8 us
    all_to_all x1, starting transfers between devices, local(): parts = lax.all_to_all(packed, ('z_lo', 'z_hi'), 0, 0, tiled=True)  7.07 us
    ppermute x2, starting transfers between devices, local(): lax.ppermute(peer, 'core', [(0, 1), (1, 0)])  6.97 us
    all_to_all x1, waiting for transfers between devices, local(): parts = lax.all_to_all(packed, ('z_lo', 'z_hi'), 0, 0, tiled=True)  6.86 us
    all_to_all x1, waiting for transfers between devices, local(): parts = lax.all_to_all(packed, 'y', 0, 0, tiled=True)  6.36 us
    ppermute x2, waiting for transfers between devices, local(): lax.ppermute(keep[1] + got[1], ('x', 'core'), far_pairs)  5.85 us
  transfers between devices with their start and end apart: 15, of which 9 were waited for; matrix products, arithmetic and copies ran while one was open for 3% of the time, Pallas kernels for 5%

profile of v2, /device:TPU:6, one launch (start us, length us, event | category | flops | bytes accessed | tf_op | source)
XLA Modules:
  0.0 106.3 jit_solution(17243537254078595347)
XLA Ops:
  0.6 0.0 copy-start
  0.6 0.0 copy-start.2
  0.7 4.3 %collective-permute-start = (s32[1,1,1,2]{3,2,1,0:T(1,128)}, s32[1,1,1,2]{3,2,1,0:T(1,128)S(1)}, u32[]{:S(2)}, u32[]{:S(2)}) collective-permute-start(s32[1,1,1,2]{3,2,1,0:T(1,128)} %param.9), channel_id=1, source_target_pairs={{0,32},{32,64},{64,96},{96,128},{128,160},{160,192},{192,224},{224... | collective-permute-start | bytes 32 | tf_op jit(solution)/shard_map/ppermute | solution.py:25
  5.0 1.1 %slice_bitcast_fusion = (f32[256,256]{1,0:T(8,128)S(1)}, f32[256,256]{1,0:T(8,128)S(1)}) fusion(f32[2,256,256]{2,1,0:T(8,128)} %param.7), kind=kLoop, calls=%fused_computation.1 | loop fusion | bytes 1048576 | tf_op jit(solution)/shard_map/squeeze | solution.py:362
  6.1 1.3 %collective-permute-start.1 = (f32[256,256]{1,0:T(8,128)S(1)}, f32[256,256]{1,0:T(8,128)S(1)}, u32[]{:S(2)}, u32[]{:S(2)}) collective-permute-start(f32[256,256]{1,0:T(8,128)S(1)} %get-tuple-element.43.own_ref.own_re), channel_id=1, source_target_pairs={{1,0},{2,1},{3,2},{4,3},{5,4},{6,5},{7,6},{8,7},{9,8},{10,9},{11,1... | collective-permute-start | bytes 786440 | tf_op jit(solution)/shard_map/ppermute | solution.py:25
  7.4 0.0 collective-permute-done
  7.4 1.3 %collective-permute-start.2 = (f32[256,256]{1,0:T(8,128)S(1)}, f32[256,256]{1,0:T(8,128)S(1)}, u32[]{:S(2)}, u32[]{:S(2)}) collective-permute-start(f32[256,256]{1,0:T(8,128)S(1)} %get-tuple-element.21.own_ref.own_im), channel_id=1, source_target_pairs={{1,0},{2,1},{3,2},{4,3},{5,4},{6,5},{7,6},{8,7},{9,8},{10,9},{11,1... | collective-permute-start | bytes 786440 | tf_op jit(solution)/shard_map/ppermute | solution.py:25
  8.7 0.8 collective-permute-done.1.right_ref.right_re
  9.5 0.6 mix.2
  10.1 1.9 %collective-permute-start.3 = (f32[256,256]{1,0:T(8,128)S(1)}, f32[256,256]{1,0:T(8,128)S(1)}, u32[]{:S(2)}, u32[]{:S(2)}) collective-permute-start(f32[256,256]{1,0:T(8,128)S(1)} %mix.2), channel_id=1, source_target_pairs={{32,0},{64,32},{96,64},{128,96},{160,128},{192,160},{224,192},{256... | collective-permute-start | bytes 786440 | tf_op jit(solution)/shard_map/ppermute | solution.py:25
  12.0 0.0 collective-permute-done.2.right_ref.right_im
  12.0 0.6 mix.3
  12.6 4.7 %collective-permute-start.4 = (f32[256,256]{1,0:T(8,128)S(1)}, f32[256,256]{1,0:T(8,128)S(1)}, u32[]{:S(2)}, u32[]{:S(2)}) collective-permute-start(f32[256,256]{1,0:T(8,128)S(1)} %mix.3), channel_id=1, source_target_pairs={{32,0},{64,32},{96,64},{128,96},{160,128},{192,160},{224,192},{256... | collective-permute-start | bytes 786440 | tf_op jit(solution)/shard_map/ppermute | solution.py:25
  17.9 0.0 copy-done
  17.9 0.0 copy-done.2
  18.0 0.0 copy-start.1
  18.0 1.4 %copy-done.1 = bf16[2,6,256,256]{3,2,1,0:T(8,128)(2,1)S(1)} copy-done((bf16[2,6,256,256]{3,2,1,0:T(8,128)(2,1)S(1)}, bf16[2,6,256,256]{3,2,1,0:T(8,128)(2,1)}, u32[]{:S(2)}) %copy-start.1) | copy-done | bytes 1572888
  19.4 0.0 copy-start.3
  19.4 0.9 copy-done.3
  20.3 0.0 copy-start.4
  20.3 1.4 %prepare.1 = (bf16[2,6,256,256]{3,2,1,0:T(8,128)(2,1)S(1)}, f32[256,256]{1,0:T(8,128)S(1)}, bf16[8,2,256,256]{3,2,1,0:T(8,128)(2,1)S(1)}, bf16[2,256,256]{2,1,0:T(8,128)(2,1)S(1)}) custom-call(bf16[2,6,256,256]{3,2,1,0:T(8,128)(2,1)S(1)} %copy-done.1, bf16[256,256]{1,0:T(8,128)(2,1)S(1)} %bitcast.15, bf16[8,2,256,256]{3,2,1,0:T(8,128)(2,1)S(1)} %copy-done, ...), custom_call_target="tpu_custom_call" | custom-call | flops 500000000 | bytes 8000000 | tf_op jit(solution)/shard_map/prepare/pallas_call | solution.py:374
  21.7 0.0 collective-permute-done.3.lower_re
  21.7 3.8 %collective-permute-done.4.lower_im = f32[256,256]{1,0:T(8,128)S(1)} collective-permute-done((f32[256,256]{1,0:T(8,128)S(1)}, f32[256,256]{1,0:T(8,128)S(1)}, u32[]{:S(2)}, u32[]{:S(2)}) %collective-permute-start.4) | collective-permute-done | bytes 262176 | tf_op jit(solution)/shard_map/ppermute | solution.py:25
  25.6 0.0 copy-done.4
  25.6 8.0 %step.1 = (f32[4,4,6,16,128]{4,3,2,1,0:T(8,128)S(1)}, f32[4,4,6,16,128]{4,3,2,1,0:T(8,128)S(1)}, f32[4,4,6,16,128]{4,3,2,1,0:T(8,128)S(1)}, f32[4,4,6,16,128]{4,...) custom-call(s32[2]{0:T(128)S(1)} %bitcast.18, s32[1]{0:T(128)} %bitcast.14.count_ref, ...), custom_call_target="tpu_custom_call" | custom-call | flops 5000000000 | bytes 12000000 | tf_op jit(solution)/shard_map/step/pallas_call | solution.py:394
  33.6 5.0 %collective-permute-start.8 = (f32[4,4,6,16,128]{4,3,2,1,0:T(8,128)S(1)}, f32[4,4,6,16,128]{4,3,2,1,0:T(8,128)S(1)}, u32[]{:S(2)}, u32[]{:S(2)}) collective-permute-start(f32[4,4,6,16,128]{4,3,2,1,0:T(8,128)S(1)} %get-tuple-element.33), channel_id=1, source_target_pairs={{0,1},{1,0},{2,3},{3,2},{4,5},{5,4},{6,7},{7,6},{8,9},{9,8},{10,11... | collective-permute-start | bytes 2359304 | tf_op jit(solution)/shard_map/ppermute | solution.py:409
  38.6 1.9 %collective-permute-start.5 = (f32[4,4,6,16,128]{4,3,2,1,0:T(8,128)S(1)}, f32[4,4,6,16,128]{4,3,2,1,0:T(8,128)S(1)}, u32[]{:S(2)}, u32[]{:S(2)}) collective-permute-start(f32[4,4,6,16,128]{4,3,2,1,0:T(8,128)S(1)} %get-tuple-element.29), channel_id=1, source_target_pairs={{0,1},{1,0},{2,3},{3,2},{4,5},{5,4},{6,7},{7,6},{8,9},{9,8},{10,11... | collective-permute-start | bytes 2359304 | tf_op jit(solution)/shard_map/ppermute | solution.py:409
  40.5 0.0 collective-permute-done.8.theirs_ref
  40.6 0.1 add_cores.3
  40.7 1.9 %collective-permute-start.9 = (f32[2,4,6,16,128]{4,3,2,1,0:T(8,128)S(1)}, f32[2,4,6,16,128]{4,3,2,1,0:T(8,128)S(1)}, u32[]{:S(2)}, u32[]{:S(2)}) collective-permute-start(f32[2,4,6,16,128]{4,3,2,1,0:T(8,128)S(1)} %get-tuple-element.35), channel_id=1, source_target_pairs={{0,32},{1,97},{32,0},{33,65},{64,96},{65,33},{96,64},{97,1},{2,34}... | collective-permute-start | bytes 1179656 | tf_op jit(solution)/shard_map/ppermute | solution.py:414
  42.6 0.2 collective-permute-done.5.theirs_ref
  42.8 0.1 add_cores.2
  42.9 3.7 %collective-permute-start.6 = (f32[2,4,6,16,128]{4,3,2,1,0:T(8,128)S(1)}, f32[2,4,6,16,128]{4,3,2,1,0:T(8,128)S(1)}, u32[]{:S(2)}, u32[]{:S(2)}) collective-permute-start(f32[2,4,6,16,128]{4,3,2,1,0:T(8,128)S(1)} %get-tuple-element.31), channel_id=1, source_target_pairs={{0,32},{1,97},{32,0},{33,65},{64,96},{65,33},{96,64},{97,1},{2,34}... | collective-permute-start | bytes 1179656 | tf_op jit(solution)/shard_map/ppermute | solution.py:414
  46.6 3.1 %collective-permute-start.11 = (f32[2,264,256]{2,1,0:T(8,128)S(1)}, f32[2,264,256]{2,1,0:T(8,128)S(1)}, u32[]{:S(2)}, u32[]{:S(2)}) collective-permute-start(f32[2,264,256]{2,1,0:T(8,128)S(1)} %get-tuple-element.37), channel_id=1, source_target_pairs={{0,1},{1,2},{2,3},{3,4},{4,5},{5,6},{6,7},{7,8},{8,9},{9,10},{10,1... | collective-permute-start | bytes 1622024 | tf_op jit(solution)/shard_map/ppermute | solution.py:25
  49.7 0.6 collective-permute-done.9.got_im
  50.4 2.9 %collective-permute-start.10 = (f32[4,6,16,128]{3,2,1,0:T(8,128)S(1)}, f32[4,6,16,128]{3,2,1,0:T(8,128)S(1)}, u32[]{:S(2)}, u32[]{:S(2)}) collective-permute-start(f32[4,6,16,128]{3,2,1,0:T(8,128)S(1)} %fusion), channel_id=1, source_target_pairs={{0,96},{1,33},{32,64},{33,1},{64,32},{65,97},{96,0},{97,65},{2,98}... | collective-permute-start | bytes 589832 | tf_op jit(solution)/shard_map/ppermute | solution.py:418
  53.3 1.3 %collective-permute-done.6.got_re = f32[2,4,6,16,128]{4,3,2,1,0:T(8,128)S(1)} collective-permute-done((f32[2,4,6,16,128]{4,3,2,1,0:T(8,128)S(1)}, f32[2,4,6,16,128]{4,3,2,1,0:T(8,128)S(1)}, u32[]{:S(2)}, u32[]{:S(2)}) %collective-permute-start.6) | collective-permute-done | bytes 393248 | tf_op jit(solution)/shard_map/ppermute | solution.py:414
  54.6 2.9 %collective-permute-start.7 = (f32[4,6,16,128]{3,2,1,0:T(8,128)S(1)}, f32[4,6,16,128]{3,2,1,0:T(8,128)S(1)}, u32[]{:S(2)}, u32[]{:S(2)}) collective-permute-start(f32[4,6,16,128]{3,2,1,0:T(8,128)S(1)} %fusion.1), channel_id=1, source_target_pairs={{0,96},{1,33},{32,64},{33,1},{64,32},{65,97},{96,0},{97,65},{2,98}... | collective-permute-start | bytes 589832 | tf_op jit(solution)/shard_map/ppermute | solution.py:418
  57.5 1.6 %collective-permute-done.10.came_im = f32[4,6,16,128]{3,2,1,0:T(8,128)S(1)} collective-permute-done((f32[4,6,16,128]{3,2,1,0:T(8,128)S(1)}, f32[4,6,16,128]{3,2,1,0:T(8,128)S(1)}, u32[]{:S(2)}, u32[]{:S(2)}) %collective-permute-start.10) | collective-permute-done | bytes 196640 | tf_op jit(solution)/shard_map/ppermute | solution.py:418
  59.1 4.2 %collective-permute-done.7.came_re = f32[4,6,16,128]{3,2,1,0:T(8,128)S(1)} collective-permute-done((f32[4,6,16,128]{3,2,1,0:T(8,128)S(1)}, f32[4,6,16,128]{3,2,1,0:T(8,128)S(1)}, u32[]{:S(2)}, u32[]{:S(2)}) %collective-permute-start.7) | collective-permute-done | bytes 196640 | tf_op jit(solution)/shard_map/ppermute | solution.py:418
  63.3 1.1 %add_columns.1 = f32[8,16,768]{2,1,0:T(8,128)} custom-call(f32[2,4,6,16,128]{4,3,2,1,0:T(8,128)S(1)} %get-tuple-element.30.kept_re, f32[2,4,6,16,128]{4,3,2,1,0:T(8,128)S(1)} %collective-permute-done.6.got_re, f32[4,6,16,128]{3,2,1,0:T(8,128)S(1)} %collective-permute-done.7.came_re, f32[2,4,6,16,128]{4,3,2,1,0:T(8,128)S(1)} %get-tuple-element.34.kept_im, ...), custom_call_target="tpu_custom_call" | custom-call | bytes 2000000 | tf_op jit(solution)/shard_map/add_columns/pallas_call | solution.py:419
  64.4 0.0 copy-start.5
  64.4 12.2 %all-to-all-start = ((f32[8,16,768]{2,1,0:T(8,128)}), f32[8,16,768]{2,1,0:T(8,128)S(1)}, u32[]{:S(2)}, u32[]{:S(2)}) async-start(f32[8,16,768]{2,1,0:T(8,128)} %add_columns.1), calls=%async_computation | async-start | bytes 786432 | tf_op jit(solution)/shard_map/all_to_all | solution.py:425
  76.7 0.0 collective-permute-done.11.moved_ref
  76.7 0.7 down.1
  77.4 5.2 %collective-permute-start.12 = (f32[2,256,256]{2,1,0:T(8,128)S(1)}, f32[2,256,256]{2,1,0:T(8,128)S(1)}, u32[]{:S(2)}, u32[]{:S(2)}) collective-permute-start(f32[2,256,256]{2,1,0:T(8,128)S(1)} %get-tuple-element.39), channel_id=1, source_target_pairs={{0,32},{32,64},{64,96},{96,128},{128,160},{160,192},{192,224},{224... | collective-permute-start | bytes 1572872 | tf_op jit(solution)/shard_map/ppermute | solution.py:25
  82.6 0.9 constant_dynamic-slice_fusion
  83.5 0.1 copy.12
  83.6 6.4 %all-to-all-done.parts_ref = f32[8,16,768]{2,1,0:T(8,128)S(1)} async-done(((f32[8,16,768]{2,1,0:T(8,128)}), f32[8,16,768]{2,1,0:T(8,128)S(1)}, u32[]{:S(2)}, u32[]{:S(2)}) %all-to-all-start) | async-done | bytes 393248 | tf_op jit(solution)/shard_map/all_to_all | solution.py:425
  90.0 0.7 add_depth.1
  90.7 7.1 %all-to-all-start.1 = ((f32[8,8,192]{2,1,0:T(8,128)}), f32[8,8,192]{2,1,0:T(8,128)S(1)}, u32[]{:S(2)}, u32[]{:S(2)}) async-start(f32[8,8,192]{2,1,0:T(8,128)} %add_depth.1), calls=%async_computation.1 | async-start | bytes 131072 | tf_op jit(solution)/shard_map/all_to_all | solution.py:427
  97.8 0.0 collective-permute-done.12
  97.8 0.0 copy-done.5
  97.8 0.9 multiply_subtract_fusion
  98.7 6.9 %all-to-all-done.1 = f32[8,8,192]{2,1,0:T(8,128)S(1)} async-done(((f32[8,8,192]{2,1,0:T(8,128)}), f32[8,8,192]{2,1,0:T(8,128)S(1)}, u32[]{:S(2)}, u32[]{:S(2)}) %all-to-all-start.1) | async-done | bytes 49184 | tf_op jit(solution)/shard_map/all_to_all | solution.py:427
  105.6 0.1 mul.42
  105.7 0.6 copy.11
  (5 shorter events, 0.1 us)
Async XLA Ops:
  0.6 17.3 %copy-start = (bf16[8,2,256,256]{3,2,1,0:T(8,128)(2,1)S(1)}, bf16[8,2,256,256]{3,2,1,0:T(8,128)(2,1)}, u32[]{:S(2)}) copy-start(bf16[8,2,256,256]{3,2,1,0:T(8,128)(2,1)} %constant.43.clone.table_in) | copy-start | bytes 6291460
  0.6 17.3 %copy-start.2 = (bf16[4,256,256]{2,1,0:T(8,128)(2,1)S(1)}, bf16[4,256,256]{2,1,0:T(8,128)(2,1)}, u32[]{:S(2)}) copy-start(bf16[4,256,256]{2,1,0:T(8,128)(2,1)} %constant.44.clone.order_in) | copy-start | bytes 1572868
  0.7 6.7 %collective-permute-start = (s32[1,1,1,2]{3,2,1,0:T(1,128)}, s32[1,1,1,2]{3,2,1,0:T(1,128)S(1)}, u32[]{:S(2)}, u32[]{:S(2)}) collective-permute-start(s32[1,1,1,2]{3,2,1,0:T(1,128)} %param.9), channel_id=1, source_target_pairs={{0,32},{32,64},{64,96},{96,128},{128,160},{160,192},{192,224},{224... | collective-permute-start | bytes 32 | tf_op jit(solution)/shard_map/ppermute | solution.py:25
  6.1 3.4 %collective-permute-start.1 = (f32[256,256]{1,0:T(8,128)S(1)}, f32[256,256]{1,0:T(8,128)S(1)}, u32[]{:S(2)}, u32[]{:S(2)}) collective-permute-start(f32[256,256]{1,0:T(8,128)S(1)} %get-tuple-element.43.own_ref.own_re), channel_id=1, source_target_pairs={{1,0},{2,1},{3,2},{4,3},{5,4},{6,5},{7,6},{8,7},{9,8},{10,9},{11,1... | collective-permute-start | bytes 786440 | tf_op jit(solution)/shard_map/ppermute | solution.py:25
  7.4 4.6 %collective-permute-start.2 = (f32[256,256]{1,0:T(8,128)S(1)}, f32[256,256]{1,0:T(8,128)S(1)}, u32[]{:S(2)}, u32[]{:S(2)}) collective-permute-start(f32[256,256]{1,0:T(8,128)S(1)} %get-tuple-element.21.own_ref.own_im), channel_id=1, source_target_pairs={{1,0},{2,1},{3,2},{4,3},{5,4},{6,5},{7,6},{8,7},{9,8},{10,9},{11,1... | collective-permute-start | bytes 786440 | tf_op jit(solution)/shard_map/ppermute | solution.py:25
  10.1 11.6 %collective-permute-start.3 = (f32[256,256]{1,0:T(8,128)S(1)}, f32[256,256]{1,0:T(8,128)S(1)}, u32[]{:S(2)}, u32[]{:S(2)}) collective-permute-start(f32[256,256]{1,0:T(8,128)S(1)} %mix.2), channel_id=1, source_target_pairs={{32,0},{64,32},{96,64},{128,96},{160,128},{192,160},{224,192},{256... | collective-permute-start | bytes 786440 | tf_op jit(solution)/shard_map/ppermute | solution.py:25
  12.6 13.0 %collective-permute-start.4 = (f32[256,256]{1,0:T(8,128)S(1)}, f32[256,256]{1,0:T(8,128)S(1)}, u32[]{:S(2)}, u32[]{:S(2)}) collective-permute-start(f32[256,256]{1,0:T(8,128)S(1)} %mix.3), channel_id=1, source_target_pairs={{32,0},{64,32},{96,64},{128,96},{160,128},{192,160},{224,192},{256... | collective-permute-start | bytes 786440 | tf_op jit(solution)/shard_map/ppermute | solution.py:25
  18.0 1.4 %copy-start.1 = (bf16[2,6,256,256]{3,2,1,0:T(8,128)(2,1)S(1)}, bf16[2,6,256,256]{3,2,1,0:T(8,128)(2,1)}, u32[]{:S(2)}) copy-start(bf16[2,6,256,256]{3,2,1,0:T(8,128)(2,1)} %probe_in.1) | copy-start | bytes 4718596
  19.4 0.9 copy-start.3
  20.3 5.3 %copy-start.4 = (s32[1,1,1,2]{3,2,1,0:T(1,128)S(1)}, s32[1,1,1,2]{3,2,1,0:T(1,128)}, u32[]{:S(2)}) copy-start(s32[1,1,1,2]{3,2,1,0:T(1,128)} %param.9) | copy-start | bytes 28
  33.6 7.0 %collective-permute-start.8 = (f32[4,4,6,16,128]{4,3,2,1,0:T(8,128)S(1)}, f32[4,4,6,16,128]{4,3,2,1,0:T(8,128)S(1)}, u32[]{:S(2)}, u32[]{:S(2)}) collective-permute-start(f32[4,4,6,16,128]{4,3,2,1,0:T(8,128)S(1)} %get-tuple-element.33), channel_id=1, source_target_pairs={{0,1},{1,0},{2,3},{3,2},{4,5},{5,4},{6,7},{7,6},{8,9},{9,8},{10,11... | collective-permute-start | bytes 2359304 | tf_op jit(solution)/shard_map/ppermute | solution.py:409
  38.6 4.2 %collective-permute-start.5 = (f32[4,4,6,16,128]{4,3,2,1,0:T(8,128)S(1)}, f32[4,4,6,16,128]{4,3,2,1,0:T(8,128)S(1)}, u32[]{:S(2)}, u32[]{:S(2)}) collective-permute-start(f32[4,4,6,16,128]{4,3,2,1,0:T(8,128)S(1)} %get-tuple-element.29), channel_id=1, source_target_pairs={{0,1},{1,0},{2,3},{3,2},{4,5},{5,4},{6,7},{7,6},{8,9},{9,8},{10,11... | collective-permute-start | bytes 2359304 | tf_op jit(solution)/shard_map/ppermute | solution.py:409
  40.7 9.7 %collective-permute-start.9 = (f32[2,4,6,16,128]{4,3,2,1,0:T(8,128)S(1)}, f32[2,4,6,16,128]{4,3,2,1,0:T(8,128)S(1)}, u32[]{:S(2)}, u32[]{:S(2)}) collective-permute-start(f32[2,4,6,16,128]{4,3,2,1,0:T(8,128)S(1)} %get-tuple-element.35), channel_id=1, source_target_pairs={{0,32},{1,97},{32,0},{33,65},{64,96},{65,33},{96,64},{97,1},{2,34}... | collective-permute-start | bytes 1179656 | tf_op jit(solution)/shard_map/ppermute | solution.py:414
  42.9 11.7 %collective-permute-start.6 = (f32[2,4,6,16,128]{4,3,2,1,0:T(8,128)S(1)}, f32[2,4,6,16,128]{4,3,2,1,0:T(8,128)S(1)}, u32[]{:S(2)}, u32[]{:S(2)}) collective-permute-start(f32[2,4,6,16,128]{4,3,2,1,0:T(8,128)S(1)} %get-tuple-element.31), channel_id=1, source_target_pairs={{0,32},{1,97},{32,0},{33,65},{64,96},{65,33},{96,64},{97,1},{2,34}... | collective-permute-start | bytes 1179656 | tf_op jit(solution)/shard_map/ppermute | solution.py:414
  46.6 30.0 %collective-permute-start.11 = (f32[2,264,256]{2,1,0:T(8,128)S(1)}, f32[2,264,256]{2,1,0:T(8,128)S(1)}, u32[]{:S(2)}, u32[]{:S(2)}) collective-permute-start(f32[2,264,256]{2,1,0:T(8,128)S(1)} %get-tuple-element.37), channel_id=1, source_target_pairs={{0,1},{1,2},{2,3},{3,4},{4,5},{5,6},{6,7},{7,8},{8,9},{9,10},{10,1... | collective-permute-start | bytes 1622024 | tf_op jit(solution)/shard_map/ppermute | solution.py:25
  50.4 8.8 %collective-permute-start.10 = (f32[4,6,16,128]{3,2,1,0:T(8,128)S(1)}, f32[4,6,16,128]{3,2,1,0:T(8,128)S(1)}, u32[]{:S(2)}, u32[]{:S(2)}) collective-permute-start(f32[4,6,16,128]{3,2,1,0:T(8,128)S(1)} %fusion), channel_id=1, source_target_pairs={{0,96},{1,33},{32,64},{33,1},{64,32},{65,97},{96,0},{97,65},{2,98}... | collective-permute-start | bytes 589832 | tf_op jit(solution)/shard_map/ppermute | solution.py:418
  54.6 8.8 %collective-permute-start.7 = (f32[4,6,16,128]{3,2,1,0:T(8,128)S(1)}, f32[4,6,16,128]{3,2,1,0:T(8,128)S(1)}, u32[]{:S(2)}, u32[]{:S(2)}) collective-permute-start(f32[4,6,16,128]{3,2,1,0:T(8,128)S(1)} %fusion.1), channel_id=1, source_target_pairs={{0,96},{1,33},{32,64},{33,1},{64,32},{65,97},{96,0},{97,65},{2,98}... | collective-permute-start | bytes 589832 | tf_op jit(solution)/shard_map/ppermute | solution.py:418
  64.4 33.4 %copy-start.5 = (f32[2,256,256]{2,1,0:T(8,128)S(1)}, f32[2,256,256]{2,1,0:T(8,128)}, u32[]{:S(2)}) copy-start(f32[2,256,256]{2,1,0:T(8,128)} %param.7) | copy-start | bytes 1572868
  64.4 25.6 %all-to-all-start = ((f32[8,16,768]{2,1,0:T(8,128)}), f32[8,16,768]{2,1,0:T(8,128)S(1)}, u32[]{:S(2)}, u32[]{:S(2)}) async-start(f32[8,16,768]{2,1,0:T(8,128)} %add_columns.1), calls=%async_computation | async-start | bytes 786432 | tf_op jit(solution)/shard_map/all_to_all | solution.py:425
  77.4 20.4 %collective-permute-start.12 = (f32[2,256,256]{2,1,0:T(8,128)S(1)}, f32[2,256,256]{2,1,0:T(8,128)S(1)}, u32[]{:S(2)}, u32[]{:S(2)}) collective-permute-start(f32[2,256,256]{2,1,0:T(8,128)S(1)} %get-tuple-element.39), channel_id=1, source_target_pairs={{0,32},{32,64},{64,96},{96,128},{128,160},{160,192},{192,224},{224... | collective-permute-start | bytes 1572872 | tf_op jit(solution)/shard_map/ppermute | solution.py:25
  90.7 14.8 %all-to-all-start.1 = ((f32[8,8,192]{2,1,0:T(8,128)}), f32[8,8,192]{2,1,0:T(8,128)S(1)}, u32[]{:S(2)}, u32[]{:S(2)}) async-start(f32[8,8,192]{2,1,0:T(8,128)} %add_depth.1), calls=%async_computation.1 | async-start | bytes 131072 | tf_op jit(solution)/shard_map/all_to_all | solution.py:427

commit v3 on v2

--- a/solution.py
+++ b/solution.py
@@ -249,7 +249,7 @@
 
 
 def main_kernel(
-    offset_ref, count_ref, own_re, own_im, right_re, right_im, lower_re, lower_im, probe_ref, measured_ref,
+    offset_ref, count_ref, own_ref, right_ref, lower_ref, probe_ref, measured_ref,
     table_ref, order_ref, mine_re_ref, mine_im_ref, peer_re_ref, peer_im_ref, stays_ref, moves_ref,
     window_ref, far_ref, a_high, a_low, b_high, b_low, mid_ref, near_ref, sum_ref, obj_ref,
 ):
@@ -260,9 +260,8 @@
     rows, cols = cells()
     in_row = rows >= row_offset
     in_col = cols >= col_offset
-    parts = ((own_re, right_re, lower_re), (own_im, right_im, lower_im))
-    for part, (own_ref, right_ref, lower_ref) in enumerate(parts):
-        mixed = jnp.where(in_row, jnp.where(in_col, own_ref[...], right_ref[...]), lower_ref[...])
+    for part in range(2):
+        mixed = jnp.where(in_row, jnp.where(in_col, own_ref[part], right_ref[part]), lower_ref[part])
         mixed = pltpu.roll(mixed, lax.rem(full - row_offset, full), 0)
         window_ref[part] = reorder(pltpu.roll(mixed, lax.rem(full - col_offset, full), 1), order_ref[0])
     sum_ref[0] = -measured_ref[:half]
@@ -283,9 +282,17 @@
         moves_ref[part, full:] = jnp.zeros((8, full), f32) + row_offset.astype(f32)
 
 
+def hold_kernel(tile_in, tile_out, sem):
+    copy = pltpu.make_async_copy(tile_in, tile_out, sem)
+    copy.start()
+    copy.wait()
+
+
 def mix_kernel(offset_ref, own_ref, right_ref, out_ref):
     rows, cols = cells()
-    out_ref[...] = jnp.where(cols >= offset_ref[1], own_ref[...], right_ref[...])
+    in_col = cols >= offset_ref[1]
+    for part in range(2):
+        out_ref[part] = jnp.where(in_col, own_ref[part], right_ref[part])
 
 
 def down_kernel(offset_ref, stays_ref, moved_ref, down_ref, held_ref):
@@ -341,7 +348,7 @@
 smem = pl.BlockSpec(memory_space=pltpu.SMEM)
 
 
-def call(kernel, name, inputs, outputs, scratch=(), flops=0, moved=0, limit=16):
+def call(kernel, name, inputs, outputs, scratch=(), flops=0, moved=0, limit=4):
     return pl.pallas_call(
         kernel,
         out_shape=tuple(outputs) if len(outputs) > 1 else outputs[0],
@@ -358,17 +365,17 @@
     rows = ("z_lo", "x")
     cols = ("z_hi", "y", "core")
     tables, orders = halves_tables()
+    right = passed_along(object_field, cols, -1)
     above_offset = passed_along(offsets, rows, 1).reshape(2)
-    own = (object_field[0], object_field[1])
-    above_offset, own_im = lax.optimization_barrier((above_offset, own[1]))
-    own = (own[0], own_im)
-    right = [passed_along(part, cols, -1) for part in own]
-    lower = []
-    for part, beside in zip(own, right):
-        mixed = call(mix_kernel, "mix", [smem, vmem, vmem], [shaped(full, full)], moved=1_000_000)(
-            above_offset, part, beside
-        )
-        lower.append(passed_along(mixed, rows, -1))
+    above_offset, tile = lax.optimization_barrier((above_offset, object_field))
+    own = call(
+        hold_kernel, "hold", [pl.BlockSpec(memory_space=pl.ANY)], [shaped(2, full, full)],
+        scratch=[pltpu.SemaphoreType.DMA], moved=1_000_000,
+    )(tile)
+    mixed = call(mix_kernel, "mix", [smem, vmem, vmem], [shaped(2, full, full)], moved=2_000_000)(
+        above_offset, own, right
+    )
+    lower = passed_along(mixed, rows, -1)
     start = (0, 0, lax.axis_index(rows) * strip, lax.axis_index(cols) * 8)
     own_probe = lax.dynamic_slice(probe_modes, start, (2, modes, strip, 8)).astype(f32)
     probe, measured, table, order = call(
@@ -389,18 +396,19 @@
         ],
         flops=500_000_000,
         moved=8_000_000,
+        limit=6,
     )(probe_modes, intensity[0, 0, 0], jnp.asarray(tables), jnp.asarray(orders))
     block_shape = (4, 4, modes, strip, half)
     mine_re, mine_im, peer_re, peer_im, stays, moves = call(
         main_kernel,
         "step",
-        [smem, smem] + [vmem] * 10,
+        [smem, smem] + [vmem] * 7,
         [shaped(*block_shape)] * 4 + [shaped(2, full, full), shaped(2, full + 8, full)],
         scratch=[pltpu.VMEM((2, full, full), f32), pltpu.VMEM((modes, 2, full, full), f32), *step_scratch],
         flops=5_000_000_000,
         moved=12_000_000,
-        limit=24,
-    )(offsets.reshape(2), counts.reshape(1), *own, *right, *lower, probe, measured, table, order)
+        limit=14,
+    )(offsets.reshape(2), counts.reshape(1), own, right, lower, probe, measured, table, order)
 
     near_pairs = [(2 * x + c, 2 * ((x ^ 1) if c == 0 else 3 - x) + c) for x in range(4) for c in range(2)]
     far_pairs = [(2 * x + c, 2 * (3 - x if c == 0 else (x ^ 1)) + c) for x in range(4) for c in range(2)]

time: 107 us -> 106 us (level)
  starting transfers between devices: 59.6 us -> 49.1 us
  waiting for transfers between devices: 25.8 us -> 35.6 us
    ppermute x7 -> x5, starting transfers between devices: 21.8 us -> 13.8 us  [passed_along(): return lax.ppermute(x, axis, pairs)]
    ppermute x7 -> x5, waiting for transfers between devices: 4.68 us -> 11.8 us  [passed_along(): return lax.ppermute(x, axis, pairs)]
    all_to_all x1, waiting for transfers between devices: 6.36 us -> 9.19 us  [local(): parts = lax.all_to_all(packed, 'y', 0, 0, tiled=True)]
    ppermute x2, starting transfers between devices: 6.97 us -> 5.16 us  [local(): lax.ppermute(peer, 'core', [(0, 1), (1, 0)])]
    unnamed x14 -> x16, local copies, waits for them, and re-layouts: 3.07 us -> 4.11 us
  transfers between devices with their start and end apart: 15 -> 13, of which waited for: 9 -> 9; matrix products, arithmetic and copies ran while one was open for 3% -> 2% of each run, Pallas kernels for 5% -> 4%
where the time goes in v3:
time: 106 us
  starting transfers between devices  49.1 us (46%)
  waiting for transfers between devices  35.6 us (34%)
  Pallas kernels  13.2 us (12%)
  local copies, waits for them, and re-layouts  5.08 us (5%)
  between operations  1.53 us (1%)
    ppermute x5, starting transfers between devices, passed_along(): return lax.ppermute(x, axis, pairs)  13.8 us
    all_to_all x1, starting transfers between devices, local(): parts = lax.all_to_all(packed, 'y', 0, 0, tiled=True)  11.9 us
    ppermute x5, waiting for transfers between devices, passed_along(): return lax.ppermute(x, axis, pairs)  11.8 us
    all_to_all x1, waiting for transfers between devices, local(): parts = lax.all_to_all(packed, 'y', 0, 0, tiled=True)  9.19 us
    pallas_call x1, Pallas kernels, local(): call(main_kernel, 'step', [smem, smem] + [vmem] * 7, [shaped(*block_shape...  8.49 us
    all_to_all x1, waiting for transfers between devices, local(): parts = lax.all_to_all(packed, ('z_lo', 'z_hi'), 0, 0, tiled=True)  6.86 us
    all_to_all x1, starting transfers between devices, local(): parts = lax.all_to_all(packed, ('z_lo', 'z_hi'), 0, 0, tiled=True)  6.6 us
    ppermute x2, starting transfers between devices, local(): lax.ppermute(keep[1] + got[1], ('x', 'core'), far_pairs)  5.99 us
  transfers between devices with their start and end apart: 13, of which 9 were waited for; matrix products, arithmetic and copies ran while one was open for 2% of the time, Pallas kernels for 4%

profile of v3, /device:TPU:6, one launch (start us, length us, event | category | flops | bytes accessed | tf_op | source)
XLA Modules:
  0.0 105.6 jit_solution(13041134085691729384)
XLA Ops:
  0.6 0.0 copy-start
  0.6 1.4 %collective-permute-start.1 = (f32[2,256,256]{2,1,0:T(8,128)}, f32[2,256,256]{2,1,0:T(8,128)S(1)}, u32[]{:S(2)}, u32[]{:S(2)}) collective-permute-start(f32[2,256,256]{2,1,0:T(8,128)} %tile_in), channel_id=1, source_target_pairs={{1,0},{2,1},{3,2},{4,3},{5,4},{6,5},{7,6},{8,7},{9,8},{10,9},{11,1... | collective-permute-start | bytes 1572872 | tf_op jit(solution)/shard_map/ppermute | solution.py:25
  2.1 4.2 %collective-permute-start = (s32[1,1,1,2]{3,2,1,0:T(1,128)}, s32[1,1,1,2]{3,2,1,0:T(1,128)S(1)}, u32[]{:S(2)}, u32[]{:S(2)}) collective-permute-start(s32[1,1,1,2]{3,2,1,0:T(1,128)} %param.9), channel_id=1, source_target_pairs={{0,32},{32,64},{64,96},{96,128},{128,160},{160,192},{192,224},{224... | collective-permute-start | bytes 32 | tf_op jit(solution)/shard_map/ppermute | solution.py:25
  6.3 1.4 %collective-permute-done = s32[1,1,1,2]{3,2,1,0:T(1,128)S(1)} collective-permute-done((s32[1,1,1,2]{3,2,1,0:T(1,128)}, s32[1,1,1,2]{3,2,1,0:T(1,128)S(1)}, u32[]{:S(2)}, u32[]{:S(2)}) %collective-permute-start) | collective-permute-done | bytes 40 | tf_op jit(solution)/shard_map/ppermute | solution.py:25
  7.7 0.0 copy-start.1
  7.7 1.0 copy-done.1
  8.7 0.0 copy-start.4
  8.8 0.0 collective-permute-done.1.right_ref
  8.8 0.6 mix.1
  9.4 2.7 %collective-permute-start.2 = (f32[2,256,256]{2,1,0:T(8,128)S(1)}, f32[2,256,256]{2,1,0:T(8,128)S(1)}, u32[]{:S(2)}, u32[]{:S(2)}) collective-permute-start(f32[2,256,256]{2,1,0:T(8,128)S(1)} %mix.1), channel_id=1, source_target_pairs={{32,0},{64,32},{96,64},{128,96},{160,128},{192,160},{224,192},{256... | collective-permute-start | bytes 1572872 | tf_op jit(solution)/shard_map/ppermute | solution.py:25
  12.7 0.0 copy-done
  12.8 0.0 copy-done.4
  12.8 0.0 copy-start.3
  12.8 1.4 %copy-done.3 = bf16[2,6,256,256]{3,2,1,0:T(8,128)(2,1)S(1)} copy-done((bf16[2,6,256,256]{3,2,1,0:T(8,128)(2,1)S(1)}, bf16[2,6,256,256]{3,2,1,0:T(8,128)(2,1)}, u32[]{:S(2)}) %copy-start.3) | copy-done | bytes 1572888
  14.2 0.0 copy-start.5
  14.2 0.9 copy-done.5
  15.1 0.0 copy-start.6
  15.1 1.4 %prepare.1 = (bf16[2,6,256,256]{3,2,1,0:T(8,128)(2,1)S(1)}, f32[256,256]{1,0:T(8,128)S(1)}, bf16[8,2,256,256]{3,2,1,0:T(8,128)(2,1)S(1)}, bf16[2,256,256]{2,1,0:T(8,128)(2,1)S(1)}) custom-call(bf16[2,6,256,256]{3,2,1,0:T(8,128)(2,1)S(1)} %copy-done.3, bf16[256,256]{1,0:T(8,128)(2,1)S(1)} %bitcast.11, bf16[8,2,256,256]{3,2,1,0:T(8,128)(2,1)S(1)} %copy-done, ...), custom_call_target="tpu_custom_call" | custom-call | flops 500000000 | bytes 8000000 | tf_op jit(solution)/shard_map/prepare/pallas_call | solution.py:381
  16.5 10.4 %collective-permute-done.2.lower_ref = f32[2,256,256]{2,1,0:T(8,128)S(1)} collective-permute-done((f32[2,256,256]{2,1,0:T(8,128)S(1)}, f32[2,256,256]{2,1,0:T(8,128)S(1)}, u32[]{:S(2)}, u32[]{:S(2)}) %collective-permute-start.2) | collective-permute-done | bytes 524320 | tf_op jit(solution)/shard_map/ppermute | solution.py:25
  26.9 0.0 copy-done.6
  26.9 8.5 %step.1 = (f32[4,4,6,16,128]{4,3,2,1,0:T(8,128)S(1)}, f32[4,4,6,16,128]{4,3,2,1,0:T(8,128)S(1)}, f32[4,4,6,16,128]{4,3,2,1,0:T(8,128)S(1)}, f32[4,4,6,16,128]{4,...) custom-call(s32[2]{0:T(128)S(1)} %bitcast.12, s32[1]{0:T(128)} %bitcast.10.count_ref, ...), custom_call_target="tpu_custom_call" | custom-call | flops 5000000000 | bytes 12000000 | tf_op jit(solution)/shard_map/step/pallas_call | solution.py:402
  35.4 3.2 %collective-permute-start.6 = (f32[4,4,6,16,128]{4,3,2,1,0:T(8,128)S(1)}, f32[4,4,6,16,128]{4,3,2,1,0:T(8,128)S(1)}, u32[]{:S(2)}, u32[]{:S(2)}) collective-permute-start(f32[4,4,6,16,128]{4,3,2,1,0:T(8,128)S(1)} %get-tuple-element.33), channel_id=1, source_target_pairs={{0,1},{1,0},{2,3},{3,2},{4,5},{5,4},{6,7},{7,6},{8,9},{9,8},{10,11... | collective-permute-start | bytes 2359304 | tf_op jit(solution)/shard_map/ppermute | solution.py:417
  38.7 1.9 %collective-permute-start.3 = (f32[4,4,6,16,128]{4,3,2,1,0:T(8,128)S(1)}, f32[4,4,6,16,128]{4,3,2,1,0:T(8,128)S(1)}, u32[]{:S(2)}, u32[]{:S(2)}) collective-permute-start(f32[4,4,6,16,128]{4,3,2,1,0:T(8,128)S(1)} %get-tuple-element.29), channel_id=1, source_target_pairs={{0,1},{1,0},{2,3},{3,2},{4,5},{5,4},{6,7},{7,6},{8,9},{9,8},{10,11... | collective-permute-start | bytes 2359304 | tf_op jit(solution)/shard_map/ppermute | solution.py:417
  40.6 0.0 collective-permute-done.6.theirs_ref
  40.6 0.1 add_cores.3
  40.7 1.9 %collective-permute-start.7 = (f32[2,4,6,16,128]{4,3,2,1,0:T(8,128)S(1)}, f32[2,4,6,16,128]{4,3,2,1,0:T(8,128)S(1)}, u32[]{:S(2)}, u32[]{:S(2)}) collective-permute-start(f32[2,4,6,16,128]{4,3,2,1,0:T(8,128)S(1)} %get-tuple-element.35), channel_id=1, source_target_pairs={{0,32},{1,97},{32,0},{33,65},{64,96},{65,33},{96,64},{97,1},{2,34}... | collective-permute-start | bytes 1179656 | tf_op jit(solution)/shard_map/ppermute | solution.py:422
  42.6 0.2 collective-permute-done.3.theirs_ref
  42.9 0.1 add_cores.2
  42.9 3.7 %collective-permute-start.4 = (f32[2,4,6,16,128]{4,3,2,1,0:T(8,128)S(1)}, f32[2,4,6,16,128]{4,3,2,1,0:T(8,128)S(1)}, u32[]{:S(2)}, u32[]{:S(2)}) collective-permute-start(f32[2,4,6,16,128]{4,3,2,1,0:T(8,128)S(1)} %get-tuple-element.31), channel_id=1, source_target_pairs={{0,32},{1,97},{32,0},{33,65},{64,96},{65,33},{96,64},{97,1},{2,34}... | collective-permute-start | bytes 1179656 | tf_op jit(solution)/shard_map/ppermute | solution.py:422
  46.7 3.1 %collective-permute-start.9 = (f32[2,264,256]{2,1,0:T(8,128)S(1)}, f32[2,264,256]{2,1,0:T(8,128)S(1)}, u32[]{:S(2)}, u32[]{:S(2)}) collective-permute-start(f32[2,264,256]{2,1,0:T(8,128)S(1)} %get-tuple-element.37), channel_id=1, source_target_pairs={{0,1},{1,2},{2,3},{3,4},{4,5},{5,6},{6,7},{7,8},{8,9},{9,10},{10,1... | collective-permute-start | bytes 1622024 | tf_op jit(solution)/shard_map/ppermute | solution.py:25
  49.8 0.6 collective-permute-done.7.got_im
  50.4 3.0 %collective-permute-start.8 = (f32[4,6,16,128]{3,2,1,0:T(8,128)S(1)}, f32[4,6,16,128]{3,2,1,0:T(8,128)S(1)}, u32[]{:S(2)}, u32[]{:S(2)}) collective-permute-start(f32[4,6,16,128]{3,2,1,0:T(8,128)S(1)} %fusion), channel_id=1, source_target_pairs={{0,96},{1,33},{32,64},{33,1},{64,32},{65,97},{96,0},{97,65},{2,98}... | collective-permute-start | bytes 589832 | tf_op jit(solution)/shard_map/ppermute | solution.py:426
  53.4 1.2 %collective-permute-done.4.got_re = f32[2,4,6,16,128]{4,3,2,1,0:T(8,128)S(1)} collective-permute-done((f32[2,4,6,16,128]{4,3,2,1,0:T(8,128)S(1)}, f32[2,4,6,16,128]{4,3,2,1,0:T(8,128)S(1)}, u32[]{:S(2)}, u32[]{:S(2)}) %collective-permute-start.4) | collective-permute-done | bytes 393248 | tf_op jit(solution)/shard_map/ppermute | solution.py:422
  54.6 3.0 %collective-permute-start.5 = (f32[4,6,16,128]{3,2,1,0:T(8,128)S(1)}, f32[4,6,16,128]{3,2,1,0:T(8,128)S(1)}, u32[]{:S(2)}, u32[]{:S(2)}) collective-permute-start(f32[4,6,16,128]{3,2,1,0:T(8,128)S(1)} %fusion.1), channel_id=1, source_target_pairs={{0,96},{1,33},{32,64},{33,1},{64,32},{65,97},{96,0},{97,65},{2,98}... | collective-permute-start | bytes 589832 | tf_op jit(solution)/shard_map/ppermute | solution.py:426
  57.6 1.6 %collective-permute-done.8.came_im = f32[4,6,16,128]{3,2,1,0:T(8,128)S(1)} collective-permute-done((f32[4,6,16,128]{3,2,1,0:T(8,128)S(1)}, f32[4,6,16,128]{3,2,1,0:T(8,128)S(1)}, u32[]{:S(2)}, u32[]{:S(2)}) %collective-permute-start.8) | collective-permute-done | bytes 196640 | tf_op jit(solution)/shard_map/ppermute | solution.py:426
  59.2 4.2 %collective-permute-done.5.came_re = f32[4,6,16,128]{3,2,1,0:T(8,128)S(1)} collective-permute-done((f32[4,6,16,128]{3,2,1,0:T(8,128)S(1)}, f32[4,6,16,128]{3,2,1,0:T(8,128)S(1)}, u32[]{:S(2)}, u32[]{:S(2)}) %collective-permute-start.5) | collective-permute-done | bytes 196640 | tf_op jit(solution)/shard_map/ppermute | solution.py:426
  63.4 1.1 %add_columns.1 = f32[8,16,768]{2,1,0:T(8,128)} custom-call(f32[2,4,6,16,128]{4,3,2,1,0:T(8,128)S(1)} %get-tuple-element.30.kept_re, f32[2,4,6,16,128]{4,3,2,1,0:T(8,128)S(1)} %collective-permute-done.4.got_re, f32[4,6,16,128]{3,2,1,0:T(8,128)S(1)} %collective-permute-done.5.came_re, f32[2,4,6,16,128]{4,3,2,1,0:T(8,128)S(1)} %get-tuple-element.34.kept_im, ...), custom_call_target="tpu_custom_call" | custom-call | bytes 2000000 | tf_op jit(solution)/shard_map/add_columns/pallas_call | solution.py:427
  64.5 0.0 copy-start.2
  64.5 11.9 %all-to-all-start = ((f32[8,16,768]{2,1,0:T(8,128)}), f32[8,16,768]{2,1,0:T(8,128)S(1)}, u32[]{:S(2)}, u32[]{:S(2)}) async-start(f32[8,16,768]{2,1,0:T(8,128)} %add_columns.1), calls=%async_computation | async-start | bytes 786432 | tf_op jit(solution)/shard_map/all_to_all | solution.py:433
  76.4 0.0 collective-permute-done.9.moved_ref
  76.4 0.7 down.1
  77.1 2.4 %collective-permute-start.10 = (f32[2,256,256]{2,1,0:T(8,128)S(1)}, f32[2,256,256]{2,1,0:T(8,128)S(1)}, u32[]{:S(2)}, u32[]{:S(2)}) collective-permute-start(f32[2,256,256]{2,1,0:T(8,128)S(1)} %get-tuple-element.39), channel_id=1, source_target_pairs={{0,32},{32,64},{64,96},{96,128},{128,160},{160,192},{192,224},{224... | collective-permute-start | bytes 1572872 | tf_op jit(solution)/shard_map/ppermute | solution.py:25
  79.5 0.9 constant_dynamic-slice_fusion
  80.4 0.1 copy.12
  80.5 9.2 %all-to-all-done.parts_ref = f32[8,16,768]{2,1,0:T(8,128)S(1)} async-done(((f32[8,16,768]{2,1,0:T(8,128)}), f32[8,16,768]{2,1,0:T(8,128)S(1)}, u32[]{:S(2)}, u32[]{:S(2)}) %all-to-all-start) | async-done | bytes 393248 | tf_op jit(solution)/shard_map/all_to_all | solution.py:433
  89.7 0.7 add_depth.1
  90.4 6.6 %all-to-all-start.1 = ((f32[8,8,192]{2,1,0:T(8,128)}), f32[8,8,192]{2,1,0:T(8,128)S(1)}, u32[]{:S(2)}, u32[]{:S(2)}) async-start(f32[8,8,192]{2,1,0:T(8,128)} %add_depth.1), calls=%async_computation.1 | async-start | bytes 131072 | tf_op jit(solution)/shard_map/all_to_all | solution.py:435
  97.0 0.0 collective-permute-done.10
  97.0 0.0 copy-done.2
  97.0 0.9 multiply_subtract_fusion
  97.9 6.9 %all-to-all-done.1 = f32[8,8,192]{2,1,0:T(8,128)S(1)} async-done(((f32[8,8,192]{2,1,0:T(8,128)}), f32[8,8,192]{2,1,0:T(8,128)S(1)}, u32[]{:S(2)}, u32[]{:S(2)}) %all-to-all-start.1) | async-done | bytes 49184 | tf_op jit(solution)/shard_map/all_to_all | solution.py:435
  104.8 0.1 mul.42
  104.9 0.6 copy.11
  (6 shorter events, 0.1 us)
Async XLA Ops:
  0.6 12.1 %copy-start = (bf16[8,2,256,256]{3,2,1,0:T(8,128)(2,1)S(1)}, bf16[8,2,256,256]{3,2,1,0:T(8,128)(2,1)}, u32[]{:S(2)}) copy-start(bf16[8,2,256,256]{3,2,1,0:T(8,128)(2,1)} %constant.43.clone.table_in) | copy-start | bytes 6291460
  0.6 8.1 %collective-permute-start.1 = (f32[2,256,256]{2,1,0:T(8,128)}, f32[2,256,256]{2,1,0:T(8,128)S(1)}, u32[]{:S(2)}, u32[]{:S(2)}) collective-permute-start(f32[2,256,256]{2,1,0:T(8,128)} %tile_in), channel_id=1, source_target_pairs={{1,0},{2,1},{3,2},{4,3},{5,4},{6,5},{7,6},{8,7},{9,8},{10,9},{11,1... | collective-permute-start | bytes 1572872 | tf_op jit(solution)/shard_map/ppermute | solution.py:25
  2.1 5.6 %collective-permute-start = (s32[1,1,1,2]{3,2,1,0:T(1,128)}, s32[1,1,1,2]{3,2,1,0:T(1,128)S(1)}, u32[]{:S(2)}, u32[]{:S(2)}) collective-permute-start(s32[1,1,1,2]{3,2,1,0:T(1,128)} %param.9), channel_id=1, source_target_pairs={{0,32},{32,64},{64,96},{96,128},{128,160},{160,192},{192,224},{224... | collective-permute-start | bytes 32 | tf_op jit(solution)/shard_map/ppermute | solution.py:25
  7.7 1.0 copy-start.1
  8.7 4.0 %copy-start.4 = (bf16[4,256,256]{2,1,0:T(8,128)(2,1)S(1)}, bf16[4,256,256]{2,1,0:T(8,128)(2,1)}, u32[]{:S(2)}) copy-start(bf16[4,256,256]{2,1,0:T(8,128)(2,1)} %constant.44.clone.order_in) | copy-start | bytes 1572868
  9.4 17.5 %collective-permute-start.2 = (f32[2,256,256]{2,1,0:T(8,128)S(1)}, f32[2,256,256]{2,1,0:T(8,128)S(1)}, u32[]{:S(2)}, u32[]{:S(2)}) collective-permute-start(f32[2,256,256]{2,1,0:T(8,128)S(1)} %mix.1), channel_id=1, source_target_pairs={{32,0},{64,32},{96,64},{128,96},{160,128},{192,160},{224,192},{256... | collective-permute-start | bytes 1572872 | tf_op jit(solution)/shard_map/ppermute | solution.py:25
  12.8 1.4 %copy-start.3 = (bf16[2,6,256,256]{3,2,1,0:T(8,128)(2,1)S(1)}, bf16[2,6,256,256]{3,2,1,0:T(8,128)(2,1)}, u32[]{:S(2)}) copy-start(bf16[2,6,256,256]{3,2,1,0:T(8,128)(2,1)} %probe_in.1) | copy-start | bytes 4718596
  14.2 0.9 copy-start.5
  15.1 11.8 %copy-start.6 = (s32[1,1,1,2]{3,2,1,0:T(1,128)S(1)}, s32[1,1,1,2]{3,2,1,0:T(1,128)}, u32[]{:S(2)}) copy-start(s32[1,1,1,2]{3,2,1,0:T(1,128)} %param.9) | copy-start | bytes 28
  35.4 5.2 %collective-permute-start.6 = (f32[4,4,6,16,128]{4,3,2,1,0:T(8,128)S(1)}, f32[4,4,6,16,128]{4,3,2,1,0:T(8,128)S(1)}, u32[]{:S(2)}, u32[]{:S(2)}) collective-permute-start(f32[4,4,6,16,128]{4,3,2,1,0:T(8,128)S(1)} %get-tuple-element.33), channel_id=1, source_target_pairs={{0,1},{1,0},{2,3},{3,2},{4,5},{5,4},{6,7},{7,6},{8,9},{9,8},{10,11... | collective-permute-start | bytes 2359304 | tf_op jit(solution)/shard_map/ppermute | solution.py:417
  38.7 4.2 %collective-permute-start.3 = (f32[4,4,6,16,128]{4,3,2,1,0:T(8,128)S(1)}, f32[4,4,6,16,128]{4,3,2,1,0:T(8,128)S(1)}, u32[]{:S(2)}, u32[]{:S(2)}) collective-permute-start(f32[4,4,6,16,128]{4,3,2,1,0:T(8,128)S(1)} %get-tuple-element.29), channel_id=1, source_target_pairs={{0,1},{1,0},{2,3},{3,2},{4,5},{5,4},{6,7},{7,6},{8,9},{9,8},{10,11... | collective-permute-start | bytes 2359304 | tf_op jit(solution)/shard_map/ppermute | solution.py:417
  40.7 9.7 %collective-permute-start.7 = (f32[2,4,6,16,128]{4,3,2,1,0:T(8,128)S(1)}, f32[2,4,6,16,128]{4,3,2,1,0:T(8,128)S(1)}, u32[]{:S(2)}, u32[]{:S(2)}) collective-permute-start(f32[2,4,6,16,128]{4,3,2,1,0:T(8,128)S(1)} %get-tuple-element.35), channel_id=1, source_target_pairs={{0,32},{1,97},{32,0},{33,65},{64,96},{65,33},{96,64},{97,1},{2,34}... | collective-permute-start | bytes 1179656 | tf_op jit(solution)/shard_map/ppermute | solution.py:422
  42.9 11.7 %collective-permute-start.4 = (f32[2,4,6,16,128]{4,3,2,1,0:T(8,128)S(1)}, f32[2,4,6,16,128]{4,3,2,1,0:T(8,128)S(1)}, u32[]{:S(2)}, u32[]{:S(2)}) collective-permute-start(f32[2,4,6,16,128]{4,3,2,1,0:T(8,128)S(1)} %get-tuple-element.31), channel_id=1, source_target_pairs={{0,32},{1,97},{32,0},{33,65},{64,96},{65,33},{96,64},{97,1},{2,34}... | collective-permute-start | bytes 1179656 | tf_op jit(solution)/shard_map/ppermute | solution.py:422
  46.7 29.7 %collective-permute-start.9 = (f32[2,264,256]{2,1,0:T(8,128)S(1)}, f32[2,264,256]{2,1,0:T(8,128)S(1)}, u32[]{:S(2)}, u32[]{:S(2)}) collective-permute-start(f32[2,264,256]{2,1,0:T(8,128)S(1)} %get-tuple-element.37), channel_id=1, source_target_pairs={{0,1},{1,2},{2,3},{3,4},{4,5},{5,6},{6,7},{7,8},{8,9},{9,10},{10,1... | collective-permute-start | bytes 1622024 | tf_op jit(solution)/shard_map/ppermute | solution.py:25
  50.4 8.8 %collective-permute-start.8 = (f32[4,6,16,128]{3,2,1,0:T(8,128)S(1)}, f32[4,6,16,128]{3,2,1,0:T(8,128)S(1)}, u32[]{:S(2)}, u32[]{:S(2)}) collective-permute-start(f32[4,6,16,128]{3,2,1,0:T(8,128)S(1)} %fusion), channel_id=1, source_target_pairs={{0,96},{1,33},{32,64},{33,1},{64,32},{65,97},{96,0},{97,65},{2,98}... | collective-permute-start | bytes 589832 | tf_op jit(solution)/shard_map/ppermute | solution.py:426
  54.6 8.8 %collective-permute-start.5 = (f32[4,6,16,128]{3,2,1,0:T(8,128)S(1)}, f32[4,6,16,128]{3,2,1,0:T(8,128)S(1)}, u32[]{:S(2)}, u32[]{:S(2)}) collective-permute-start(f32[4,6,16,128]{3,2,1,0:T(8,128)S(1)} %fusion.1), channel_id=1, source_target_pairs={{0,96},{1,33},{32,64},{33,1},{64,32},{65,97},{96,0},{97,65},{2,98}... | collective-permute-start | bytes 589832 | tf_op jit(solution)/shard_map/ppermute | solution.py:426
  64.5 32.6 %copy-start.2 = (f32[2,256,256]{2,1,0:T(8,128)S(1)}, f32[2,256,256]{2,1,0:T(8,128)}, u32[]{:S(2)}) copy-start(f32[2,256,256]{2,1,0:T(8,128)} %tile_in) | copy-start | bytes 1572868
  64.5 25.2 %all-to-all-start = ((f32[8,16,768]{2,1,0:T(8,128)}), f32[8,16,768]{2,1,0:T(8,128)S(1)}, u32[]{:S(2)}, u32[]{:S(2)}) async-start(f32[8,16,768]{2,1,0:T(8,128)} %add_columns.1), calls=%async_computation | async-start | bytes 786432 | tf_op jit(solution)/shard_map/all_to_all | solution.py:433
  77.1 19.9 %collective-permute-start.10 = (f32[2,256,256]{2,1,0:T(8,128)S(1)}, f32[2,256,256]{2,1,0:T(8,128)S(1)}, u32[]{:S(2)}, u32[]{:S(2)}) collective-permute-start(f32[2,256,256]{2,1,0:T(8,128)S(1)} %get-tuple-element.39), channel_id=1, source_target_pairs={{0,32},{32,64},{64,96},{96,128},{128,160},{160,192},{192,224},{224... | collective-permute-start | bytes 1572872 | tf_op jit(solution)/shard_map/ppermute | solution.py:25
  90.4 14.4 %all-to-all-start.1 = ((f32[8,8,192]{2,1,0:T(8,128)}), f32[8,8,192]{2,1,0:T(8,128)S(1)}, u32[]{:S(2)}, u32[]{:S(2)}) async-start(f32[8,8,192]{2,1,0:T(8,128)} %add_depth.1), calls=%async_computation.1 | async-start | bytes 131072 | tf_op jit(solution)/shard_map/all_to_all | solution.py:435

commit v4 on v3

--- a/solution.py
+++ b/solution.py
@@ -332,6 +332,16 @@
     for z in range(4):
         for z_hi in range(2):
             out_ref[2 * z + z_hi] = total[z_hi * 8 : z_hi * 8 + 8, z * 192 : z * 192 + 192]
+
+
+def finish_kernel(parts_ref, own_ref, out_ref):
+    total = parts_ref[0]
+    for i in range(1, 8):
+        total = total + parts_ref[i]
+    for part in range(2):
+        for mode in range(modes):
+            at = (part * modes + mode) * strip
+            out_ref[part, mode] = own_ref[part, mode] - (512.0 ** -0.5) * total[:, at : at + strip]
 
 
 def shaped(*shape, dtype=f32):
@@ -433,8 +443,9 @@
     parts = lax.all_to_all(packed, "y", 0, 0, tiled=True)
     packed = call(depth_kernel, "add_depth", [vmem], [shaped(8, 8, 192)], moved=500_000)(parts)
     parts = lax.all_to_all(packed, ("z_lo", "z_hi"), 0, 0, tiled=True)
-    share = jnp.sum(parts, axis=0).reshape(8, 2, modes, strip).transpose(1, 2, 3, 0)
-    probe_new = own_probe - (512.0 ** -0.5) * share
+    probe_new = call(finish_kernel, "finish", [vmem] * 2, [shaped(2, modes, 8, strip)], moved=200_000)(
+        parts, own_probe.transpose(0, 1, 3, 2)
+    ).transpose(0, 1, 3, 2)
 
     object_new = object_field - object_rate * (held + from_above)
     return (object_new, probe_new)

time: 106 us -> 106 us (level)
    unnamed x16 -> x15, local copies, waits for them, and re-layouts: 4.11 us -> 3.46 us
where the time goes in v4:
time: 106 us
  starting transfers between devices  49.1 us (46%)
  waiting for transfers between devices  35.6 us (34%)
  Pallas kernels  13.9 us (13%)
  local copies, waits for them, and re-layouts  4.36 us (4%)
  between operations  1.51 us (1%)
    ppermute x5, starting transfers between devices, passed_along(): return lax.ppermute(x, axis, pairs)  13.8 us
    all_to_all x1, starting transfers between devices, local(): parts = lax.all_to_all(packed, 'y', 0, 0, tiled=True)  11.9 us
    ppermute x5, waiting for transfers between devices, passed_along(): return lax.ppermute(x, axis, pairs)  11.8 us
    all_to_all x1, waiting for transfers between devices, local(): parts = lax.all_to_all(packed, 'y', 0, 0, tiled=True)  9.19 us
    pallas_call x1, Pallas kernels, local(): call(main_kernel, 'step', [smem, smem] + [vmem] * 7, [shaped(*block_shape...  8.49 us
    all_to_all x1, waiting for transfers between devices, local(): parts = lax.all_to_all(packed, ('z_lo', 'z_hi'), 0, 0, tiled=True)  6.86 us
    all_to_all x1, starting transfers between devices, local(): parts = lax.all_to_all(packed, ('z_lo', 'z_hi'), 0, 0, tiled=True)  6.6 us
    ppermute x2, starting transfers between devices, local(): lax.ppermute(keep[1] + got[1], ('x', 'core'), far_pairs)  5.99 us
  transfers between devices with their start and end apart: 13, of which 9 were waited for; matrix products, arithmetic and copies ran while one was open for 2% of the time, Pallas kernels for 4%

profile of v4, /device:TPU:6, one launch (start us, length us, event | category | flops | bytes accessed | tf_op | source)
XLA Modules:
  0.0 105.5 jit_solution(3061482424266398558)
XLA Ops:
  0.6 0.0 copy-start
  0.6 1.4 %collective-permute-start.1 = (f32[2,256,256]{2,1,0:T(8,128)}, f32[2,256,256]{2,1,0:T(8,128)S(1)}, u32[]{:S(2)}, u32[]{:S(2)}) collective-permute-start(f32[2,256,256]{2,1,0:T(8,128)} %tile_in), channel_id=1, source_target_pairs={{1,0},{2,1},{3,2},{4,3},{5,4},{6,5},{7,6},{8,7},{9,8},{10,9},{11,1... | collective-permute-start | bytes 1572872 | tf_op jit(solution)/shard_map/ppermute | solution.py:25
  2.1 4.2 %collective-permute-start = (s32[1,1,1,2]{3,2,1,0:T(1,128)}, s32[1,1,1,2]{3,2,1,0:T(1,128)S(1)}, u32[]{:S(2)}, u32[]{:S(2)}) collective-permute-start(s32[1,1,1,2]{3,2,1,0:T(1,128)} %param.9), channel_id=1, source_target_pairs={{0,32},{32,64},{64,96},{96,128},{128,160},{160,192},{192,224},{224... | collective-permute-start | bytes 32 | tf_op jit(solution)/shard_map/ppermute | solution.py:25
  6.3 1.4 %collective-permute-done = s32[1,1,1,2]{3,2,1,0:T(1,128)S(1)} collective-permute-done((s32[1,1,1,2]{3,2,1,0:T(1,128)}, s32[1,1,1,2]{3,2,1,0:T(1,128)S(1)}, u32[]{:S(2)}, u32[]{:S(2)}) %collective-permute-start) | collective-permute-done | bytes 40 | tf_op jit(solution)/shard_map/ppermute | solution.py:25
  7.7 0.0 copy-start.1
  7.7 1.0 copy-done.1
  8.7 0.0 copy-start.4
  8.8 0.0 collective-permute-done.1.right_ref
  8.8 0.6 mix.1
  9.4 2.7 %collective-permute-start.2 = (f32[2,256,256]{2,1,0:T(8,128)S(1)}, f32[2,256,256]{2,1,0:T(8,128)S(1)}, u32[]{:S(2)}, u32[]{:S(2)}) collective-permute-start(f32[2,256,256]{2,1,0:T(8,128)S(1)} %mix.1), channel_id=1, source_target_pairs={{32,0},{64,32},{96,64},{128,96},{160,128},{192,160},{224,192},{256... | collective-permute-start | bytes 1572872 | tf_op jit(solution)/shard_map/ppermute | solution.py:25
  12.7 0.0 copy-done
  12.8 0.0 copy-done.4
  12.8 0.0 copy-start.3
  12.8 1.4 %copy-done.3 = bf16[2,6,256,256]{3,2,1,0:T(8,128)(2,1)S(1)} copy-done((bf16[2,6,256,256]{3,2,1,0:T(8,128)(2,1)S(1)}, bf16[2,6,256,256]{3,2,1,0:T(8,128)(2,1)}, u32[]{:S(2)}) %copy-start.3) | copy-done | bytes 1572888
  14.2 0.0 copy-start.5
  14.2 0.9 copy-done.5
  15.1 0.0 copy-start.6
  15.1 1.4 %prepare.1 = (bf16[2,6,256,256]{3,2,1,0:T(8,128)(2,1)S(1)}, f32[256,256]{1,0:T(8,128)S(1)}, bf16[8,2,256,256]{3,2,1,0:T(8,128)(2,1)S(1)}, bf16[2,256,256]{2,1,0:T(8,128)(2,1)S(1)}) custom-call(bf16[2,6,256,256]{3,2,1,0:T(8,128)(2,1)S(1)} %copy-done.3, bf16[256,256]{1,0:T(8,128)(2,1)S(1)} %bitcast.12, bf16[8,2,256,256]{3,2,1,0:T(8,128)(2,1)S(1)} %copy-done, ...), custom_call_target="tpu_custom_call" | custom-call | flops 500000000 | bytes 8000000 | tf_op jit(solution)/shard_map/prepare/pallas_call | solution.py:391
  16.5 10.4 %collective-permute-done.2.lower_ref = f32[2,256,256]{2,1,0:T(8,128)S(1)} collective-permute-done((f32[2,256,256]{2,1,0:T(8,128)S(1)}, f32[2,256,256]{2,1,0:T(8,128)S(1)}, u32[]{:S(2)}, u32[]{:S(2)}) %collective-permute-start.2) | collective-permute-done | bytes 524320 | tf_op jit(solution)/shard_map/ppermute | solution.py:25
  26.9 0.0 copy-done.6
  26.9 8.5 %step.1 = (f32[4,4,6,16,128]{4,3,2,1,0:T(8,128)S(1)}, f32[4,4,6,16,128]{4,3,2,1,0:T(8,128)S(1)}, f32[4,4,6,16,128]{4,3,2,1,0:T(8,128)S(1)}, f32[4,4,6,16,128]{4,...) custom-call(s32[2]{0:T(128)S(1)} %bitcast.13, s32[1]{0:T(128)} %bitcast.11.count_ref, ...), custom_call_target="tpu_custom_call" | custom-call | flops 5000000000 | bytes 12000000 | tf_op jit(solution)/shard_map/step/pallas_call | solution.py:412
  35.4 3.2 %collective-permute-start.6 = (f32[4,4,6,16,128]{4,3,2,1,0:T(8,128)S(1)}, f32[4,4,6,16,128]{4,3,2,1,0:T(8,128)S(1)}, u32[]{:S(2)}, u32[]{:S(2)}) collective-permute-start(f32[4,4,6,16,128]{4,3,2,1,0:T(8,128)S(1)} %get-tuple-element.33), channel_id=1, source_target_pairs={{0,1},{1,0},{2,3},{3,2},{4,5},{5,4},{6,7},{7,6},{8,9},{9,8},{10,11... | collective-permute-start | bytes 2359304 | tf_op jit(solution)/shard_map/ppermute | solution.py:427
  38.7 1.9 %collective-permute-start.3 = (f32[4,4,6,16,128]{4,3,2,1,0:T(8,128)S(1)}, f32[4,4,6,16,128]{4,3,2,1,0:T(8,128)S(1)}, u32[]{:S(2)}, u32[]{:S(2)}) collective-permute-start(f32[4,4,6,16,128]{4,3,2,1,0:T(8,128)S(1)} %get-tuple-element.29), channel_id=1, source_target_pairs={{0,1},{1,0},{2,3},{3,2},{4,5},{5,4},{6,7},{7,6},{8,9},{9,8},{10,11... | collective-permute-start | bytes 2359304 | tf_op jit(solution)/shard_map/ppermute | solution.py:427
  40.6 0.0 collective-permute-done.6.theirs_ref
  40.6 0.1 add_cores.3
  40.7 1.9 %collective-permute-start.7 = (f32[2,4,6,16,128]{4,3,2,1,0:T(8,128)S(1)}, f32[2,4,6,16,128]{4,3,2,1,0:T(8,128)S(1)}, u32[]{:S(2)}, u32[]{:S(2)}) collective-permute-start(f32[2,4,6,16,128]{4,3,2,1,0:T(8,128)S(1)} %get-tuple-element.35), channel_id=1, source_target_pairs={{0,32},{1,97},{32,0},{33,65},{64,96},{65,33},{96,64},{97,1},{2,34}... | collective-permute-start | bytes 1179656 | tf_op jit(solution)/shard_map/ppermute | solution.py:432
  42.6 0.2 collective-permute-done.3.theirs_ref
  42.9 0.1 add_cores.2
  42.9 3.7 %collective-permute-start.4 = (f32[2,4,6,16,128]{4,3,2,1,0:T(8,128)S(1)}, f32[2,4,6,16,128]{4,3,2,1,0:T(8,128)S(1)}, u32[]{:S(2)}, u32[]{:S(2)}) collective-permute-start(f32[2,4,6,16,128]{4,3,2,1,0:T(8,128)S(1)} %get-tuple-element.31), channel_id=1, source_target_pairs={{0,32},{1,97},{32,0},{33,65},{64,96},{65,33},{96,64},{97,1},{2,34}... | collective-permute-start | bytes 1179656 | tf_op jit(solution)/shard_map/ppermute | solution.py:432
  46.7 3.1 %collective-permute-start.9 = (f32[2,264,256]{2,1,0:T(8,128)S(1)}, f32[2,264,256]{2,1,0:T(8,128)S(1)}, u32[]{:S(2)}, u32[]{:S(2)}) collective-permute-start(f32[2,264,256]{2,1,0:T(8,128)S(1)} %get-tuple-element.37), channel_id=1, source_target_pairs={{0,1},{1,2},{2,3},{3,4},{4,5},{5,6},{6,7},{7,8},{8,9},{9,10},{10,1... | collective-permute-start | bytes 1622024 | tf_op jit(solution)/shard_map/ppermute | solution.py:25
  49.8 0.6 collective-permute-done.7.got_im
  50.4 3.0 %collective-permute-start.8 = (f32[4,6,16,128]{3,2,1,0:T(8,128)S(1)}, f32[4,6,16,128]{3,2,1,0:T(8,128)S(1)}, u32[]{:S(2)}, u32[]{:S(2)}) collective-permute-start(f32[4,6,16,128]{3,2,1,0:T(8,128)S(1)} %fusion), channel_id=1, source_target_pairs={{0,96},{1,33},{32,64},{33,1},{64,32},{65,97},{96,0},{97,65},{2,98}... | collective-permute-start | bytes 589832 | tf_op jit(solution)/shard_map/ppermute | solution.py:436
  53.4 1.2 %collective-permute-done.4.got_re = f32[2,4,6,16,128]{4,3,2,1,0:T(8,128)S(1)} collective-permute-done((f32[2,4,6,16,128]{4,3,2,1,0:T(8,128)S(1)}, f32[2,4,6,16,128]{4,3,2,1,0:T(8,128)S(1)}, u32[]{:S(2)}, u32[]{:S(2)}) %collective-permute-start.4) | collective-permute-done | bytes 393248 | tf_op jit(solution)/shard_map/ppermute | solution.py:432
  54.6 3.0 %collective-permute-start.5 = (f32[4,6,16,128]{3,2,1,0:T(8,128)S(1)}, f32[4,6,16,128]{3,2,1,0:T(8,128)S(1)}, u32[]{:S(2)}, u32[]{:S(2)}) collective-permute-start(f32[4,6,16,128]{3,2,1,0:T(8,128)S(1)} %fusion.1), channel_id=1, source_target_pairs={{0,96},{1,33},{32,64},{33,1},{64,32},{65,97},{96,0},{97,65},{2,98}... | collective-permute-start | bytes 589832 | tf_op jit(solution)/shard_map/ppermute | solution.py:436
  57.6 1.6 %collective-permute-done.8.came_im = f32[4,6,16,128]{3,2,1,0:T(8,128)S(1)} collective-permute-done((f32[4,6,16,128]{3,2,1,0:T(8,128)S(1)}, f32[4,6,16,128]{3,2,1,0:T(8,128)S(1)}, u32[]{:S(2)}, u32[]{:S(2)}) %collective-permute-start.8) | collective-permute-done | bytes 196640 | tf_op jit(solution)/shard_map/ppermute | solution.py:436
  59.2 4.2 %collective-permute-done.5.came_re = f32[4,6,16,128]{3,2,1,0:T(8,128)S(1)} collective-permute-done((f32[4,6,16,128]{3,2,1,0:T(8,128)S(1)}, f32[4,6,16,128]{3,2,1,0:T(8,128)S(1)}, u32[]{:S(2)}, u32[]{:S(2)}) %collective-permute-start.5) | collective-permute-done | bytes 196640 | tf_op jit(solution)/shard_map/ppermute | solution.py:436
  63.4 1.1 %add_columns.1 = f32[8,16,768]{2,1,0:T(8,128)} custom-call(f32[2,4,6,16,128]{4,3,2,1,0:T(8,128)S(1)} %get-tuple-element.30.kept_re, f32[2,4,6,16,128]{4,3,2,1,0:T(8,128)S(1)} %collective-permute-done.4.got_re, f32[4,6,16,128]{3,2,1,0:T(8,128)S(1)} %collective-permute-done.5.came_re, f32[2,4,6,16,128]{4,3,2,1,0:T(8,128)S(1)} %get-tuple-element.34.kept_im, ...), custom_call_target="tpu_custom_call" | custom-call | bytes 2000000 | tf_op jit(solution)/shard_map/add_columns/pallas_call | solution.py:437
  64.5 0.0 copy-start.2
  64.5 11.9 %all-to-all-start = ((f32[8,16,768]{2,1,0:T(8,128)}), f32[8,16,768]{2,1,0:T(8,128)S(1)}, u32[]{:S(2)}, u32[]{:S(2)}) async-start(f32[8,16,768]{2,1,0:T(8,128)} %add_columns.1), calls=%async_computation | async-start | bytes 786432 | tf_op jit(solution)/shard_map/all_to_all | solution.py:443
  76.4 0.0 collective-permute-done.9.moved_ref
  76.4 0.7 down.1
  77.1 2.4 %collective-permute-start.10 = (f32[2,256,256]{2,1,0:T(8,128)S(1)}, f32[2,256,256]{2,1,0:T(8,128)S(1)}, u32[]{:S(2)}, u32[]{:S(2)}) collective-permute-start(f32[2,256,256]{2,1,0:T(8,128)S(1)} %get-tuple-element.39), channel_id=1, source_target_pairs={{0,32},{32,64},{64,96},{96,128},{128,160},{160,192},{192,224},{224... | collective-permute-start | bytes 1572872 | tf_op jit(solution)/shard_map/ppermute | solution.py:25
  79.5 0.9 constant_dynamic-slice_fusion
  80.4 0.1 copy.10
  80.5 9.2 %all-to-all-done.parts_ref = f32[8,16,768]{2,1,0:T(8,128)S(1)} async-done(((f32[8,16,768]{2,1,0:T(8,128)}), f32[8,16,768]{2,1,0:T(8,128)S(1)}, u32[]{:S(2)}, u32[]{:S(2)}) %all-to-all-start) | async-done | bytes 393248 | tf_op jit(solution)/shard_map/all_to_all | solution.py:443
  89.7 0.7 add_depth.1
  90.4 6.6 %all-to-all-start.1 = ((f32[8,8,192]{2,1,0:T(8,128)}), f32[8,8,192]{2,1,0:T(8,128)S(1)}, u32[]{:S(2)}, u32[]{:S(2)}) async-start(f32[8,8,192]{2,1,0:T(8,128)} %add_depth.1), calls=%async_computation.1 | async-start | bytes 131072 | tf_op jit(solution)/shard_map/all_to_all | solution.py:445
  97.0 0.0 collective-permute-done.10
  97.0 0.0 copy-done.2
  97.0 0.9 multiply_subtract_fusion
  97.9 6.9 %all-to-all-done.1.parts_ref = f32[8,8,192]{2,1,0:T(8,128)S(1)} async-done(((f32[8,8,192]{2,1,0:T(8,128)}), f32[8,8,192]{2,1,0:T(8,128)S(1)}, u32[]{:S(2)}, u32[]{:S(2)}) %all-to-all-start.1) | async-done | bytes 49184 | tf_op jit(solution)/shard_map/all_to_all | solution.py:445
  104.8 0.7 finish.1
  (4 shorter events, 0.1 us)
Async XLA Ops:
  0.6 12.1 %copy-start = (bf16[8,2,256,256]{3,2,1,0:T(8,128)(2,1)S(1)}, bf16[8,2,256,256]{3,2,1,0:T(8,128)(2,1)}, u32[]{:S(2)}) copy-start(bf16[8,2,256,256]{3,2,1,0:T(8,128)(2,1)} %constant.39.clone.table_in) | copy-start | bytes 6291460
  0.6 8.1 %collective-permute-start.1 = (f32[2,256,256]{2,1,0:T(8,128)}, f32[2,256,256]{2,1,0:T(8,128)S(1)}, u32[]{:S(2)}, u32[]{:S(2)}) collective-permute-start(f32[2,256,256]{2,1,0:T(8,128)} %tile_in), channel_id=1, source_target_pairs={{1,0},{2,1},{3,2},{4,3},{5,4},{6,5},{7,6},{8,7},{9,8},{10,9},{11,1... | collective-permute-start | bytes 1572872 | tf_op jit(solution)/shard_map/ppermute | solution.py:25
  2.1 5.6 %collective-permute-start = (s32[1,1,1,2]{3,2,1,0:T(1,128)}, s32[1,1,1,2]{3,2,1,0:T(1,128)S(1)}, u32[]{:S(2)}, u32[]{:S(2)}) collective-permute-start(s32[1,1,1,2]{3,2,1,0:T(1,128)} %param.9), channel_id=1, source_target_pairs={{0,32},{32,64},{64,96},{96,128},{128,160},{160,192},{192,224},{224... | collective-permute-start | bytes 32 | tf_op jit(solution)/shard_map/ppermute | solution.py:25
  7.7 1.0 copy-start.1
  8.7 4.0 %copy-start.4 = (bf16[4,256,256]{2,1,0:T(8,128)(2,1)S(1)}, bf16[4,256,256]{2,1,0:T(8,128)(2,1)}, u32[]{:S(2)}) copy-start(bf16[4,256,256]{2,1,0:T(8,128)(2,1)} %constant.40.clone.order_in) | copy-start | bytes 1572868
  9.4 17.5 %collective-permute-start.2 = (f32[2,256,256]{2,1,0:T(8,128)S(1)}, f32[2,256,256]{2,1,0:T(8,128)S(1)}, u32[]{:S(2)}, u32[]{:S(2)}) collective-permute-start(f32[2,256,256]{2,1,0:T(8,128)S(1)} %mix.1), channel_id=1, source_target_pairs={{32,0},{64,32},{96,64},{128,96},{160,128},{192,160},{224,192},{256... | collective-permute-start | bytes 1572872 | tf_op jit(solution)/shard_map/ppermute | solution.py:25
  12.8 1.4 %copy-start.3 = (bf16[2,6,256,256]{3,2,1,0:T(8,128)(2,1)S(1)}, bf16[2,6,256,256]{3,2,1,0:T(8,128)(2,1)}, u32[]{:S(2)}) copy-start(bf16[2,6,256,256]{3,2,1,0:T(8,128)(2,1)} %probe_in.1) | copy-start | bytes 4718596
  14.2 0.9 copy-start.5
  15.1 11.8 %copy-start.6 = (s32[1,1,1,2]{3,2,1,0:T(1,128)S(1)}, s32[1,1,1,2]{3,2,1,0:T(1,128)}, u32[]{:S(2)}) copy-start(s32[1,1,1,2]{3,2,1,0:T(1,128)} %param.9) | copy-start | bytes 28
  35.4 5.2 %collective-permute-start.6 = (f32[4,4,6,16,128]{4,3,2,1,0:T(8,128)S(1)}, f32[4,4,6,16,128]{4,3,2,1,0:T(8,128)S(1)}, u32[]{:S(2)}, u32[]{:S(2)}) collective-permute-start(f32[4,4,6,16,128]{4,3,2,1,0:T(8,128)S(1)} %get-tuple-element.33), channel_id=1, source_target_pairs={{0,1},{1,0},{2,3},{3,2},{4,5},{5,4},{6,7},{7,6},{8,9},{9,8},{10,11... | collective-permute-start | bytes 2359304 | tf_op jit(solution)/shard_map/ppermute | solution.py:427
  38.7 4.2 %collective-permute-start.3 = (f32[4,4,6,16,128]{4,3,2,1,0:T(8,128)S(1)}, f32[4,4,6,16,128]{4,3,2,1,0:T(8,128)S(1)}, u32[]{:S(2)}, u32[]{:S(2)}) collective-permute-start(f32[4,4,6,16,128]{4,3,2,1,0:T(8,128)S(1)} %get-tuple-element.29), channel_id=1, source_target_pairs={{0,1},{1,0},{2,3},{3,2},{4,5},{5,4},{6,7},{7,6},{8,9},{9,8},{10,11... | collective-permute-start | bytes 2359304 | tf_op jit(solution)/shard_map/ppermute | solution.py:427
  40.7 9.7 %collective-permute-start.7 = (f32[2,4,6,16,128]{4,3,2,1,0:T(8,128)S(1)}, f32[2,4,6,16,128]{4,3,2,1,0:T(8,128)S(1)}, u32[]{:S(2)}, u32[]{:S(2)}) collective-permute-start(f32[2,4,6,16,128]{4,3,2,1,0:T(8,128)S(1)} %get-tuple-element.35), channel_id=1, source_target_pairs={{0,32},{1,97},{32,0},{33,65},{64,96},{65,33},{96,64},{97,1},{2,34}... | collective-permute-start | bytes 1179656 | tf_op jit(solution)/shard_map/ppermute | solution.py:432
  42.9 11.7 %collective-permute-start.4 = (f32[2,4,6,16,128]{4,3,2,1,0:T(8,128)S(1)}, f32[2,4,6,16,128]{4,3,2,1,0:T(8,128)S(1)}, u32[]{:S(2)}, u32[]{:S(2)}) collective-permute-start(f32[2,4,6,16,128]{4,3,2,1,0:T(8,128)S(1)} %get-tuple-element.31), channel_id=1, source_target_pairs={{0,32},{1,97},{32,0},{33,65},{64,96},{65,33},{96,64},{97,1},{2,34}... | collective-permute-start | bytes 1179656 | tf_op jit(solution)/shard_map/ppermute | solution.py:432
  46.7 29.7 %collective-permute-start.9 = (f32[2,264,256]{2,1,0:T(8,128)S(1)}, f32[2,264,256]{2,1,0:T(8,128)S(1)}, u32[]{:S(2)}, u32[]{:S(2)}) collective-permute-start(f32[2,264,256]{2,1,0:T(8,128)S(1)} %get-tuple-element.37), channel_id=1, source_target_pairs={{0,1},{1,2},{2,3},{3,4},{4,5},{5,6},{6,7},{7,8},{8,9},{9,10},{10,1... | collective-permute-start | bytes 1622024 | tf_op jit(solution)/shard_map/ppermute | solution.py:25
  50.4 8.8 %collective-permute-start.8 = (f32[4,6,16,128]{3,2,1,0:T(8,128)S(1)}, f32[4,6,16,128]{3,2,1,0:T(8,128)S(1)}, u32[]{:S(2)}, u32[]{:S(2)}) collective-permute-start(f32[4,6,16,128]{3,2,1,0:T(8,128)S(1)} %fusion), channel_id=1, source_target_pairs={{0,96},{1,33},{32,64},{33,1},{64,32},{65,97},{96,0},{97,65},{2,98}... | collective-permute-start | bytes 589832 | tf_op jit(solution)/shard_map/ppermute | solution.py:436
  54.6 8.8 %collective-permute-start.5 = (f32[4,6,16,128]{3,2,1,0:T(8,128)S(1)}, f32[4,6,16,128]{3,2,1,0:T(8,128)S(1)}, u32[]{:S(2)}, u32[]{:S(2)}) collective-permute-start(f32[4,6,16,128]{3,2,1,0:T(8,128)S(1)} %fusion.1), channel_id=1, source_target_pairs={{0,96},{1,33},{32,64},{33,1},{64,32},{65,97},{96,0},{97,65},{2,98}... | collective-permute-start | bytes 589832 | tf_op jit(solution)/shard_map/ppermute | solution.py:436
  64.5 32.6 %copy-start.2 = (f32[2,256,256]{2,1,0:T(8,128)S(1)}, f32[2,256,256]{2,1,0:T(8,128)}, u32[]{:S(2)}) copy-start(f32[2,256,256]{2,1,0:T(8,128)} %tile_in) | copy-start | bytes 1572868
  64.5 25.2 %all-to-all-start = ((f32[8,16,768]{2,1,0:T(8,128)}), f32[8,16,768]{2,1,0:T(8,128)S(1)}, u32[]{:S(2)}, u32[]{:S(2)}) async-start(f32[8,16,768]{2,1,0:T(8,128)} %add_columns.1), calls=%async_computation | async-start | bytes 786432 | tf_op jit(solution)/shard_map/all_to_all | solution.py:443
  77.1 19.9 %collective-permute-start.10 = (f32[2,256,256]{2,1,0:T(8,128)S(1)}, f32[2,256,256]{2,1,0:T(8,128)S(1)}, u32[]{:S(2)}, u32[]{:S(2)}) collective-permute-start(f32[2,256,256]{2,1,0:T(8,128)S(1)} %get-tuple-element.39), channel_id=1, source_target_pairs={{0,32},{32,64},{64,96},{96,128},{128,160},{160,192},{192,224},{224... | collective-permute-start | bytes 1572872 | tf_op jit(solution)/shard_map/ppermute | solution.py:25
  90.4 14.4 %all-to-all-start.1 = ((f32[8,8,192]{2,1,0:T(8,128)}), f32[8,8,192]{2,1,0:T(8,128)S(1)}, u32[]{:S(2)}, u32[]{:S(2)}) async-start(f32[8,8,192]{2,1,0:T(8,128)} %add_depth.1), calls=%async_computation.1 | async-start | bytes 131072 | tf_op jit(solution)/shard_map/all_to_all | solution.py:445

commit v5 on v4

--- a/solution.py
+++ b/solution.py
@@ -315,14 +315,15 @@
 
 
 def columns_kernel(kept_re, got_re, came_re, kept_im, got_im, came_im, out_ref):
-    for part, (kept_ref, got_ref, came_ref) in enumerate(((kept_re, got_re, came_re), (kept_im, got_im, came_im))):
-        for z in range(4):
-            turned = (kept_ref[0, z] + got_ref[0, z] + came_ref[z]).reshape(96, half).T
-            lane = z * 192 + part * 96
-            for y in range(8):
-                for z_hi in range(2):
-                    at = z_hi * 64 + y * 8
-                    out_ref[y, z_hi * 8 : z_hi * 8 + 8, lane : lane + 96] = turned[at : at + 8]
+    pieces = []
+    for z in range(4):
+        for kept_ref, got_ref, came_ref in ((kept_re, got_re, came_re), (kept_im, got_im, came_im)):
+            pieces.append((kept_ref[0, z] + got_ref[0, z] + came_ref[z]).reshape(96, half))
+    turned = jnp.concatenate(pieces, axis=0).T
+    for y in range(8):
+        for z_hi in range(2):
+            at = z_hi * 64 + y * 8
+            out_ref[y, z_hi * 8 : z_hi * 8 + 8] = turned[at : at + 8]
 
 
 def depth_kernel(parts_ref, out_ref):

time: 106 us -> 106 us (level)
  no operation moved by 1% of the time
where the time goes in v5:
time: 106 us; the launch traced here: 105 us
  starting transfers between devices  49.1 us (46%)
  waiting for transfers between devices  35.6 us (34%)
  Pallas kernels  13.8 us (13%)
  local copies, waits for them, and re-layouts  4.36 us (4%)
  between operations  1.51 us (1%)
    ppermute x5, starting transfers between devices, passed_along(): return lax.ppermute(x, axis, pairs)  13.8 us
    all_to_all x1, starting transfers between devices, local(): parts = lax.all_to_all(packed, 'y', 0, 0, tiled=True)  11.9 us
    ppermute x5, waiting for transfers between devices, passed_along(): return lax.ppermute(x, axis, pairs)  11.8 us
    all_to_all x1, waiting for transfers between devices, local(): parts = lax.all_to_all(packed, 'y', 0, 0, tiled=True)  9.19 us
    pallas_call x1, Pallas kernels, local(): call(main_kernel, 'step', [smem, smem] + [vmem] * 7, [shaped(*block_shape...  8.49 us
    all_to_all x1, waiting for transfers between devices, local(): parts = lax.all_to_all(packed, ('z_lo', 'z_hi'), 0, 0, tiled=True)  6.86 us
    all_to_all x1, starting transfers between devices, local(): parts = lax.all_to_all(packed, ('z_lo', 'z_hi'), 0, 0, tiled=True)  6.6 us
    ppermute x2, starting transfers between devices, local(): lax.ppermute(keep[1] + got[1], ('x', 'core'), far_pairs)  5.99 us
  transfers between devices with their start and end apart: 13, of which 9 were waited for; matrix products, arithmetic and copies ran while one was open for 2% of the time, Pallas kernels for 4%

profile of v5, /device:TPU:6, one launch (start us, length us, event | category | flops | bytes accessed | tf_op | source)
XLA Modules:
  0.0 105.4 jit_solution(10423332458953078301)
XLA Ops:
  0.6 0.0 copy-start
  0.6 1.4 %collective-permute-start.1 = (f32[2,256,256]{2,1,0:T(8,128)}, f32[2,256,256]{2,1,0:T(8,128)S(1)}, u32[]{:S(2)}, u32[]{:S(2)}) collective-permute-start(f32[2,256,256]{2,1,0:T(8,128)} %tile_in), channel_id=1, source_target_pairs={{1,0},{2,1},{3,2},{4,3},{5,4},{6,5},{7,6},{8,7},{9,8},{10,9},{11,1... | collective-permute-start | bytes 1572872 | tf_op jit(solution)/shard_map/ppermute | solution.py:25
  2.1 4.2 %collective-permute-start = (s32[1,1,1,2]{3,2,1,0:T(1,128)}, s32[1,1,1,2]{3,2,1,0:T(1,128)S(1)}, u32[]{:S(2)}, u32[]{:S(2)}) collective-permute-start(s32[1,1,1,2]{3,2,1,0:T(1,128)} %param.9), channel_id=1, source_target_pairs={{0,32},{32,64},{64,96},{96,128},{128,160},{160,192},{192,224},{224... | collective-permute-start | bytes 32 | tf_op jit(solution)/shard_map/ppermute | solution.py:25
  6.3 1.4 %collective-permute-done = s32[1,1,1,2]{3,2,1,0:T(1,128)S(1)} collective-permute-done((s32[1,1,1,2]{3,2,1,0:T(1,128)}, s32[1,1,1,2]{3,2,1,0:T(1,128)S(1)}, u32[]{:S(2)}, u32[]{:S(2)}) %collective-permute-start) | collective-permute-done | bytes 40 | tf_op jit(solution)/shard_map/ppermute | solution.py:25
  7.7 0.0 copy-start.1
  7.7 1.0 copy-done.1
  8.7 0.0 copy-start.4
  8.8 0.0 collective-permute-done.1.right_ref
  8.8 0.6 mix.1
  9.4 2.7 %collective-permute-start.2 = (f32[2,256,256]{2,1,0:T(8,128)S(1)}, f32[2,256,256]{2,1,0:T(8,128)S(1)}, u32[]{:S(2)}, u32[]{:S(2)}) collective-permute-start(f32[2,256,256]{2,1,0:T(8,128)S(1)} %mix.1), channel_id=1, source_target_pairs={{32,0},{64,32},{96,64},{128,96},{160,128},{192,160},{224,192},{256... | collective-permute-start | bytes 1572872 | tf_op jit(solution)/shard_map/ppermute | solution.py:25
  12.7 0.0 copy-done
  12.8 0.0 copy-done.4
  12.8 0.0 copy-start.3
  12.8 1.4 %copy-done.3 = bf16[2,6,256,256]{3,2,1,0:T(8,128)(2,1)S(1)} copy-done((bf16[2,6,256,256]{3,2,1,0:T(8,128)(2,1)S(1)}, bf16[2,6,256,256]{3,2,1,0:T(8,128)(2,1)}, u32[]{:S(2)}) %copy-start.3) | copy-done | bytes 1572888
  14.2 0.0 copy-start.5
  14.2 0.9 copy-done.5
  15.1 0.0 copy-start.6
  15.1 1.4 %prepare.1 = (bf16[2,6,256,256]{3,2,1,0:T(8,128)(2,1)S(1)}, f32[256,256]{1,0:T(8,128)S(1)}, bf16[8,2,256,256]{3,2,1,0:T(8,128)(2,1)S(1)}, bf16[2,256,256]{2,1,0:T(8,128)(2,1)S(1)}) custom-call(bf16[2,6,256,256]{3,2,1,0:T(8,128)(2,1)S(1)} %copy-done.3, bf16[256,256]{1,0:T(8,128)(2,1)S(1)} %bitcast.12, bf16[8,2,256,256]{3,2,1,0:T(8,128)(2,1)S(1)} %copy-done, ...), custom_call_target="tpu_custom_call" | custom-call | flops 500000000 | bytes 8000000 | tf_op jit(solution)/shard_map/prepare/pallas_call | solution.py:392
  16.5 10.4 %collective-permute-done.2.lower_ref = f32[2,256,256]{2,1,0:T(8,128)S(1)} collective-permute-done((f32[2,256,256]{2,1,0:T(8,128)S(1)}, f32[2,256,256]{2,1,0:T(8,128)S(1)}, u32[]{:S(2)}, u32[]{:S(2)}) %collective-permute-start.2) | collective-permute-done | bytes 524320 | tf_op jit(solution)/shard_map/ppermute | solution.py:25
  26.9 0.0 copy-done.6
  26.9 8.5 %step.1 = (f32[4,4,6,16,128]{4,3,2,1,0:T(8,128)S(1)}, f32[4,4,6,16,128]{4,3,2,1,0:T(8,128)S(1)}, f32[4,4,6,16,128]{4,3,2,1,0:T(8,128)S(1)}, f32[4,4,6,16,128]{4,...) custom-call(s32[2]{0:T(128)S(1)} %bitcast.13, s32[1]{0:T(128)} %bitcast.11.count_ref, ...), custom_call_target="tpu_custom_call" | custom-call | flops 5000000000 | bytes 12000000 | tf_op jit(solution)/shard_map/step/pallas_call | solution.py:413
  35.4 3.2 %collective-permute-start.6 = (f32[4,4,6,16,128]{4,3,2,1,0:T(8,128)S(1)}, f32[4,4,6,16,128]{4,3,2,1,0:T(8,128)S(1)}, u32[]{:S(2)}, u32[]{:S(2)}) collective-permute-start(f32[4,4,6,16,128]{4,3,2,1,0:T(8,128)S(1)} %get-tuple-element.33), channel_id=1, source_target_pairs={{0,1},{1,0},{2,3},{3,2},{4,5},{5,4},{6,7},{7,6},{8,9},{9,8},{10,11... | collective-permute-start | bytes 2359304 | tf_op jit(solution)/shard_map/ppermute | solution.py:428
  38.7 1.9 %collective-permute-start.3 = (f32[4,4,6,16,128]{4,3,2,1,0:T(8,128)S(1)}, f32[4,4,6,16,128]{4,3,2,1,0:T(8,128)S(1)}, u32[]{:S(2)}, u32[]{:S(2)}) collective-permute-start(f32[4,4,6,16,128]{4,3,2,1,0:T(8,128)S(1)} %get-tuple-element.29), channel_id=1, source_target_pairs={{0,1},{1,0},{2,3},{3,2},{4,5},{5,4},{6,7},{7,6},{8,9},{9,8},{10,11... | collective-permute-start | bytes 2359304 | tf_op jit(solution)/shard_map/ppermute | solution.py:428
  40.6 0.0 collective-permute-done.6.theirs_ref
  40.6 0.1 add_cores.3
  40.7 1.9 %collective-permute-start.7 = (f32[2,4,6,16,128]{4,3,2,1,0:T(8,128)S(1)}, f32[2,4,6,16,128]{4,3,2,1,0:T(8,128)S(1)}, u32[]{:S(2)}, u32[]{:S(2)}) collective-permute-start(f32[2,4,6,16,128]{4,3,2,1,0:T(8,128)S(1)} %get-tuple-element.35), channel_id=1, source_target_pairs={{0,32},{1,97},{32,0},{33,65},{64,96},{65,33},{96,64},{97,1},{2,34}... | collective-permute-start | bytes 1179656 | tf_op jit(solution)/shard_map/ppermute | solution.py:433
  42.6 0.2 collective-permute-done.3.theirs_ref
  42.9 0.1 add_cores.2
  42.9 3.7 %collective-permute-start.4 = (f32[2,4,6,16,128]{4,3,2,1,0:T(8,128)S(1)}, f32[2,4,6,16,128]{4,3,2,1,0:T(8,128)S(1)}, u32[]{:S(2)}, u32[]{:S(2)}) collective-permute-start(f32[2,4,6,16,128]{4,3,2,1,0:T(8,128)S(1)} %get-tuple-element.31), channel_id=1, source_target_pairs={{0,32},{1,97},{32,0},{33,65},{64,96},{65,33},{96,64},{97,1},{2,34}... | collective-permute-start | bytes 1179656 | tf_op jit(solution)/shard_map/ppermute | solution.py:433
  46.7 3.1 %collective-permute-start.9 = (f32[2,264,256]{2,1,0:T(8,128)S(1)}, f32[2,264,256]{2,1,0:T(8,128)S(1)}, u32[]{:S(2)}, u32[]{:S(2)}) collective-permute-start(f32[2,264,256]{2,1,0:T(8,128)S(1)} %get-tuple-element.37), channel_id=1, source_target_pairs={{0,1},{1,2},{2,3},{3,4},{4,5},{5,6},{6,7},{7,8},{8,9},{9,10},{10,1... | collective-permute-start | bytes 1622024 | tf_op jit(solution)/shard_map/ppermute | solution.py:25
  49.8 0.6 collective-permute-done.7.got_im
  50.4 3.0 %collective-permute-start.8 = (f32[4,6,16,128]{3,2,1,0:T(8,128)S(1)}, f32[4,6,16,128]{3,2,1,0:T(8,128)S(1)}, u32[]{:S(2)}, u32[]{:S(2)}) collective-permute-start(f32[4,6,16,128]{3,2,1,0:T(8,128)S(1)} %fusion), channel_id=1, source_target_pairs={{0,96},{1,33},{32,64},{33,1},{64,32},{65,97},{96,0},{97,65},{2,98}... | collective-permute-start | bytes 589832 | tf_op jit(solution)/shard_map/ppermute | solution.py:437
  53.4 1.2 %collective-permute-done.4.got_re = f32[2,4,6,16,128]{4,3,2,1,0:T(8,128)S(1)} collective-permute-done((f32[2,4,6,16,128]{4,3,2,1,0:T(8,128)S(1)}, f32[2,4,6,16,128]{4,3,2,1,0:T(8,128)S(1)}, u32[]{:S(2)}, u32[]{:S(2)}) %collective-permute-start.4) | collective-permute-done | bytes 393248 | tf_op jit(solution)/shard_map/ppermute | solution.py:433
  54.6 3.0 %collective-permute-start.5 = (f32[4,6,16,128]{3,2,1,0:T(8,128)S(1)}, f32[4,6,16,128]{3,2,1,0:T(8,128)S(1)}, u32[]{:S(2)}, u32[]{:S(2)}) collective-permute-start(f32[4,6,16,128]{3,2,1,0:T(8,128)S(1)} %fusion.1), channel_id=1, source_target_pairs={{0,96},{1,33},{32,64},{33,1},{64,32},{65,97},{96,0},{97,65},{2,98}... | collective-permute-start | bytes 589832 | tf_op jit(solution)/shard_map/ppermute | solution.py:437
  57.6 1.6 %collective-permute-done.8.came_im = f32[4,6,16,128]{3,2,1,0:T(8,128)S(1)} collective-permute-done((f32[4,6,16,128]{3,2,1,0:T(8,128)S(1)}, f32[4,6,16,128]{3,2,1,0:T(8,128)S(1)}, u32[]{:S(2)}, u32[]{:S(2)}) %collective-permute-start.8) | collective-permute-done | bytes 196640 | tf_op jit(solution)/shard_map/ppermute | solution.py:437
  59.2 4.2 %collective-permute-done.5.came_re = f32[4,6,16,128]{3,2,1,0:T(8,128)S(1)} collective-permute-done((f32[4,6,16,128]{3,2,1,0:T(8,128)S(1)}, f32[4,6,16,128]{3,2,1,0:T(8,128)S(1)}, u32[]{:S(2)}, u32[]{:S(2)}) %collective-permute-start.5) | collective-permute-done | bytes 196640 | tf_op jit(solution)/shard_map/ppermute | solution.py:437
  63.4 0.9 add_columns.1
  64.3 0.0 copy-start.2
  64.3 11.9 %all-to-all-start = ((f32[8,16,768]{2,1,0:T(8,128)}), f32[8,16,768]{2,1,0:T(8,128)S(1)}, u32[]{:S(2)}, u32[]{:S(2)}) async-start(f32[8,16,768]{2,1,0:T(8,128)} %add_columns.1), calls=%async_computation | async-start | bytes 786432 | tf_op jit(solution)/shard_map/all_to_all | solution.py:444
  76.2 0.0 collective-permute-done.9.moved_ref
  76.2 0.7 down.1
  77.0 2.4 %collective-permute-start.10 = (f32[2,256,256]{2,1,0:T(8,128)S(1)}, f32[2,256,256]{2,1,0:T(8,128)S(1)}, u32[]{:S(2)}, u32[]{:S(2)}) collective-permute-start(f32[2,256,256]{2,1,0:T(8,128)S(1)} %get-tuple-element.39), channel_id=1, source_target_pairs={{0,32},{32,64},{64,96},{96,128},{128,160},{160,192},{192,224},{224... | collective-permute-start | bytes 1572872 | tf_op jit(solution)/shard_map/ppermute | solution.py:25
  79.4 0.9 constant_dynamic-slice_fusion
  80.3 0.1 copy.10
  80.4 9.2 %all-to-all-done.parts_ref = f32[8,16,768]{2,1,0:T(8,128)S(1)} async-done(((f32[8,16,768]{2,1,0:T(8,128)}), f32[8,16,768]{2,1,0:T(8,128)S(1)}, u32[]{:S(2)}, u32[]{:S(2)}) %all-to-all-start) | async-done | bytes 393248 | tf_op jit(solution)/shard_map/all_to_all | solution.py:444
  89.6 0.7 add_depth.1
  90.3 6.6 %all-to-all-start.1 = ((f32[8,8,192]{2,1,0:T(8,128)}), f32[8,8,192]{2,1,0:T(8,128)S(1)}, u32[]{:S(2)}, u32[]{:S(2)}) async-start(f32[8,8,192]{2,1,0:T(8,128)} %add_depth.1), calls=%async_computation.1 | async-start | bytes 131072 | tf_op jit(solution)/shard_map/all_to_all | solution.py:446
  96.9 0.0 collective-permute-done.10
  96.9 0.0 copy-done.2
  96.9 0.9 multiply_subtract_fusion
  97.8 6.9 %all-to-all-done.1.parts_ref = f32[8,8,192]{2,1,0:T(8,128)S(1)} async-done(((f32[8,8,192]{2,1,0:T(8,128)}), f32[8,8,192]{2,1,0:T(8,128)S(1)}, u32[]{:S(2)}, u32[]{:S(2)}) %all-to-all-start.1) | async-done | bytes 49184 | tf_op jit(solution)/shard_map/all_to_all | solution.py:446
  104.7 0.7 finish.1
  (4 shorter events, 0.1 us)
Async XLA Ops:
  0.6 12.1 %copy-start = (bf16[8,2,256,256]{3,2,1,0:T(8,128)(2,1)S(1)}, bf16[8,2,256,256]{3,2,1,0:T(8,128)(2,1)}, u32[]{:S(2)}) copy-start(bf16[8,2,256,256]{3,2,1,0:T(8,128)(2,1)} %constant.39.clone.table_in) | copy-start | bytes 6291460
  0.6 8.1 %collective-permute-start.1 = (f32[2,256,256]{2,1,0:T(8,128)}, f32[2,256,256]{2,1,0:T(8,128)S(1)}, u32[]{:S(2)}, u32[]{:S(2)}) collective-permute-start(f32[2,256,256]{2,1,0:T(8,128)} %tile_in), channel_id=1, source_target_pairs={{1,0},{2,1},{3,2},{4,3},{5,4},{6,5},{7,6},{8,7},{9,8},{10,9},{11,1... | collective-permute-start | bytes 1572872 | tf_op jit(solution)/shard_map/ppermute | solution.py:25
  2.1 5.6 %collective-permute-start = (s32[1,1,1,2]{3,2,1,0:T(1,128)}, s32[1,1,1,2]{3,2,1,0:T(1,128)S(1)}, u32[]{:S(2)}, u32[]{:S(2)}) collective-permute-start(s32[1,1,1,2]{3,2,1,0:T(1,128)} %param.9), channel_id=1, source_target_pairs={{0,32},{32,64},{64,96},{96,128},{128,160},{160,192},{192,224},{224... | collective-permute-start | bytes 32 | tf_op jit(solution)/shard_map/ppermute | solution.py:25
  7.7 1.0 copy-start.1
  8.7 4.0 %copy-start.4 = (bf16[4,256,256]{2,1,0:T(8,128)(2,1)S(1)}, bf16[4,256,256]{2,1,0:T(8,128)(2,1)}, u32[]{:S(2)}) copy-start(bf16[4,256,256]{2,1,0:T(8,128)(2,1)} %constant.40.clone.order_in) | copy-start | bytes 1572868
  9.4 17.5 %collective-permute-start.2 = (f32[2,256,256]{2,1,0:T(8,128)S(1)}, f32[2,256,256]{2,1,0:T(8,128)S(1)}, u32[]{:S(2)}, u32[]{:S(2)}) collective-permute-start(f32[2,256,256]{2,1,0:T(8,128)S(1)} %mix.1), channel_id=1, source_target_pairs={{32,0},{64,32},{96,64},{128,96},{160,128},{192,160},{224,192},{256... | collective-permute-start | bytes 1572872 | tf_op jit(solution)/shard_map/ppermute | solution.py:25
  12.8 1.4 %copy-start.3 = (bf16[2,6,256,256]{3,2,1,0:T(8,128)(2,1)S(1)}, bf16[2,6,256,256]{3,2,1,0:T(8,128)(2,1)}, u32[]{:S(2)}) copy-start(bf16[2,6,256,256]{3,2,1,0:T(8,128)(2,1)} %probe_in.1) | copy-start | bytes 4718596
  14.2 0.9 copy-start.5
  15.1 11.8 %copy-start.6 = (s32[1,1,1,2]{3,2,1,0:T(1,128)S(1)}, s32[1,1,1,2]{3,2,1,0:T(1,128)}, u32[]{:S(2)}) copy-start(s32[1,1,1,2]{3,2,1,0:T(1,128)} %param.9) | copy-start | bytes 28
  35.4 5.2 %collective-permute-start.6 = (f32[4,4,6,16,128]{4,3,2,1,0:T(8,128)S(1)}, f32[4,4,6,16,128]{4,3,2,1,0:T(8,128)S(1)}, u32[]{:S(2)}, u32[]{:S(2)}) collective-permute-start(f32[4,4,6,16,128]{4,3,2,1,0:T(8,128)S(1)} %get-tuple-element.33), channel_id=1, source_target_pairs={{0,1},{1,0},{2,3},{3,2},{4,5},{5,4},{6,7},{7,6},{8,9},{9,8},{10,11... | collective-permute-start | bytes 2359304 | tf_op jit(solution)/shard_map/ppermute | solution.py:428
  38.7 4.2 %collective-permute-start.3 = (f32[4,4,6,16,128]{4,3,2,1,0:T(8,128)S(1)}, f32[4,4,6,16,128]{4,3,2,1,0:T(8,128)S(1)}, u32[]{:S(2)}, u32[]{:S(2)}) collective-permute-start(f32[4,4,6,16,128]{4,3,2,1,0:T(8,128)S(1)} %get-tuple-element.29), channel_id=1, source_target_pairs={{0,1},{1,0},{2,3},{3,2},{4,5},{5,4},{6,7},{7,6},{8,9},{9,8},{10,11... | collective-permute-start | bytes 2359304 | tf_op jit(solution)/shard_map/ppermute | solution.py:428
  40.7 9.7 %collective-permute-start.7 = (f32[2,4,6,16,128]{4,3,2,1,0:T(8,128)S(1)}, f32[2,4,6,16,128]{4,3,2,1,0:T(8,128)S(1)}, u32[]{:S(2)}, u32[]{:S(2)}) collective-permute-start(f32[2,4,6,16,128]{4,3,2,1,0:T(8,128)S(1)} %get-tuple-element.35), channel_id=1, source_target_pairs={{0,32},{1,97},{32,0},{33,65},{64,96},{65,33},{96,64},{97,1},{2,34}... | collective-permute-start | bytes 1179656 | tf_op jit(solution)/shard_map/ppermute | solution.py:433
  42.9 11.7 %collective-permute-start.4 = (f32[2,4,6,16,128]{4,3,2,1,0:T(8,128)S(1)}, f32[2,4,6,16,128]{4,3,2,1,0:T(8,128)S(1)}, u32[]{:S(2)}, u32[]{:S(2)}) collective-permute-start(f32[2,4,6,16,128]{4,3,2,1,0:T(8,128)S(1)} %get-tuple-element.31), channel_id=1, source_target_pairs={{0,32},{1,97},{32,0},{33,65},{64,96},{65,33},{96,64},{97,1},{2,34}... | collective-permute-start | bytes 1179656 | tf_op jit(solution)/shard_map/ppermute | solution.py:433
  46.7 29.5 %collective-permute-start.9 = (f32[2,264,256]{2,1,0:T(8,128)S(1)}, f32[2,264,256]{2,1,0:T(8,128)S(1)}, u32[]{:S(2)}, u32[]{:S(2)}) collective-permute-start(f32[2,264,256]{2,1,0:T(8,128)S(1)} %get-tuple-element.37), channel_id=1, source_target_pairs={{0,1},{1,2},{2,3},{3,4},{4,5},{5,6},{6,7},{7,8},{8,9},{9,10},{10,1... | collective-permute-start | bytes 1622024 | tf_op jit(solution)/shard_map/ppermute | solution.py:25
  50.4 8.8 %collective-permute-start.8 = (f32[4,6,16,128]{3,2,1,0:T(8,128)S(1)}, f32[4,6,16,128]{3,2,1,0:T(8,128)S(1)}, u32[]{:S(2)}, u32[]{:S(2)}) collective-permute-start(f32[4,6,16,128]{3,2,1,0:T(8,128)S(1)} %fusion), channel_id=1, source_target_pairs={{0,96},{1,33},{32,64},{33,1},{64,32},{65,97},{96,0},{97,65},{2,98}... | collective-permute-start | bytes 589832 | tf_op jit(solution)/shard_map/ppermute | solution.py:437
  54.6 8.8 %collective-permute-start.5 = (f32[4,6,16,128]{3,2,1,0:T(8,128)S(1)}, f32[4,6,16,128]{3,2,1,0:T(8,128)S(1)}, u32[]{:S(2)}, u32[]{:S(2)}) collective-permute-start(f32[4,6,16,128]{3,2,1,0:T(8,128)S(1)} %fusion.1), channel_id=1, source_target_pairs={{0,96},{1,33},{32,64},{33,1},{64,32},{65,97},{96,0},{97,65},{2,98}... | collective-permute-start | bytes 589832 | tf_op jit(solution)/shard_map/ppermute | solution.py:437
  64.3 32.6 %copy-start.2 = (f32[2,256,256]{2,1,0:T(8,128)S(1)}, f32[2,256,256]{2,1,0:T(8,128)}, u32[]{:S(2)}) copy-start(f32[2,256,256]{2,1,0:T(8,128)} %tile_in) | copy-start | bytes 1572868
  64.3 25.2 %all-to-all-start = ((f32[8,16,768]{2,1,0:T(8,128)}), f32[8,16,768]{2,1,0:T(8,128)S(1)}, u32[]{:S(2)}, u32[]{:S(2)}) async-start(f32[8,16,768]{2,1,0:T(8,128)} %add_columns.1), calls=%async_computation | async-start | bytes 786432 | tf_op jit(solution)/shard_map/all_to_all | solution.py:444
  77.0 19.9 %collective-permute-start.10 = (f32[2,256,256]{2,1,0:T(8,128)S(1)}, f32[2,256,256]{2,1,0:T(8,128)S(1)}, u32[]{:S(2)}, u32[]{:S(2)}) collective-permute-start(f32[2,256,256]{2,1,0:T(8,128)S(1)} %get-tuple-element.39), channel_id=1, source_target_pairs={{0,32},{32,64},{64,96},{96,128},{128,160},{160,192},{192,224},{224... | collective-permute-start | bytes 1572872 | tf_op jit(solution)/shard_map/ppermute | solution.py:25
  90.3 14.4 %all-to-all-start.1 = ((f32[8,8,192]{2,1,0:T(8,128)}), f32[8,8,192]{2,1,0:T(8,128)S(1)}, u32[]{:S(2)}, u32[]{:S(2)}) async-start(f32[8,8,192]{2,1,0:T(8,128)} %add_depth.1), calls=%async_computation.1 | async-start | bytes 131072 | tf_op jit(solution)/shard_map/all_to_all | solution.py:446
